TPU v7x, 32 devices: a whole 2x2x4 slice. The times are simulated.
32 devices in a mesh: rows: 32 (over z, y, x, core).
Axes of the slice: x: 2, y: 2, z: 4, core: 2. Of those that a mesh axis runs over, the one named last changes fastest.
Arguments:
- hamiltonian: float32 [49152, 1728], P('rows'), may hold values from -0.15625 to 0.15625
- subspace: float32 [49152, 128], P('rows'), may hold values from -6 to 6
- block_cols: int32 [768, 27], P('rows'), may hold values from 0 to 775, as said below
- far_list: int32 [32, 8], P('rows'), may hold values from -1 to 767, as said below
Outputs:
- filtered: float32 [49152, 128], P('rows')
Inputs may be any that keep to these rules, and one draw needn't show every extreme that they name: `far_list`: row d holds in slots 0 to c_d - 1 distinct block indices owned by device d xor (4) (that device owns blocks k * 24 to k * 24 + 23 for its index k), and -1 in its other slots; c_d is 2 or more, and device 0 fills all 8 slots. `block_cols`: entry 0 of row i is i; the next 24 entries are distinct blocks (i + o) mod 768 with 0 < |o| <= 13; the last two are 768 + s for two distinct filled slots s of far_list's row of the device that owns row i.
All inputs are finite; a program needn't handle non-finite values.
Results may differ from a plain program's by a relative error of at most 0.000058.
Values sent between devices are 32-bit elements; how exact they have to be, the bound alone decides.
No kernel may reach another device: no remote copies, remote signals or barrier semaphores. Data moves between devices by JAX's collectives and lax.ppermute only.
A program may use at most 128 MiB of HBM per device.

v0:
```python
import jax
import jax.numpy as jnp
from jax import lax
from jax.sharding import PartitionSpec as P

CENTER = 0.25
HALF_WIDTH = 1.5


def partner(value, axis, bit):
    mask = 2**bit
    pairs = [(source, source ^ mask) for source in range(lax.axis_size(axis))]
    return lax.ppermute(value, axis, pairs)


def extended_2(value, sides, width):
    for axis, dim in sides:
        devices, length = (lax.axis_size(axis), value.shape[dim])
        up = [(i, (i + 1) % devices) for i in range(devices)]
        down = [(j, i) for i, j in up]
        last = lax.slice_in_dim(value, length - width, length, axis=dim)
        leading = lax.slice_in_dim(value, 0, width, axis=dim)
        before = lax.ppermute(last, axis, up)
        after = lax.ppermute(leading, axis, down)
        value = jnp.concatenate([before, value, after], axis=dim)
    return value


def gather_blocks(extended, positions, block_size):
    sub_width = extended.shape[1]
    blocks = extended.reshape(-1, block_size, sub_width)
    picked = blocks[positions]
    return picked.reshape(positions.shape[0], positions.shape[1] * block_size, sub_width)


def per_device(hamiltonian, subspace, block_cols, far_list):
    block_rows, entries = block_cols.shape
    block_size = hamiltonian.shape[1] // entries
    sub_width = subspace.shape[1]
    slot_total = far_list.shape[1]
    device_count = lax.axis_size("rows")
    my_index = lax.axis_index("rows")
    block_total = block_rows * device_count
    swap_level = (device_count // 8).bit_length() - 1
    first_row = my_index * block_rows
    inband = block_cols < block_total
    slot_index = jnp.clip(block_cols - block_total, 0, slot_total - 1)
    asked_list = partner(far_list, "rows", swap_level)
    valid_mask = (asked_list[0] >= 0).astype(jnp.float32)
    local_index = jnp.clip(asked_list[0] - first_row, 0, block_rows - 1)
    band_count = block_rows + 2 * block_rows
    positions = jnp.where(
        inband, (block_cols - first_row + block_rows) % block_total, band_count + slot_index
    )
    ham_slab = hamiltonian.reshape(block_rows, block_size, entries * block_size)

    def apply_operator(vectors):
        band_panel = extended_2(vectors, (("rows", 0),), block_rows * block_size)
        outgoing = (
            vectors.reshape(block_rows, block_size, sub_width)[local_index]
            * valid_mask[:, None, None]
        )
        remote = partner(outgoing.reshape(slot_total * block_size, sub_width), "rows", swap_level)
        extended = jnp.concatenate([band_panel, remote], axis=0)
        picked = gather_blocks(extended, positions, block_size)
        result = jnp.einsum("irm,imk->irk", ham_slab, picked, precision=lax.Precision.HIGHEST)
        return result.reshape(block_rows * block_size, sub_width)

    first_term = (apply_operator(subspace) - CENTER * subspace) / HALF_WIDTH
    second = apply_operator(first_term)
    return 2.0 / HALF_WIDTH * (second - CENTER * first_term) - subspace


def solution(mesh):
    placed = (P("rows", None), P("rows", None), P("rows", None), P("rows", None))
    return jax.shard_map(
        per_device, mesh=mesh, in_specs=placed, out_specs=P("rows", None), check_vma=False
    )
```

profile of v0, /device:TPU:0, one launch (start us, length us, event | category | flops | bytes accessed | tf_op | source)
XLA Modules:
  0.0 105.3 jit_solution(14886949911842592040)
XLA Ops:
  0.0 6.4 %collective-permute-start.1 = (f32[1536,128]{1,0:T(8,128)}, f32[1536,128]{1,0:T(8,128)S(1)}, u32[]{:S(2)}, u32[]{:S(2)}) collective-permute-start(f32[1536,128]{1,0:T(8,128)} %param.5), channel_id=1, source_target_pairs={{1,0},{2,1},{3,2},{4,3},{5,4},{6,5},{7,6},{8,7},{9,8},{10,9},{11,1... | collective-permute-start | bytes 2359304 | tf_op jit(solution)/shard_map/ppermute | solution.py:24
  6.4 0.0 collective-permute-start
  6.4 0.0 collective-permute-start.2
  6.4 3.7 %collective-permute-done.2 = s32[1,8]{1,0:T(1,128)S(1)} collective-permute-done((s32[1,8]{1,0:T(1,128)}, s32[1,8]{1,0:T(1,128)S(1)}, u32[]{:S(2)}, u32[]{:S(2)}) %collective-permute-start.2) | collective-permute-done | bytes 64 | tf_op jit(solution)/shard_map/ppermute | solution.py:13
  10.1 0.1 mul.38
  10.1 0.1 mul.39
  10.2 1.7 %gather_fusion = f32[8,64,128]{2,1,0:T(8,128)S(1)} fusion(f32[24,64,128]{2,1,0:T(8,128)} %bitcast.43, s32[1024]{0:T(1024)S(1)} %pad_clamp_fusion.1), kind=kCustom, calls=%fused_computation | custom fusion | bytes 524320 | tf_op jit(solution)/shard_map/gather | solution.py:60
  11.9 0.0 copy-start
  11.9 0.1 bitcast_multiply_fusion.1
  12.1 0.1 collective-permute-start.3
  12.2 0.8 compare_select_fusion
  12.9 0.1 reshape.90
  13.0 11.8 %copy.7 = f32[1536,1728]{1,0:T(8,128)} copy(f32[1536,1728]{0,1:T(8,128)} %param.4) | data formatting | bytes 21233664 | tf_op args[0]
  24.8 0.0 collective-permute-done.3
  24.8 0.0 copy-start.5
  24.8 0.0 collective-permute-done.1
  24.8 0.7 copy-done.5
  25.5 0.0 copy-start.3
  25.5 0.9 copy-done.3
  26.4 0.0 collective-permute-done
  26.4 0.0 copy-done
  26.4 1.6 %pad_maximum_fusion = f32[5120,128]{1,0:T(8,128)S(1)} fusion(f32[512,128]{1,0:T(8,128)} %copy-done.5, f32[1536,128]{1,0:T(8,128)} %copy-done.3, f32[1536,128]{1,0:T(8,128)S(1)} %copy-done, f32[1536,128]{1,0:T(8,128)} %collective-permute-done), kind=kLoop, calls=%fused_computation.4 | loop fusion | flops 1966080 | bytes 5242880 | tf_op jit(solution)/shard_map/concatenate | solution.py:64
  28.0 8.3 %gather_fusion.1 = f32[648,64,128]{2,1,0:T(8,128)} fusion(f32[80,64,128]{2,1,0:T(8,128)S(1)} %bitcast.40, s32[1024]{0:T(1024)S(1)} %pad_clamp_fusion), kind=kCustom, calls=%fused_computation.1 | custom fusion | bytes 42469920 | tf_op jit(solution)/shard_map/gather | solution.py:32
  36.4 18.1 %fusion.9 = f32[24,128,64]{1,2,0:T(8,128)S(1)} fusion(f32[24,1728,128]{2,1,0:T(8,128)} %bitcast.42, f32[24,64,1728]{2,1,0:T(8,128)} %bitcast.37), kind=kOutput, calls=%fused_computation.26 | convolution fusion | flops 4076863488 | bytes 32636928 | tf_op jit(solution)/shard_map/irm,imk->irk/dot_general | solution.py:66
  54.4 0.1 fusion.2
  54.6 0.0 copy-start.2
  54.6 4.7 %collective-permute-start.5 = (f32[1536,128]{1,0:T(8,128)S(1)}, f32[1536,128]{1,0:T(8,128)S(1)}, u32[]{:S(2)}, u32[]{:S(2)}) collective-permute-start(f32[1536,128]{1,0:T(8,128)S(1)} %fusion.2), channel_id=1, source_target_pairs={{1,0},{2,1},{3,2},{4,3},{5,4},{6,5},{7,6},{8,7},{9,8},{10,9},{11,1... | collective-permute-start | bytes 2359304 | tf_op jit(solution)/shard_map/ppermute | solution.py:24
  59.3 0.0 collective-permute-start.4
  59.3 0.6 gather_fusion.2
  59.8 0.1 bitcast_multiply_fusion
  60.0 0.1 collective-permute-start.6
  60.1 14.8 %collective-permute-done.6 = f32[512,128]{1,0:T(8,128)S(1)} collective-permute-done((f32[512,128]{1,0:T(8,128)S(1)}, f32[512,128]{1,0:T(8,128)S(1)}, u32[]{:S(2)}, u32[]{:S(2)}) %collective-permute-start.6) | collective-permute-done | bytes 262176 | tf_op jit(solution)/shard_map/ppermute | solution.py:13
  74.8 0.0 collective-permute-done.5
  74.9 0.0 copy-done.2
  74.9 0.0 copy-start.4
  74.9 0.9 copy-done.4
  75.7 0.0 collective-permute-done.4
  75.7 1.8 %pad_maximum_fusion.1 = f32[5120,128]{1,0:T(8,128)S(1)} fusion(f32[512,128]{1,0:T(8,128)S(1)} %collective-permute-done.6, f32[1536,128]{1,0:T(8,128)} %copy-done.4, f32[1536,128]{1,0:T(8,128)} %copy-done.2, f32[1536,128]{1,0:T(8,128)} %collective-permute-done.4), kind=kLoop, calls=%fused_computation.5 | loop fusion | flops 1966080 | bytes 5242880 | tf_op jit(solution)/shard_map/concatenate | solution.py:64
  77.5 8.3 %gather_fusion.3 = f32[648,64,128]{2,1,0:T(8,128)} fusion(f32[80,64,128]{2,1,0:T(8,128)S(1)} %bitcast.39, s32[1024]{0:T(1024)S(1)} %pad_clamp_fusion), kind=kCustom, calls=%fused_computation.3 | custom fusion | bytes 42469920 | tf_op jit(solution)/shard_map/gather | solution.py:32
  85.9 0.0 copy-start.1
  85.9 18.4 %fusion.10 = f32[24,128,64]{1,2,0:T(8,128)S(1)} fusion(f32[24,1728,128]{2,1,0:T(8,128)} %bitcast.41, f32[24,64,1728]{2,1,0:T(8,128)} %bitcast.38), kind=kOutput, calls=%fused_computation.27 | convolution fusion | flops 4076863488 | bytes 32636928 | tf_op jit(solution)/shard_map/irm,imk->irk/dot_general | solution.py:66
  104.2 0.0 copy-done.1
  104.2 1.1 %fusion.1 = f32[1536,128]{1,0:T(8,128)} fusion(f32[1536,128]{1,0:T(8,128)S(1)} %copy-done.1, f32[24,128,64]{1,2,0:T(8,128)S(1)} %fusion.10, f32[24,128,64]{1,2,0:T(8,128)S(1)} %fusion.9), kind=kLoop, calls=%fused_computation.8 | loop fusion | flops 1179648 | bytes 3145728 | tf_op jit(solution)/shard_map/sub | solution.py:71
  (4 shorter events, 0.0 us)
Async XLA Ops:
  0.0 24.8 %collective-permute-start.1 = (f32[1536,128]{1,0:T(8,128)}, f32[1536,128]{1,0:T(8,128)S(1)}, u32[]{:S(2)}, u32[]{:S(2)}) collective-permute-start(f32[1536,128]{1,0:T(8,128)} %param.5), channel_id=1, source_target_pairs={{1,0},{2,1},{3,2},{4,3},{5,4},{6,5},{7,6},{8,7},{9,8},{10,9},{11,1... | collective-permute-start | bytes 2359304 | tf_op jit(solution)/shard_map/ppermute | solution.py:24
  6.4 20.0 %collective-permute-start = (f32[1536,128]{1,0:T(8,128)}, f32[1536,128]{1,0:T(8,128)}, u32[]{:S(2)}, u32[]{:S(2)}) collective-permute-start(f32[1536,128]{1,0:T(8,128)} %param.5), channel_id=1, source_target_pairs={{0,1},{1,2},{2,3},{3,4},{4,5},{5,6},{6,7},{7,8},{8,9},{9,10},{10,1... | collective-permute-start | bytes 2359304 | tf_op jit(solution)/shard_map/ppermute | solution.py:23
  6.4 3.7 %collective-permute-start.2 = (s32[1,8]{1,0:T(1,128)}, s32[1,8]{1,0:T(1,128)S(1)}, u32[]{:S(2)}, u32[]{:S(2)}) collective-permute-start(s32[1,8]{1,0:T(1,128)} %param.7), channel_id=1, source_target_pairs={{0,4},{1,5},{2,6},{3,7},{4,0},{5,1},{6,2},{7,3},{8,12},{9,13},{10,... | collective-permute-start | bytes 104 | tf_op jit(solution)/shard_map/ppermute | solution.py:13
  11.9 14.5 %copy-start = (f32[1536,128]{1,0:T(8,128)S(1)}, f32[1536,128]{1,0:T(8,128)}, u32[]{:S(2)}) copy-start(f32[1536,128]{1,0:T(8,128)} %param.5) | copy-start | bytes 2359300
  12.1 12.7 %collective-permute-start.3 = (f32[512,128]{1,0:T(8,128)S(1)}, f32[512,128]{1,0:T(8,128)S(1)}, u32[]{:S(2)}, u32[]{:S(2)}) collective-permute-start(f32[512,128]{1,0:T(8,128)S(1)} %bitcast_multiply_fusion.1), channel_id=1, source_target_pairs={{0,4},{1,5},{2,6},{3,7},{4,0},{5,1},{6,2},{7,3},{8,12},{9,13},{10,... | collective-permute-start | bytes 786440 | tf_op jit(solution)/shard_map/ppermute | solution.py:13
  24.8 0.7 copy-start.5
  25.5 0.9 copy-start.3
  54.6 20.3 %copy-start.2 = (f32[1536,128]{1,0:T(8,128)}, f32[1536,128]{1,0:T(8,128)S(1)}, u32[]{:S(2)}) copy-start(f32[1536,128]{1,0:T(8,128)S(1)} %fusion.2) | copy-start | bytes 2359300
  54.6 20.3 %collective-permute-start.5 = (f32[1536,128]{1,0:T(8,128)S(1)}, f32[1536,128]{1,0:T(8,128)S(1)}, u32[]{:S(2)}, u32[]{:S(2)}) collective-permute-start(f32[1536,128]{1,0:T(8,128)S(1)} %fusion.2), channel_id=1, source_target_pairs={{1,0},{2,1},{3,2},{4,3},{5,4},{6,5},{7,6},{8,7},{9,8},{10,9},{11,1... | collective-permute-start | bytes 2359304 | tf_op jit(solution)/shard_map/ppermute | solution.py:24
  59.3 16.5 %collective-permute-start.4 = (f32[1536,128]{1,0:T(8,128)S(1)}, f32[1536,128]{1,0:T(8,128)}, u32[]{:S(2)}, u32[]{:S(2)}) collective-permute-start(f32[1536,128]{1,0:T(8,128)S(1)} %fusion.2), channel_id=1, source_target_pairs={{0,1},{1,2},{2,3},{3,4},{4,5},{5,6},{6,7},{7,8},{8,9},{9,10},{10,1... | collective-permute-start | bytes 2359304 | tf_op jit(solution)/shard_map/ppermute | solution.py:23
  60.0 14.9 %collective-permute-start.6 = (f32[512,128]{1,0:T(8,128)S(1)}, f32[512,128]{1,0:T(8,128)S(1)}, u32[]{:S(2)}, u32[]{:S(2)}) collective-permute-start(f32[512,128]{1,0:T(8,128)S(1)} %bitcast_multiply_fusion), channel_id=1, source_target_pairs={{0,4},{1,5},{2,6},{3,7},{4,0},{5,1},{6,2},{7,3},{8,12},{9,13},{10,... | collective-permute-start | bytes 786440 | tf_op jit(solution)/shard_map/ppermute | solution.py:13
  74.9 0.9 copy-start.4
  85.9 18.4 %copy-start.1 = (f32[1536,128]{1,0:T(8,128)S(1)}, f32[1536,128]{1,0:T(8,128)}, u32[]{:S(2)}) copy-start(f32[1536,128]{1,0:T(8,128)} %param.5) | copy-start | bytes 2359300
where the time goes:
time: 106 us; the launch traced here: 105 us
  matrix products  36.4 us (34%)
  local copies, waits for them, and re-layouts  33.4 us (32%)
  waiting for transfers between devices  18.5 us (17%)
  starting transfers between devices  11.2 us (11%)
  other arithmetic  5.61 us (5%)
    dot_general x2, matrix products, apply_operator(): jnp.einsum('irm,imk->irk', ham_slab, picked, precision=lax.Precision.HIGH...  36.4 us
    ppermute x3, waiting for transfers between devices, partner(): return lax.ppermute(value, axis, pairs)  18.5 us
    gather x2, local copies, waits for them, and re-layouts, gather_blocks(): picked = blocks[positions]  16.7 us
    unnamed x13, local copies, waits for them, and re-layouts  14.2 us
    ppermute x2, starting transfers between devices, extended_2(): after = lax.ppermute(leading, axis, down)  11.1 us
    concatenate x2, other arithmetic, apply_operator(): extended = jnp.concatenate([band_panel, remote], axis=0)  3.4 us
    gather x2, local copies, waits for them, and re-layouts, apply_operator(): vectors.reshape(block_rows, block_size, sub_width)[local_index]  2.26 us
  transfers between devices with their start and end apart: 7, of which 2 were waited for; matrix products, arithmetic and copies ran while one was open for 15% of the time, Pallas kernels for 0%

commit v1 on v0

v1 whole, which is shorter than its diff:
```python
import functools

import jax
import jax.numpy as jnp
from jax import lax
from jax.experimental import pallas as pl
from jax.experimental.pallas import tpu as pltpu
from jax.sharding import PartitionSpec as P

CENTER = 0.25
HALF_WIDTH = 1.5
REACH = 13


def partner(value, axis, bit):
    mask = 2**bit
    pairs = [(source, source ^ mask) for source in range(lax.axis_size(axis))]
    return lax.ppermute(value, axis, pairs)


def halo(above, below, axis):
    devices = lax.axis_size(axis)
    up = [(i, (i + 1) % devices) for i in range(devices)]
    down = [(j, i) for i, j in up]
    return lax.ppermute(above, axis, up), lax.ppermute(below, axis, down)


def split(value):
    high = value.astype(jnp.bfloat16)
    return high, (value - high.astype(jnp.float32)).astype(jnp.bfloat16)


def band_kernel(pairs, entries, slots, size, inverse, ham_t, band, staged, sems):
    depth = entries * size
    lane = lax.broadcasted_iota(jnp.int32, (size, 2 * size), 1)

    def fetch(p):
        return pltpu.make_async_copy(
            ham_t.at[:, pl.ds(p * 2 * size, 2 * size)],
            staged.at[p, pl.ds(0, depth), :],
            sems.at[p],
        )

    for p in range(pairs):
        fetch(p).start()
    for p in range(pairs):
        staged[p, depth:, :] = jnp.zeros((size, 2 * size), jnp.float32)

    def one_pair(p, carry):
        fetch(p).wait()
        for q in range(slots):
            even = inverse[2 * p, q] * size
            odd = inverse[2 * p + 1, q] * size
            first = staged[p, pl.ds(pl.multiple_of(even, size), size), :]
            second = staged[p, pl.ds(pl.multiple_of(odd, size), size), :]
            high, low = split(jnp.where(lane < size, first, second))
            band[p, q * size : (q + 1) * size, : 2 * size] = high
            band[p, q * size : (q + 1) * size, 2 * size :] = low
        return carry

    lax.fori_loop(0, pairs, one_pair, 0)


def make_band(inverse, ham_t, size):
    depth, rows = ham_t.shape
    entries = depth // size
    pairs = rows // (2 * size)
    slots = inverse.shape[1]
    return pl.pallas_call(
        functools.partial(band_kernel, pairs, entries, slots, size),
        out_shape=pltpu.VMEM((pairs, slots * size, 4 * size), jnp.bfloat16),
        in_specs=[
            pl.BlockSpec(memory_space=pltpu.SMEM),
            pl.BlockSpec(memory_space=pl.ANY),
        ],
        out_specs=pl.BlockSpec(memory_space=pltpu.VMEM),
        scratch_shapes=[
            pltpu.VMEM((pairs, depth + size, 2 * size), jnp.float32),
            pltpu.SemaphoreType.DMA((pairs,)),
        ],
        compiler_params=pltpu.CompilerParams(vmem_limit_bytes=16 * 2**20),
        cost_estimate=pl.CostEstimate(
            flops=0, bytes_accessed=2 * 4 * depth * rows, transcendentals=0
        ),
        name="band",
    )(inverse, ham_t)


def apply_kernel(size, first, asked, own, lower, upper, far, band, *rest):
    if first:
        result, to_lower, to_upper, to_far, turned = rest
    else:
        start, result, turned = rest
    width = own.shape[1]
    tile = 2 * size
    near = lower.shape[0]
    rows = own.shape[0]
    panel = rows + 2 * near
    pieces = [(0, lower), (near, own), (near + rows, upper), (panel, far)]
    total = panel + far.shape[0]

    def rows_of(begin):
        parts = []
        for offset, ref in pieces:
            lo = max(begin, offset)
            hi = min(begin + tile, offset + ref.shape[0])
            if lo < hi:
                parts.append(ref[lo - offset : hi - offset, :])
        return parts[0] if len(parts) == 1 else jnp.concatenate(parts, axis=0)

    for begin in range(0, total, tile):
        high, low = split(rows_of(begin).T)
        turned[:width, begin : begin + tile] = high
        turned[width:, begin : begin + tile] = low

    reach = tile + 2 * near
    for p in range(rows // tile):
        at = p * tile
        sums = jnp.dot(
            turned[:, at : at + reach],
            band[p, :reach, :],
            preferred_element_type=jnp.float32,
        ) + jnp.dot(
            turned[:, panel:], band[p, reach:, :], preferred_element_type=jnp.float32
        )
        small = sums[width:, tile:] + sums[width:, :tile] + sums[:width, tile:]
        product = (small + sums[:width, :tile]).T
        here = own[at : at + tile, :]
        shifted = product - CENTER * here
        if first:
            value = shifted * (1.0 / HALF_WIDTH)
            result[at : at + tile, :] = value
            count = min(tile, near - at)
            if count > 0:
                to_lower[at : at + count, :] = value[:count]
            skip = max(0, rows - near - at)
            if skip < tile:
                base = at + skip - (rows - near)
                to_upper[base : base + tile - skip, :] = value[skip:]
        else:
            result[at : at + tile, :] = (
                2.0 / HALF_WIDTH * shifted - start[at : at + tile, :]
            )
    if first:
        for slot in range(to_far.shape[0] // size):
            row = pl.multiple_of(asked[slot] * size, size)
            to_far[slot * size : (slot + 1) * size, :] = result[pl.ds(row, size), :]


def run_apply(size, asked, own, lower, upper, far, band, start=None):
    first = start is None
    rows, width = own.shape
    near = lower.shape[0]
    total = rows + 2 * near + far.shape[0]
    f32 = jnp.float32
    out_shape = [jax.ShapeDtypeStruct(own.shape, f32)]
    if first:
        out_shape += [
            jax.ShapeDtypeStruct(lower.shape, f32),
            jax.ShapeDtypeStruct(upper.shape, f32),
            jax.ShapeDtypeStruct(far.shape, f32),
        ]
    operands = [asked, own, lower, upper, far, band] + ([] if first else [start])
    vmem = pl.BlockSpec(memory_space=pltpu.VMEM)
    return pl.pallas_call(
        functools.partial(apply_kernel, size, first),
        out_shape=out_shape,
        in_specs=[pl.BlockSpec(memory_space=pltpu.SMEM)] + [vmem] * (len(operands) - 1),
        out_specs=[vmem] * len(out_shape),
        scratch_shapes=[pltpu.VMEM((2 * width, total), jnp.bfloat16)],
        compiler_params=pltpu.CompilerParams(vmem_limit_bytes=16 * 2**20),
        cost_estimate=pl.CostEstimate(
            flops=2 * 2 * width * band.size, bytes_accessed=2 * band.size, transcendentals=0
        ),
        name="apply",
    )(*operands)


def far_kernel(size, asked, own, out):
    for slot in range(out.shape[0] // size):
        row = pl.multiple_of(asked[slot] * size, size)
        out[slot * size : (slot + 1) * size, :] = own[pl.ds(row, size), :]


def gather_far(asked, own, size):
    return pl.pallas_call(
        functools.partial(far_kernel, size),
        out_shape=jax.ShapeDtypeStruct((asked.shape[0] * size, own.shape[1]), own.dtype),
        in_specs=[
            pl.BlockSpec(memory_space=pltpu.SMEM),
            pl.BlockSpec(memory_space=pltpu.VMEM),
        ],
        out_specs=pl.BlockSpec(memory_space=pltpu.VMEM),
        compiler_params=pltpu.CompilerParams(vmem_limit_bytes=4 * 2**20),
        name="far",
    )(asked, own)


def per_device(hamiltonian, subspace, block_cols, far_list):
    block_rows, entries = block_cols.shape
    size = hamiltonian.shape[1] // entries
    slot_total = far_list.shape[1]
    device_count = lax.axis_size("rows")
    first_row = lax.axis_index("rows") * block_rows
    block_total = block_rows * device_count
    swap_level = (device_count // 8).bit_length() - 1
    near = REACH * size
    rows = block_rows * size

    asked_list = partner(far_list, "rows", swap_level)
    lower, upper = halo(subspace[rows - near :], subspace[:near], "rows")
    asked = jnp.clip(asked_list[0] - first_row, 0, block_rows - 1)
    outgoing = gather_far(asked, subspace, size)

    pair_row = first_row + 2 * (jnp.arange(block_rows, dtype=jnp.int32)[:, None] // 2)
    reach = 2 + 2 * REACH
    places = jnp.where(
        block_cols < block_total,
        (block_cols - pair_row + REACH + block_total) % block_total,
        reach + block_cols - block_total,
    )
    slots = jnp.arange(reach + slot_total, dtype=jnp.int32)
    entry = jnp.arange(entries, dtype=jnp.int32)[None, :, None]
    hit = places[:, :, None] == slots[None, None, :]
    inverse = entries + jnp.sum(jnp.where(hit, entry - entries, 0), axis=1)

    far = partner(outgoing, "rows", swap_level)
    inverse, _ = lax.optimization_barrier((inverse, outgoing))
    band = make_band(inverse, hamiltonian.T, size)

    value, to_lower, to_upper, to_far = run_apply(
        size, asked, subspace, lower, upper, far, band
    )
    far = partner(to_far, "rows", swap_level)
    lower, upper = halo(to_upper, to_lower, "rows")
    return run_apply(size, asked, value, lower, upper, far, band, subspace)[0]


def solution(mesh):
    placed = (P("rows", None), P("rows", None), P("rows", None), P("rows", None))
    return jax.shard_map(
        per_device, mesh=mesh, in_specs=placed, out_specs=P("rows", None), check_vma=False
    )
```

time: 106 us -> 46.1 us (0.43)
  matrix products: 36.4 us -> 0 us
  local copies, waits for them, and re-layouts: 33.4 us -> 6.42 us
  Pallas kernels: 0 us -> 15.9 us
  waiting for transfers between devices: 18.5 us -> 10.2 us
  other arithmetic: 5.61 us -> 0.99 us
    dot_general x2 -> x0, matrix products: 36.4 us -> none  [apply_operator(): jnp.einsum('irm,imk->irk', ham_slab, picked, precision=lax.Precision.HIGH...]
    gather x4 -> x0, local copies, waits for them, and re-layouts: 19 us -> none  [the longest x2 16.7 us: gather_blocks(): picked = blocks[positions]]
    pallas_call x0 -> x4, Pallas kernels: none -> 15.9 us  [the longest x2 10.2 us: run_apply(): pl.pallas_call(functools.partial(apply_kernel, size, first), out_shape=ou...]
    unnamed x13 -> x6, local copies, waits for them, and re-layouts: 14.2 us -> 5.14 us
    ppermute x3, waiting for transfers between devices: 18.5 us -> 10.2 us  [partner(): return lax.ppermute(value, axis, pairs)]
    concatenate x2 -> x0, other arithmetic: 3.4 us -> none  [apply_operator(): extended = jnp.concatenate([band_panel, remote], axis=0)]
    ppermute x3, starting transfers between devices: 0.14 us -> 3.04 us  [partner(): return lax.ppermute(value, axis, pairs)]
    ppermute x4, starting transfers between devices: 11.1 us -> 9.1 us  [halo(): return (lax.ppermute(above, axis, up), lax.ppermute(below, axis, down))]
  transfers between devices with their start and end apart: 7 -> 7, of which waited for: 2 -> 2; matrix products, arithmetic and copies ran while one was open for 15% -> 5% of each run, Pallas kernels for 0% -> 13%
where the time goes in v1:
time: 46.1 us; the launch traced here: 45.8 us
  Pallas kernels  15.9 us (34%)
  starting transfers between devices  12.1 us (26%)
  waiting for transfers between devices  10.2 us (22%)
  local copies, waits for them, and re-layouts  6.42 us (14%)
  other arithmetic  0.99 us (2%)
    ppermute x3, waiting for transfers between devices, partner(): return lax.ppermute(value, axis, pairs)  10.2 us
    pallas_call x2, Pallas kernels, run_apply(): pl.pallas_call(functools.partial(apply_kernel, size, first), out_shape=ou...  10.2 us
    ppermute x4, starting transfers between devices, halo(): return (lax.ppermute(above, axis, up), lax.ppermute(below, axis, down))  9.1 us
    pallas_call x1, Pallas kernels, make_band(): pl.pallas_call(functools.partial(band_kernel, pairs, entries, slots, size...  5.2 us
    unnamed x6, local copies, waits for them, and re-layouts  5.14 us
    ppermute x3, starting transfers between devices, partner(): return lax.ppermute(value, axis, pairs)  3.04 us
    slice x1, local copies, waits for them, and re-layouts, per_device(): lower, upper = halo(subspace[rows - near:], subspace[:near], 'rows')  1.19 us
  transfers between devices with their start and end apart: 7, of which 2 were waited for; matrix products, arithmetic and copies ran while one was open for 5% of the time, Pallas kernels for 13%

profile of v1, /device:TPU:0, one launch (start us, length us, event | category | flops | bytes accessed | tf_op | source)
XLA Modules:
  0.0 45.8 jit_solution(11935808414278427639)
XLA Ops:
  0.0 0.0 copy-start.1
  0.0 3.0 %collective-permute-start = (s32[1,8]{1,0:T(1,128)}, s32[1,8]{1,0:T(1,128)S(1)}, u32[]{:S(2)}, u32[]{:S(2)}) collective-permute-start(s32[1,8]{1,0:T(1,128)} %param.7), channel_id=1, source_target_pairs={{0,4},{1,5},{2,6},{3,7},{4,0},{5,1},{6,2},{7,3},{8,12},{9,13},{10,... | collective-permute-start | bytes 104 | tf_op jit(solution)/shard_map/ppermute | solution.py:18
  3.0 1.2 %fusion.6 = (f32[832,128]{1,0:T(8,128)S(1)}, f32[832,128]{1,0:T(8,128)S(1)}) fusion(f32[1536,128]{1,0:T(8,128)} %rest_0_.1), kind=kLoop, calls=%fused_computation.17 | loop fusion | bytes 1703936 | tf_op jit(solution)/shard_map/slice | solution.py:211
  4.2 3.7 %collective-permute-start.2 = (f32[832,128]{1,0:T(8,128)S(1)}, f32[832,128]{1,0:T(8,128)S(1)}, u32[]{:S(2)}, u32[]{:S(2)}) collective-permute-start(f32[832,128]{1,0:T(8,128)S(1)} %get-tuple-element.15), channel_id=1, source_target_pairs={{1,0},{2,1},{3,2},{4,3},{5,4},{6,5},{7,6},{8,7},{9,8},{10,9},{11,1... | collective-permute-start | bytes 1277960 | tf_op jit(solution)/shard_map/ppermute | solution.py:25
  7.9 0.0 collective-permute-start.1
  7.9 0.8 %fusion = s32[24,27]{1,0:T(8,128)S(1)} fusion(s32[24,27]{1,0:T(8,128)} %param.6, s32[24]{0:T(128)S(1)} %fusion.5), kind=kLoop, calls=%fused_computation.3 | loop fusion | flops 7128 | bytes 5280 | tf_op jit(solution)/shard_map/jit(_where)/select_n | solution.py:217
  8.7 0.1 copy.5
  8.8 0.0 collective-permute-done
  8.8 0.0 copy-start
  8.8 1.1 %copy-done = f32[1536,128]{1,0:T(8,128)S(1)} copy-done((f32[1536,128]{1,0:T(8,128)S(1)}, f32[1536,128]{1,0:T(8,128)}, u32[]{:S(2)}) %copy-start) | copy-done | bytes 786456
  9.9 0.6 %far.1 = f32[512,128]{1,0:T(8,128)S(1)} custom-call(s32[8]{0:T(128)S(1)} %clamp_bitcast_fusion.asked, f32[1536,128]{1,0:T(8,128)S(1)} %copy-done), custom_call_target="tpu_custom_call" | custom-call | tf_op jit(solution)/shard_map/far/pallas_call | solution.py:186
  10.5 0.1 collective-permute-start.3
  10.6 0.2 select_reduce_fusion
  10.8 0.0 copy-start.2
  10.8 4.0 %copy-done.2 = f32[1536,1728]{0,1:T(8,128)S(1)} copy-done((f32[1536,1728]{0,1:T(8,128)S(1)}, f32[1536,1728]{0,1:T(8,128)}, u32[]{:S(2)}) %copy-start.2) | copy-done | bytes 10616856
  14.8 5.2 %band.1 = bf16[12,2304,256]{2,1,0:T(8,128)(2,1)S(1)} custom-call(s32[24,36]{1,0:T(8,128)S(1)} %broadcast_add_fusion.inverse, f32[1728,1536]{1,0:T(8,128)S(1)} %bitcast.3), custom_call_target="tpu_custom_call" | custom-call | bytes 21233664 | tf_op jit(solution)/shard_map/band/pallas_call | solution.py:69
  20.0 1.5 %collective-permute-done.3.far = f32[512,128]{1,0:T(8,128)S(1)} collective-permute-done((f32[512,128]{1,0:T(8,128)S(1)}, f32[512,128]{1,0:T(8,128)S(1)}, u32[]{:S(2)}, u32[]{:S(2)}) %collective-permute-start.3) | collective-permute-done | bytes 262176 | tf_op jit(solution)/shard_map/ppermute | solution.py:18
  21.5 0.0 collective-permute-done.2.upper
  21.5 0.0 collective-permute-done.1.lower
  21.5 0.0 copy-done.1
  21.5 4.6 %apply.2 = (f32[1536,128]{1,0:T(8,128)S(1)}, f32[832,128]{1,0:T(8,128)S(1)}, f32[832,128]{1,0:T(8,128)S(1)}, f32[512,128]{1,0:T(8,128)S(1)}) custom-call(s32[8]{0:T(128)S(1)} %clamp_bitcast_fusion.asked, f32[1536,128]{1,0:T(8,128)S(1)} %copy-done.1, f32[832,128]{1,0:T(8,128)S(1)} %collective-permute-done.1.lower, ...), custom_call_target="tpu_custom_call" | custom-call | flops 3623878656 | bytes 14155776 | tf_op jit(solution)/shard_map/apply/pallas_call | solution.py:165
  26.2 0.1 collective-permute-start.4
  26.2 5.3 %collective-permute-start.5 = (f32[832,128]{1,0:T(8,128)S(1)}, f32[832,128]{1,0:T(8,128)S(1)}, u32[]{:S(2)}, u32[]{:S(2)}) collective-permute-start(f32[832,128]{1,0:T(8,128)S(1)} %get-tuple-element.13), channel_id=1, source_target_pairs={{1,0},{2,1},{3,2},{4,3},{5,4},{6,5},{7,6},{8,7},{9,8},{10,9},{11,1... | collective-permute-start | bytes 1277960 | tf_op jit(solution)/shard_map/ppermute | solution.py:25
  31.6 0.0 collective-permute-start.6
  31.6 8.7 %collective-permute-done.6.far = f32[512,128]{1,0:T(8,128)S(1)} collective-permute-done((f32[512,128]{1,0:T(8,128)S(1)}, f32[512,128]{1,0:T(8,128)S(1)}, u32[]{:S(2)}, u32[]{:S(2)}) %collective-permute-start.6) | collective-permute-done | bytes 262176 | tf_op jit(solution)/shard_map/ppermute | solution.py:18
  40.3 0.0 collective-permute-done.4.lower
  40.3 0.0 collective-permute-done.5.upper
  40.3 5.5 %apply.3 = f32[1536,128]{1,0:T(8,128)} custom-call(s32[8]{0:T(128)S(1)} %clamp_bitcast_fusion.asked, f32[1536,128]{1,0:T(8,128)S(1)} %get-tuple-element.11.own, f32[832,128]{1,0:T(8,128)S(1)} %collective-permute-done.4.lower, f32[832,128]{1,0:T(8,128)S(1)} %collective-permute-done.5.upper, f32[512,128]{1,0:T(8,128)S(1)} %collective-permute-done.6.far, ...), custom_call_target="tpu_custom_call" | custom-call | flops 3623878656 | bytes 14155776 | tf_op jit(solution)/shard_map/apply/pallas_call | solution.py:165
  (4 shorter events, 0.0 us)
Async XLA Ops:
  0.0 21.5 %copy-start.1 = (f32[1536,128]{1,0:T(8,128)S(1)}, f32[1536,128]{1,0:T(8,128)}, u32[]{:S(2)}) copy-start(f32[1536,128]{1,0:T(8,128)} %rest_0_.1) | copy-start | bytes 2359300
  0.0 8.8 %collective-permute-start = (s32[1,8]{1,0:T(1,128)}, s32[1,8]{1,0:T(1,128)S(1)}, u32[]{:S(2)}, u32[]{:S(2)}) collective-permute-start(s32[1,8]{1,0:T(1,128)} %param.7), channel_id=1, source_target_pairs={{0,4},{1,5},{2,6},{3,7},{4,0},{5,1},{6,2},{7,3},{8,12},{9,13},{10,... | collective-permute-start | bytes 104 | tf_op jit(solution)/shard_map/ppermute | solution.py:18
  4.2 17.3 %collective-permute-start.2 = (f32[832,128]{1,0:T(8,128)S(1)}, f32[832,128]{1,0:T(8,128)S(1)}, u32[]{:S(2)}, u32[]{:S(2)}) collective-permute-start(f32[832,128]{1,0:T(8,128)S(1)} %get-tuple-element.15), channel_id=1, source_target_pairs={{1,0},{2,1},{3,2},{4,3},{5,4},{6,5},{7,6},{8,7},{9,8},{10,9},{11,1... | collective-permute-start | bytes 1277960 | tf_op jit(solution)/shard_map/ppermute | solution.py:25
  7.9 13.6 %collective-permute-start.1 = (f32[832,128]{1,0:T(8,128)S(1)}, f32[832,128]{1,0:T(8,128)S(1)}, u32[]{:S(2)}, u32[]{:S(2)}) collective-permute-start(f32[832,128]{1,0:T(8,128)S(1)} %get-tuple-element.16), channel_id=1, source_target_pairs={{0,1},{1,2},{2,3},{3,4},{4,5},{5,6},{6,7},{7,8},{8,9},{9,10},{10,1... | collective-permute-start | bytes 1277960 | tf_op jit(solution)/shard_map/ppermute | solution.py:25
  8.8 1.1 %copy-start = (f32[1536,128]{1,0:T(8,128)S(1)}, f32[1536,128]{1,0:T(8,128)}, u32[]{:S(2)}) copy-start(f32[1536,128]{1,0:T(8,128)} %rest_0_.1) | copy-start | bytes 2359300
  10.5 11.0 %collective-permute-start.3 = (f32[512,128]{1,0:T(8,128)S(1)}, f32[512,128]{1,0:T(8,128)S(1)}, u32[]{:S(2)}, u32[]{:S(2)}) collective-permute-start(f32[512,128]{1,0:T(8,128)S(1)} %far.1), channel_id=1, source_target_pairs={{0,4},{1,5},{2,6},{3,7},{4,0},{5,1},{6,2},{7,3},{8,12},{9,13},{10,... | collective-permute-start | bytes 786440 | tf_op jit(solution)/shard_map/ppermute | solution.py:18
  10.8 4.0 %copy-start.2 = (f32[1536,1728]{0,1:T(8,128)S(1)}, f32[1536,1728]{0,1:T(8,128)}, u32[]{:S(2)}) copy-start(f32[1536,1728]{0,1:T(8,128)} %param.4) | copy-start | bytes 31850500
  26.2 14.1 %collective-permute-start.4 = (f32[832,128]{1,0:T(8,128)S(1)}, f32[832,128]{1,0:T(8,128)S(1)}, u32[]{:S(2)}, u32[]{:S(2)}) collective-permute-start(f32[832,128]{1,0:T(8,128)S(1)} %get-tuple-element.12), channel_id=1, source_target_pairs={{0,1},{1,2},{2,3},{3,4},{4,5},{5,6},{6,7},{7,8},{8,9},{9,10},{10,1... | collective-permute-start | bytes 1277960 | tf_op jit(solution)/shard_map/ppermute | solution.py:25
  26.2 14.1 %collective-permute-start.5 = (f32[832,128]{1,0:T(8,128)S(1)}, f32[832,128]{1,0:T(8,128)S(1)}, u32[]{:S(2)}, u32[]{:S(2)}) collective-permute-start(f32[832,128]{1,0:T(8,128)S(1)} %get-tuple-element.13), channel_id=1, source_target_pairs={{1,0},{2,1},{3,2},{4,3},{5,4},{6,5},{7,6},{8,7},{9,8},{10,9},{11,1... | collective-permute-start | bytes 1277960 | tf_op jit(solution)/shard_map/ppermute | solution.py:25
  31.6 8.7 %collective-permute-start.6 = (f32[512,128]{1,0:T(8,128)S(1)}, f32[512,128]{1,0:T(8,128)S(1)}, u32[]{:S(2)}, u32[]{:S(2)}) collective-permute-start(f32[512,128]{1,0:T(8,128)S(1)} %get-tuple-element.14), channel_id=1, source_target_pairs={{0,4},{1,5},{2,6},{3,7},{4,0},{5,1},{6,2},{7,3},{8,12},{9,13},{10,... | collective-permute-start | bytes 786440 | tf_op jit(solution)/shard_map/ppermute | solution.py:18

commit v2 on v0

v2 whole, which is shorter than its diff:
```python
import functools

import jax
import jax.numpy as jnp
from jax import lax
from jax.experimental import pallas as pl
from jax.experimental.pallas import tpu as pltpu
from jax.sharding import PartitionSpec as P

CENTER = 0.25
HALF_WIDTH = 1.5
REACH = 13
PARTS = 2
F32 = jnp.float32
VMEM = pl.BlockSpec(memory_space=pltpu.VMEM)
SMEM = pl.BlockSpec(memory_space=pltpu.SMEM)


def partner(value, axis, bit):
    mask = 2**bit
    pairs = [(source, source ^ mask) for source in range(lax.axis_size(axis))]
    return lax.ppermute(value, axis, pairs)


def halo(above, below, axis):
    devices = lax.axis_size(axis)
    up = [(i, (i + 1) % devices) for i in range(devices)]
    down = [(j, i) for i, j in up]
    return lax.ppermute(above, axis, up), lax.ppermute(below, axis, down)


def split(value):
    high = value.astype(jnp.bfloat16)
    return high, (value - high.astype(F32)).astype(jnp.bfloat16)


def fold(sums):
    width, tile = sums.shape[0] // 2, sums.shape[1] // 2
    small = sums[width:, tile:] + sums[width:, :tile] + sums[:width, tile:]
    return small + sums[:width, :tile]


def params(limit):
    return pltpu.CompilerParams(vmem_limit_bytes=limit * 2**20)


def cost(flops, moved):
    return pl.CostEstimate(flops=flops, bytes_accessed=moved, transcendentals=0)


class Plan:
    def __init__(self, size, rows, width, slots):
        self.size, self.rows, self.width = size, rows, width
        self.tile = 2 * size
        self.pairs = rows // self.tile
        self.near = (REACH + 1) // 2
        self.far = slots * size // self.tile
        self.edge = self.near * self.tile
        self.part = width // PARTS
        self.outer = 2 * self.near + self.far
        self.places = 2 * (self.outer + self.pairs)

    def outer_range(self, p):
        extra = p + self.near - self.pairs + 1
        if isinstance(p, int):
            return min(p, self.near), self.near + self.far + max(0, extra)
        return jnp.minimum(p, self.near), self.near + self.far + jnp.maximum(0, extra)

    def own_range(self, p):
        return max(0, p - self.near), min(self.pairs, p + self.near + 1)


def write_far(plan, asked, source, write):
    tile, size = plan.tile, plan.size
    lane = lax.broadcasted_iota(jnp.int32, (source.shape[0], tile), 1)

    def block(slot, want):
        index = asked[slot]
        at = pl.multiple_of((index // 2) * tile, tile)
        value = source[:, pl.ds(at, tile)]
        return jnp.where(index % 2 == want, value, pltpu.roll(value, size, 1))

    for t in range(plan.far):
        value = jnp.where(lane < size, block(2 * t, 0), block(2 * t + 1, 1))
        write(t * tile, value)


def pack_kernel(plan, natural, turned, *sends):
    tile, edge, part = plan.tile, plan.edge, plan.part
    for p in range(plan.pairs):
        turned[:, p * tile : (p + 1) * tile] = natural[p * tile : (p + 1) * tile, :].T
    for h in range(PARTS):
        rows = slice(h * part, (h + 1) * part)
        sends[2 * h][...] = turned[rows, plan.rows - edge :]
        sends[2 * h + 1][...] = turned[rows, :edge]


def pack(plan, natural):
    edge = jax.ShapeDtypeStruct((plan.part, plan.edge), F32)
    return pl.pallas_call(
        functools.partial(pack_kernel, plan),
        out_shape=[pltpu.VMEM((plan.width, plan.rows), F32)] + [edge] * (2 * PARTS),
        in_specs=[VMEM],
        out_specs=[VMEM] * (1 + 2 * PARTS),
        compiler_params=params(8),
        name="pack",
    )(natural)


def far_kernel(plan, asked, turned, out):
    def write(at, value):
        out[:, at : at + plan.tile] = value

    write_far(plan, asked, turned, write)


def gather_far(plan, asked, turned):
    return pl.pallas_call(
        functools.partial(far_kernel, plan),
        out_shape=jax.ShapeDtypeStruct((plan.width, plan.far * plan.tile), F32),
        in_specs=[SMEM, VMEM],
        out_specs=VMEM,
        compiler_params=params(8),
        name="far",
    )(asked, turned)


def band_kernel(plan, depth, inverse, ham_t, vectors, band, inner, staged, halves, sems):
    size, tile, width = plan.size, plan.tile, plan.width
    lane = lax.broadcasted_iota(jnp.int32, (size, tile), 1)

    def fetch(p):
        return pltpu.make_async_copy(
            ham_t.at[:, pl.ds(pl.multiple_of(p * tile, tile), tile)],
            staged.at[p, pl.ds(0, depth), :],
            sems.at[p],
        )

    for p in range(plan.pairs):
        fetch(p).start()
    for p in range(plan.pairs):
        staged[p, depth:, :] = jnp.zeros((size, tile), F32)
    for p in range(plan.pairs):
        at = p * tile
        high, low = split(vectors[:, at : at + tile])
        halves[:width, at : at + tile] = high
        halves[width:, at : at + tile] = low

    def place(p, q, at):
        even = pl.multiple_of(inverse[2 * p, q] * size, size)
        odd = pl.multiple_of(inverse[2 * p + 1, q] * size, size)
        first = staged[p, pl.ds(even, size), :]
        second = staged[p, pl.ds(odd, size), :]
        high, low = split(jnp.where(lane < size, first, second))
        band[p, pl.ds(at, size), :tile] = high
        band[p, pl.ds(at, size), tile:] = low

    def one_pair(p, carry):
        fetch(p).wait()
        for q in range(2 * plan.outer, plan.places):
            place(p, q, q * size)
        sums = jnp.dot(
            halves[...], band[p, plan.outer * tile :, :], preferred_element_type=F32
        )
        inner[:, pl.ds(pl.multiple_of(p * tile, tile), tile)] = fold(sums)

        def outer_tile(t, carry):
            for q in range(2):
                at = pl.multiple_of(t * tile + q * size, size)
                place(p, 2 * t + q, at)
            return carry

        lax.fori_loop(*plan.outer_range(p), outer_tile, 0)
        return carry

    lax.fori_loop(0, plan.pairs, one_pair, 0)


def make_band(plan, inverse, ham_t, vectors):
    depth, rows = ham_t.shape
    size, tile = plan.size, plan.tile
    return pl.pallas_call(
        functools.partial(band_kernel, plan, depth),
        out_shape=[
            pltpu.VMEM((plan.pairs, plan.places * size, 2 * tile), jnp.bfloat16),
            pltpu.VMEM((plan.width, rows), F32),
        ],
        in_specs=[SMEM, pl.BlockSpec(memory_space=pltpu.HBM), VMEM],
        out_specs=[VMEM, VMEM],
        scratch_shapes=[
            pltpu.VMEM((plan.pairs, depth + size, tile), F32),
            pltpu.VMEM((2 * plan.width, rows), jnp.bfloat16),
            pltpu.SemaphoreType.DMA((plan.pairs,)),
        ],
        compiler_params=params(16),
        cost_estimate=cost(8 * plan.width * rows * rows, 2 * 4 * depth * rows),
        name="band",
    )(inverse, pltpu.with_memory_space_constraint(ham_t, pltpu.HBM), vectors)


def inner_kernel(plan, *refs):
    vectors, band, inner, halves = refs[:PARTS], *refs[PARTS:]
    tile, width, part = plan.tile, plan.width, plan.part
    for p in range(plan.pairs):
        at = p * tile
        for h, ref in enumerate(vectors):
            high, low = split(ref[:, at : at + tile])
            halves[h * part : (h + 1) * part, at : at + tile] = high
            halves[width + h * part : width + (h + 1) * part, at : at + tile] = low
    base = plan.outer * tile
    for p in range(plan.pairs):
        begin, end = (tile * bound for bound in plan.own_range(p))
        sums = jnp.dot(
            halves[:, begin:end],
            band[p, base + begin : base + end, :],
            preferred_element_type=F32,
        )
        inner[:, p * tile : (p + 1) * tile] = fold(sums)


def run_inner(plan, vectors, band):
    return pl.pallas_call(
        functools.partial(inner_kernel, plan),
        out_shape=pltpu.VMEM((plan.width, plan.rows), F32),
        in_specs=[VMEM] * (PARTS + 1),
        out_specs=VMEM,
        scratch_shapes=[pltpu.VMEM((2 * plan.width, plan.rows), jnp.bfloat16)],
        compiler_params=params(8),
        cost_estimate=cost(8 * plan.width * plan.rows**2, 0),
        name="inner",
    )(*vectors, band)


def outer_products(plan, h, lower, far, upper, band, halves):
    tile, part = plan.tile, plan.part
    at = 0
    for ref in (lower, far, upper):
        rows = slice(h * part, (h + 1) * part) if ref.shape[0] > part else slice(None)
        for begin in range(0, ref.shape[1], tile):
            high, low = split(ref[rows, begin : begin + tile])
            halves[:part, at : at + tile] = high
            halves[part:, at : at + tile] = low
            at += tile
    for p in range(plan.pairs):
        begin, end = (tile * bound for bound in plan.outer_range(p))
        sums = jnp.dot(
            halves[:, begin:end], band[p, begin:end, :], preferred_element_type=F32
        )
        yield p * tile, fold(sums)


def first_kernel(
    plan, h, asked, lower, far, upper, band, inner, own, value, to_upper, to_lower, to_far, halves
):
    tile, edge, part = plan.tile, plan.edge, plan.part
    rows = slice(h * part, (h + 1) * part)
    for at, product in outer_products(plan, h, lower, far, upper, band, halves):
        lanes = slice(at, at + tile)
        shifted = product + inner[rows, lanes] - CENTER * own[rows, lanes]
        term = shifted * (1.0 / HALF_WIDTH)
        value[:, lanes] = term
        if at < edge:
            to_lower[:, lanes] = term
        skip = plan.rows - edge
        if at >= skip:
            to_upper[:, at - skip : at - skip + tile] = term

    def write(at, term):
        to_far[:, at : at + tile] = term

    write_far(plan, asked, value, write)


def run_first(plan, h, asked, arrived, band, inner, own):
    edge = jax.ShapeDtypeStruct((plan.part, plan.edge), F32)
    far = jax.ShapeDtypeStruct((plan.part, plan.far * plan.tile), F32)
    return pl.pallas_call(
        functools.partial(first_kernel, plan, h),
        out_shape=[pltpu.VMEM((plan.part, plan.rows), F32), edge, edge, far],
        in_specs=[SMEM] + [VMEM] * 6,
        out_specs=[VMEM] * 4,
        scratch_shapes=[pltpu.VMEM((2 * plan.part, plan.outer * plan.tile), jnp.bfloat16)],
        compiler_params=params(8),
        cost_estimate=cost(8 * plan.part * plan.rows**2, 0),
        name="first",
    )(asked, *arrived, band, inner, own)


def second_kernel(plan, h, lower, far, upper, band, inner, own, start, *rest):
    earlier, out, halves = rest[:-2], *rest[-2:]
    tile, part = plan.tile, plan.part
    rows = slice(h * part, (h + 1) * part)
    for at, product in outer_products(plan, h, lower, far, upper, band, halves):
        lanes = slice(at, at + tile)
        shifted = product + inner[rows, lanes] - CENTER * own[:, lanes]
        term = 2.0 / HALF_WIDTH * shifted - start[rows, lanes]
        if h < PARTS - 1:
            out[:, lanes] = term
        else:
            whole = [ref[:, lanes] for ref in earlier] + [term]
            out[lanes, :] = jnp.concatenate(whole, axis=0).T


def run_second(plan, h, arrived, band, inner, own, start, earlier):
    if h < PARTS - 1:
        out, earlier = pltpu.VMEM((plan.part, plan.rows), F32), []
    else:
        out = jax.ShapeDtypeStruct((plan.rows, plan.width), F32)
    return pl.pallas_call(
        functools.partial(second_kernel, plan, h),
        out_shape=out,
        in_specs=[VMEM] * (7 + len(earlier)),
        out_specs=VMEM,
        scratch_shapes=[pltpu.VMEM((2 * plan.part, plan.outer * plan.tile), jnp.bfloat16)],
        compiler_params=params(8),
        cost_estimate=cost(8 * plan.part * plan.rows**2, 0),
        name="second",
    )(*arrived, band, inner, own, start, *earlier)


def after(value, *others):
    return lax.optimization_barrier((value, *others))[0]


def per_device(hamiltonian, subspace, block_cols, far_list):
    block_rows, entries = block_cols.shape
    size = hamiltonian.shape[1] // entries
    device_count = lax.axis_size("rows")
    first_row = lax.axis_index("rows") * block_rows
    block_total = block_rows * device_count
    swap_level = (device_count // 8).bit_length() - 1
    plan = Plan(size, block_rows * size, subspace.shape[1], far_list.shape[1])

    asked_list = partner(far_list, "rows", swap_level)
    start, *sends = pack(plan, subspace)
    asked = jnp.clip(asked_list[0] - first_row, 0, block_rows - 1)

    listed = gather_far(plan, asked, start)
    far = partner(listed, "rows", swap_level)
    arrived = []
    for h in range(PARTS):
        above, below = sends[2 * h : 2 * h + 2]
        if h > 0:
            above, below = lax.optimization_barrier((above, below, listed))[:2]
        lower, upper = halo(above, below, "rows")
        arrived.append((lower, far, upper))

    near, far_slots = 2 * plan.near, 2 * plan.far
    shift = (block_cols - first_row + near + block_total) % block_total
    places = jnp.where(
        block_cols >= block_total,
        near + block_cols - block_total,
        jnp.where(
            shift < near,
            shift,
            jnp.where(
                shift < near + block_rows,
                shift - near + 2 * plan.outer,
                shift - block_rows + far_slots,
            ),
        ),
    )
    every = jnp.arange(plan.places, dtype=jnp.int32)[None, None, :]
    entry = jnp.arange(entries, dtype=jnp.int32)[None, :, None]
    hit = places[:, :, None] == every
    inverse = entries + jnp.sum(jnp.where(hit, entry - entries, 0), axis=1)

    band, inner = make_band(plan, after(inverse, listed), hamiltonian.T, start)

    values, later = [], []
    for h in range(PARTS):
        if values:
            inner = after(inner, values[-1])
        value, above, below, listed = run_first(
            plan, h, asked, arrived[h], band, inner, start
        )
        values.append(value)
        far = partner(listed, "rows", swap_level)
        lower, upper = halo(above, below, "rows")
        later.append((lower, far, upper))
    inner = run_inner(plan, values, band)
    result = []
    for h in range(PARTS):
        if result:
            inner = after(inner, result[-1])
        out = run_second(plan, h, later[h], band, inner, values[h], start, result)
        result.append(out)
    return result[-1]


def solution(mesh):
    placed = (P("rows", None), P("rows", None), P("rows", None), P("rows", None))
    return jax.shard_map(
        per_device, mesh=mesh, in_specs=placed, out_specs=P("rows", None), check_vma=False
    )
```

time: 106 us -> 48.8 us (0.46)
  matrix products: 36.4 us -> 0 us
  local copies, waits for them, and re-layouts: 33.4 us -> 1.22 us
  Pallas kernels: 0 us -> 21.5 us
  waiting for transfers between devices: 18.5 us -> 0.08 us
  starting transfers between devices: 11.2 us -> 24.7 us
  other arithmetic: 5.61 us -> 0.92 us
    dot_general x2 -> x0, matrix products: 36.4 us -> none  [apply_operator(): jnp.einsum('irm,imk->irk', ham_slab, picked, precision=lax.Precision.HIGH...]
    pallas_call x0 -> x8, Pallas kernels: none -> 21.5 us  [the longest x1 10.2 us: make_band(): pl.pallas_call(functools.partial(band_kernel, plan, depth), out_shape=[pl...]
    gather x4 -> x0, local copies, waits for them, and re-layouts: 19 us -> none  [the longest x2 16.7 us: gather_blocks(): picked = blocks[positions]]
    ppermute x3 -> x4, waiting for transfers between devices: 18.5 us -> 0.01 us  [partner(): return lax.ppermute(value, axis, pairs)]
    unnamed x13 -> x2, local copies, waits for them, and re-layouts: 14.2 us -> 1.13 us
    ppermute x4 -> x8, starting transfers between devices: 11.1 us -> 21.5 us  [halo(): return (lax.ppermute(above, axis, up), lax.ppermute(below, axis, down))]
    concatenate x2 -> x0, other arithmetic: 3.4 us -> none  [apply_operator(): extended = jnp.concatenate([band_panel, remote], axis=0)]
    ppermute x3 -> x4, starting transfers between devices: 0.14 us -> 3.18 us  [partner(): return lax.ppermute(value, axis, pairs)]
  transfers between devices with their start and end apart: 7 -> 12, of which waited for: 2 -> 0; matrix products, arithmetic and copies ran while one was open for 15% -> 2% of each run, Pallas kernels for 0% -> 40%
where the time goes in v2:
time: 48.8 us; the launch traced here: 48.6 us
  starting transfers between devices  24.7 us (51%)
  Pallas kernels  21.5 us (44%)
  local copies, waits for them, and re-layouts  1.22 us (2%)
  other arithmetic  0.92 us (2%)
    ppermute x8, starting transfers between devices, halo(): return (lax.ppermute(above, axis, up), lax.ppermute(below, axis, down))  21.5 us
    pallas_call x1, Pallas kernels, make_band(): pl.pallas_call(functools.partial(band_kernel, plan, depth), out_shape=[pl...  10.2 us
    pallas_call x2, Pallas kernels, run_first(): pl.pallas_call(functools.partial(first_kernel, plan, h), out_shape=[pltpu...  3.76 us
    pallas_call x2, Pallas kernels, run_second(): pl.pallas_call(functools.partial(second_kernel, plan, h), out_shape=out,...  3.44 us
    ppermute x4, starting transfers between devices, partner(): return lax.ppermute(value, axis, pairs)  3.18 us
    pallas_call x1, Pallas kernels, run_inner(): pl.pallas_call(functools.partial(inner_kernel, plan), out_shape=pltpu.VME...  2.36 us
    unnamed x2, local copies, waits for them, and re-layouts  1.13 us
    pallas_call x1, Pallas kernels, pack(): pl.pallas_call(functools.partial(pack_kernel, plan), out_shape=[pltpu.VME...  1.03 us
  transfers between devices with their start and end apart: 12, of which 0 were waited for; matrix products, arithmetic and copies ran while one was open for 2% of the time, Pallas kernels for 40%

profile of v2, /device:TPU:0, one launch (start us, length us, event | category | flops | bytes accessed | tf_op | source)
XLA Modules:
  0.0 48.6 jit_solution(4647633659082781410)
XLA Ops:
  0.0 3.0 %collective-permute-start = (s32[1,8]{1,0:T(1,128)}, s32[1,8]{1,0:T(1,128)S(1)}, u32[]{:S(2)}, u32[]{:S(2)}) collective-permute-start(s32[1,8]{1,0:T(1,128)} %param.7), channel_id=1, source_target_pairs={{0,4},{1,5},{2,6},{3,7},{4,0},{5,1},{6,2},{7,3},{8,12},{9,13},{10,... | collective-permute-start | bytes 104 | tf_op jit(solution)/shard_map/ppermute | solution.py:22
  3.0 0.0 copy-start
  3.0 1.1 %copy-done = f32[1536,128]{1,0:T(8,128)S(1)} copy-done((f32[1536,128]{1,0:T(8,128)S(1)}, f32[1536,128]{1,0:T(8,128)}, u32[]{:S(2)}) %copy-start) | copy-done | bytes 786456
  4.1 1.0 %pack.1 = (f32[128,1536]{1,0:T(8,128)S(1)}, f32[64,896]{1,0:T(8,128)}, f32[64,896]{1,0:T(8,128)}, f32[64,896]{1,0:T(8,128)}, f32[64,896]{1,0:T(8,128)S(1)}) custom-call(f32[1536,128]{1,0:T(8,128)S(1)} %copy-done), custom_call_target="tpu_custom_call" | custom-call | tf_op jit(solution)/shard_map/pack/pallas_call | solution.py:100
  5.1 0.0 collective-permute-start.4
  5.1 5.3 %collective-permute-start.5 = (f32[64,896]{1,0:T(8,128)}, f32[64,896]{1,0:T(8,128)S(1)}, u32[]{:S(2)}, u32[]{:S(2)}) collective-permute-start(f32[64,896]{1,0:T(8,128)} %get-tuple-element.34), channel_id=1, source_target_pairs={{1,0},{2,1},{3,2},{4,3},{5,4},{6,5},{7,6},{8,7},{9,8},{10,9},{11,1... | collective-permute-start | bytes 688136 | tf_op jit(solution)/shard_map/ppermute | solution.py:29
  10.5 0.7 %fusion = s32[24,27]{1,0:T(8,128)S(1)} fusion(s32[24,27]{1,0:T(8,128)} %param.6, s32[]{:T(128)S(6)} %mul.3), kind=kLoop, calls=%fused_computation.4 | loop fusion | flops 11016 | bytes 5188 | tf_op jit(solution)/shard_map/jit(_where)/select_n | solution.py:350
  11.2 0.1 copy.5
  11.3 0.2 select_reduce_fusion
  11.5 0.0 collective-permute-done
  11.5 0.8 %far.1 = f32[128,512]{1,0:T(8,128)S(1)} custom-call(s32[8]{0:T(128)S(1)} %clamp_bitcast_fusion.asked, f32[128,1536]{1,0:T(8,128)S(1)} %get-tuple-element.27.turned.vectors.own.start), custom_call_target="tpu_custom_call" | custom-call | tf_op jit(solution)/shard_map/far/pallas_call | solution.py:118
  12.3 0.1 collective-permute-start.2
  12.4 0.1 collective-permute-start.1
  12.4 5.3 %collective-permute-start.3 = (f32[64,896]{1,0:T(8,128)S(1)}, f32[64,896]{1,0:T(8,128)S(1)}, u32[]{:S(2)}, u32[]{:S(2)}) collective-permute-start(f32[64,896]{1,0:T(8,128)S(1)} %get-tuple-element.29), channel_id=1, source_target_pairs={{1,0},{2,1},{3,2},{4,3},{5,4},{6,5},{7,6},{8,7},{9,8},{10,9},{11,1... | collective-permute-start | bytes 688136 | tf_op jit(solution)/shard_map/ppermute | solution.py:29
  17.8 10.2 %band.1 = (bf16[12,3840,256]{2,1,0:T(8,128)(2,1)S(1)}, f32[128,1536]{1,0:T(8,128)S(1)}) custom-call(s32[24,60]{1,0:T(8,128)S(1)} %broadcast_add_fusion.inverse, f32[1728,1536]{1,0:T(8,128)} %bitcast.3, f32[128,1536]{1,0:T(8,128)S(1)} %get-tuple-element.27.turned.vectors.own.start), custom_call_target="tpu_custom_call" | custom-call | flops 2415919104 | bytes 21233664 | tf_op jit(solution)/shard_map/band/pallas_call | solution.py:182
  27.9 0.0 collective-permute-done.4.lower
  27.9 0.0 collective-permute-done.5.upper
  27.9 0.0 collective-permute-done.2.far
  28.0 1.9 %first.2 = (f32[64,1536]{1,0:T(8,128)S(1)}, f32[64,896]{1,0:T(8,128)S(1)}, f32[64,896]{1,0:T(8,128)S(1)}, f32[64,512]{1,0:T(8,128)S(1)}) custom-call(s32[8]{0:T(128)S(1)} %clamp_bitcast_fusion.asked, f32[64,896]{1,0:T(8,128)S(1)} %collective-permute-done.4.lower, f32[128,512]{1,0:T(8,128)S(1)} %collective-permute-done.2.far, ...), custom_call_target="tpu_custom_call" | custom-call | flops 1207959552 | tf_op jit(solution)/shard_map/first/pallas_call | solution.py:277
  29.8 0.1 collective-permute-start.10
  29.9 0.1 collective-permute-start.9
  30.0 5.3 %collective-permute-start.11 = (f32[64,896]{1,0:T(8,128)S(1)}, f32[64,896]{1,0:T(8,128)S(1)}, u32[]{:S(2)}, u32[]{:S(2)}) collective-permute-start(f32[64,896]{1,0:T(8,128)S(1)} %get-tuple-element.43), channel_id=1, source_target_pairs={{1,0},{2,1},{3,2},{4,3},{5,4},{6,5},{7,6},{8,7},{9,8},{10,9},{11,1... | collective-permute-start | bytes 688136 | tf_op jit(solution)/shard_map/ppermute | solution.py:29
  35.3 0.0 collective-permute-done.1.lower
  35.3 0.0 collective-permute-done.3.upper
  35.3 1.9 %first.3 = (f32[64,1536]{1,0:T(8,128)S(1)}, f32[64,896]{1,0:T(8,128)S(1)}, f32[64,896]{1,0:T(8,128)S(1)}, f32[64,512]{1,0:T(8,128)S(1)}) custom-call(s32[8]{0:T(128)S(1)} %clamp_bitcast_fusion.asked, f32[64,896]{1,0:T(8,128)S(1)} %collective-permute-done.1.lower, f32[128,512]{1,0:T(8,128)S(1)} %collective-permute-done.2.far, ...), custom_call_target="tpu_custom_call" | custom-call | flops 1207959552 | tf_op jit(solution)/shard_map/first/pallas_call | solution.py:277
  37.2 0.1 collective-permute-start.7
  37.3 0.1 collective-permute-start.6
  37.4 0.0 collective-permute-done.10.far
  37.4 5.3 %collective-permute-start.8 = (f32[64,896]{1,0:T(8,128)S(1)}, f32[64,896]{1,0:T(8,128)S(1)}, u32[]{:S(2)}, u32[]{:S(2)}) collective-permute-start(f32[64,896]{1,0:T(8,128)S(1)} %get-tuple-element.39), channel_id=1, source_target_pairs={{1,0},{2,1},{3,2},{4,3},{5,4},{6,5},{7,6},{8,7},{9,8},{10,9},{11,1... | collective-permute-start | bytes 688136 | tf_op jit(solution)/shard_map/ppermute | solution.py:29
  42.7 2.4 %inner.1 = f32[128,1536]{1,0:T(8,128)S(1)} custom-call(f32[64,1536]{1,0:T(8,128)S(1)} %get-tuple-element.35.refs_0_.own, f32[64,1536]{1,0:T(8,128)S(1)} %get-tuple-element.40.refs_1_.own, bf16[12,3840,256]{2,1,0:T(8,128)(2,1)S(1)} %get-tuple-element.31.band.refs_2_), custom_call_target="tpu_custom_call" | custom-call | flops 2415919104 | tf_op jit(solution)/shard_map/inner/pallas_call | solution.py:222
  45.1 0.0 collective-permute-done.9.lower
  45.1 0.0 collective-permute-done.11.upper
  45.1 1.2 %second.2.rest_0_ = f32[64,1536]{1,0:T(8,128)S(1)} custom-call(f32[64,896]{1,0:T(8,128)S(1)} %collective-permute-done.9.lower, f32[64,512]{1,0:T(8,128)S(1)} %collective-permute-done.10.far, f32[64,896]{1,0:T(8,128)S(1)} %collective-permute-done.11.upper, bf16[12,3840,256]{2,1,0:T(8,128)(2,1)S(1)} %get-tuple-element.31.band.refs_2_, f32[128,1536]{1,0:T(8,128)S(1)} %inner.1, ...), custom_call_target="tpu_custom_call" | custom-call | flops 1207959552 | tf_op jit(solution)/shard_map/second/pallas_call | solution.py:309
  46.3 0.0 collective-permute-done.7.far
  46.3 0.1 collective-permute-done.6.lower
  46.4 0.0 collective-permute-done.8.upper
  46.4 2.2 %second.3 = f32[1536,128]{1,0:T(8,128)} custom-call(f32[64,896]{1,0:T(8,128)S(1)} %collective-permute-done.6.lower, f32[64,512]{1,0:T(8,128)S(1)} %collective-permute-done.7.far, f32[64,896]{1,0:T(8,128)S(1)} %collective-permute-done.8.upper, bf16[12,3840,256]{2,1,0:T(8,128)(2,1)S(1)} %get-tuple-element.31.band.refs_2_, f32[128,1536]{1,0:T(8,128)S(1)} %inner.1, ...), custom_call_target="tpu_custom_call" | custom-call | flops 1207959552 | tf_op jit(solution)/shard_map/second/pallas_call | solution.py:309
  (3 shorter events, 0.0 us)
Async XLA Ops:
  0.0 11.5 %collective-permute-start = (s32[1,8]{1,0:T(1,128)}, s32[1,8]{1,0:T(1,128)S(1)}, u32[]{:S(2)}, u32[]{:S(2)}) collective-permute-start(s32[1,8]{1,0:T(1,128)} %param.7), channel_id=1, source_target_pairs={{0,4},{1,5},{2,6},{3,7},{4,0},{5,1},{6,2},{7,3},{8,12},{9,13},{10,... | collective-permute-start | bytes 104 | tf_op jit(solution)/shard_map/ppermute | solution.py:22
  3.0 1.1 %copy-start = (f32[1536,128]{1,0:T(8,128)S(1)}, f32[1536,128]{1,0:T(8,128)}, u32[]{:S(2)}) copy-start(f32[1536,128]{1,0:T(8,128)} %natural.1) | copy-start | bytes 2359300
  5.1 22.8 %collective-permute-start.4 = (f32[64,896]{1,0:T(8,128)}, f32[64,896]{1,0:T(8,128)S(1)}, u32[]{:S(2)}, u32[]{:S(2)}) collective-permute-start(f32[64,896]{1,0:T(8,128)} %get-tuple-element.33), channel_id=1, source_target_pairs={{0,1},{1,2},{2,3},{3,4},{4,5},{5,6},{6,7},{7,8},{8,9},{9,10},{10,1... | collective-permute-start | bytes 688136 | tf_op jit(solution)/shard_map/ppermute | solution.py:29
  5.1 22.8 %collective-permute-start.5 = (f32[64,896]{1,0:T(8,128)}, f32[64,896]{1,0:T(8,128)S(1)}, u32[]{:S(2)}, u32[]{:S(2)}) collective-permute-start(f32[64,896]{1,0:T(8,128)} %get-tuple-element.34), channel_id=1, source_target_pairs={{1,0},{2,1},{3,2},{4,3},{5,4},{6,5},{7,6},{8,7},{9,8},{10,9},{11,1... | collective-permute-start | bytes 688136 | tf_op jit(solution)/shard_map/ppermute | solution.py:29
  12.3 15.7 %collective-permute-start.2 = (f32[128,512]{1,0:T(8,128)S(1)}, f32[128,512]{1,0:T(8,128)S(1)}, u32[]{:S(2)}, u32[]{:S(2)}) collective-permute-start(f32[128,512]{1,0:T(8,128)S(1)} %far.1), channel_id=1, source_target_pairs={{0,4},{1,5},{2,6},{3,7},{4,0},{5,1},{6,2},{7,3},{8,12},{9,13},{10,... | collective-permute-start | bytes 786440 | tf_op jit(solution)/shard_map/ppermute | solution.py:22
  12.4 23.0 %collective-permute-start.1 = (f32[64,896]{1,0:T(8,128)}, f32[64,896]{1,0:T(8,128)S(1)}, u32[]{:S(2)}, u32[]{:S(2)}) collective-permute-start(f32[64,896]{1,0:T(8,128)} %get-tuple-element.28), channel_id=1, source_target_pairs={{0,1},{1,2},{2,3},{3,4},{4,5},{5,6},{6,7},{7,8},{8,9},{9,10},{10,1... | collective-permute-start | bytes 688136 | tf_op jit(solution)/shard_map/ppermute | solution.py:29
  12.4 22.9 %collective-permute-start.3 = (f32[64,896]{1,0:T(8,128)S(1)}, f32[64,896]{1,0:T(8,128)S(1)}, u32[]{:S(2)}, u32[]{:S(2)}) collective-permute-start(f32[64,896]{1,0:T(8,128)S(1)} %get-tuple-element.29), channel_id=1, source_target_pairs={{1,0},{2,1},{3,2},{4,3},{5,4},{6,5},{7,6},{8,7},{9,8},{10,9},{11,1... | collective-permute-start | bytes 688136 | tf_op jit(solution)/shard_map/ppermute | solution.py:29
  29.8 7.5 %collective-permute-start.10 = (f32[64,512]{1,0:T(8,128)S(1)}, f32[64,512]{1,0:T(8,128)S(1)}, u32[]{:S(2)}, u32[]{:S(2)}) collective-permute-start(f32[64,512]{1,0:T(8,128)S(1)} %get-tuple-element.42), channel_id=1, source_target_pairs={{0,4},{1,5},{2,6},{3,7},{4,0},{5,1},{6,2},{7,3},{8,12},{9,13},{10,... | collective-permute-start | bytes 393224 | tf_op jit(solution)/shard_map/ppermute | solution.py:22
  29.9 15.1 %collective-permute-start.9 = (f32[64,896]{1,0:T(8,128)S(1)}, f32[64,896]{1,0:T(8,128)S(1)}, u32[]{:S(2)}, u32[]{:S(2)}) collective-permute-start(f32[64,896]{1,0:T(8,128)S(1)} %get-tuple-element.41), channel_id=1, source_target_pairs={{0,1},{1,2},{2,3},{3,4},{4,5},{5,6},{6,7},{7,8},{8,9},{9,10},{10,1... | collective-permute-start | bytes 688136 | tf_op jit(solution)/shard_map/ppermute | solution.py:29
  30.0 15.1 %collective-permute-start.11 = (f32[64,896]{1,0:T(8,128)S(1)}, f32[64,896]{1,0:T(8,128)S(1)}, u32[]{:S(2)}, u32[]{:S(2)}) collective-permute-start(f32[64,896]{1,0:T(8,128)S(1)} %get-tuple-element.43), channel_id=1, source_target_pairs={{1,0},{2,1},{3,2},{4,3},{5,4},{6,5},{7,6},{8,7},{9,8},{10,9},{11,1... | collective-permute-start | bytes 688136 | tf_op jit(solution)/shard_map/ppermute | solution.py:29
  37.2 9.1 %collective-permute-start.7 = (f32[64,512]{1,0:T(8,128)S(1)}, f32[64,512]{1,0:T(8,128)S(1)}, u32[]{:S(2)}, u32[]{:S(2)}) collective-permute-start(f32[64,512]{1,0:T(8,128)S(1)} %get-tuple-element.38), channel_id=1, source_target_pairs={{0,4},{1,5},{2,6},{3,7},{4,0},{5,1},{6,2},{7,3},{8,12},{9,13},{10,... | collective-permute-start | bytes 393224 | tf_op jit(solution)/shard_map/ppermute | solution.py:22
  37.3 9.1 %collective-permute-start.6 = (f32[64,896]{1,0:T(8,128)S(1)}, f32[64,896]{1,0:T(8,128)S(1)}, u32[]{:S(2)}, u32[]{:S(2)}) collective-permute-start(f32[64,896]{1,0:T(8,128)S(1)} %get-tuple-element.37), channel_id=1, source_target_pairs={{0,1},{1,2},{2,3},{3,4},{4,5},{5,6},{6,7},{7,8},{8,9},{9,10},{10,1... | collective-permute-start | bytes 688136 | tf_op jit(solution)/shard_map/ppermute | solution.py:29
  37.4 9.0 %collective-permute-start.8 = (f32[64,896]{1,0:T(8,128)S(1)}, f32[64,896]{1,0:T(8,128)S(1)}, u32[]{:S(2)}, u32[]{:S(2)}) collective-permute-start(f32[64,896]{1,0:T(8,128)S(1)} %get-tuple-element.39), channel_id=1, source_target_pairs={{1,0},{2,1},{3,2},{4,3},{5,4},{6,5},{7,6},{8,7},{9,8},{10,9},{11,1... | collective-permute-start | bytes 688136 | tf_op jit(solution)/shard_map/ppermute | solution.py:29

commit v3 on v2

v3 whole, which is shorter than its diff:
```python
import functools

import jax
import jax.numpy as jnp
from jax import lax
from jax.experimental import pallas as pl
from jax.experimental.pallas import tpu as pltpu
from jax.sharding import PartitionSpec as P

CENTER = 0.25
HALF_WIDTH = 1.5
REACH = 13
PARTS = 1
F32 = jnp.float32
VMEM = pl.BlockSpec(memory_space=pltpu.VMEM)
SMEM = pl.BlockSpec(memory_space=pltpu.SMEM)


def partner(value, axis, bit):
    mask = 2**bit
    pairs = [(source, source ^ mask) for source in range(lax.axis_size(axis))]
    return lax.ppermute(value, axis, pairs)


def swap_chips(value, axis):
    devices = lax.axis_size(axis)
    pairs = [(i, (i + (1 if i % 2 else -1)) % devices) for i in range(devices)]
    return lax.ppermute(value, axis, pairs)


def split(value):
    high = value.astype(jnp.bfloat16)
    return high, (value - high.astype(F32)).astype(jnp.bfloat16)


def fold(sums):
    width, tile = sums.shape[0] // 2, sums.shape[1] // 2
    small = sums[width:, tile:] + sums[width:, :tile] + sums[:width, tile:]
    return small + sums[:width, :tile]


def params(limit):
    return pltpu.CompilerParams(vmem_limit_bytes=limit * 2**20)


def cost(flops, moved):
    return pl.CostEstimate(flops=flops, bytes_accessed=moved, transcendentals=0)


class Plan:
    def __init__(self, size, rows, width, slots):
        self.size, self.rows, self.width = size, rows, width
        self.tile = 2 * size
        self.pairs = rows // self.tile
        self.near = (REACH + 1) // 2
        self.far = slots * size // self.tile
        self.edge = self.near * self.tile
        self.part = width // PARTS
        self.outer = 2 * self.near + self.far
        self.places = 2 * (self.outer + self.pairs)

    def outer_range(self, p):
        extra = p + self.near - self.pairs + 1
        if isinstance(p, int):
            return min(p, self.near), self.near + self.far + max(0, extra)
        return jnp.minimum(p, self.near), self.near + self.far + jnp.maximum(0, extra)

    def own_range(self, p):
        begin, end = p - self.near, p + self.near + 1
        if isinstance(p, int):
            return max(0, begin), min(self.pairs, end)
        return jnp.maximum(0, begin), jnp.minimum(self.pairs, end)


def write_far(plan, asked, source, write):
    tile, size = plan.tile, plan.size
    lane = lax.broadcasted_iota(jnp.int32, (source.shape[0], tile), 1)

    def block(slot, want):
        index = lax.rem(asked[0, slot] + 2 * plan.pairs, 2 * plan.pairs)
        at = pl.multiple_of((index // 2) * tile, tile)
        value = source[:, pl.ds(at, tile)]
        return jnp.where(index % 2 == want, value, pltpu.roll(value, size, 1))

    for t in range(plan.far):
        value = jnp.where(lane < size, block(2 * t, 0), block(2 * t + 1, 1))
        write(t * tile, value)


def write_sends(plan, side, source, rows, away, near):
    skip = plan.rows - plan.edge
    odd = side[0]
    for ref, at in ((away, odd * skip), (near, (1 - odd) * skip)):
        ref[...] = source[rows, pl.ds(pl.multiple_of(at, plan.tile), plan.edge)]


def pack_kernel(plan, chunks, side, natural, turned, *rest):
    sends, staged, sems = rest[:-2], *rest[-2:]
    tile, part, step = plan.tile, plan.part, plan.rows // chunks

    def fetch(c):
        return pltpu.make_async_copy(
            natural.at[pl.ds(c * step, step), :],
            staged.at[pl.ds(c * step, step), :],
            sems.at[c],
        )

    for c in range(chunks):
        fetch(c).start()
    for c in range(chunks):
        fetch(c).wait()
        for at in range(c * step, (c + 1) * step, tile):
            turned[:, at : at + tile] = staged[at : at + tile, :].T
    for h in range(PARTS):
        rows = slice(h * part, (h + 1) * part)
        write_sends(plan, side, turned, rows, *sends[2 * h : 2 * h + 2])


def pack(plan, side, natural):
    edge = jax.ShapeDtypeStruct((plan.part, plan.edge), F32)
    chunks = 4 if plan.pairs % 4 == 0 else 1
    return pl.pallas_call(
        functools.partial(pack_kernel, plan, chunks),
        out_shape=[pltpu.VMEM((plan.width, plan.rows), F32)] + [edge] * (2 * PARTS),
        in_specs=[SMEM, pl.BlockSpec(memory_space=pltpu.HBM)],
        out_specs=[VMEM] * (1 + 2 * PARTS),
        scratch_shapes=[
            pltpu.VMEM((plan.rows, plan.width), F32),
            pltpu.SemaphoreType.DMA((chunks,)),
        ],
        compiler_params=params(8),
        name="pack",
    )(side, pltpu.with_memory_space_constraint(natural, pltpu.HBM))


def far_kernel(plan, asked, turned, out):
    def write(at, value):
        out[:, at : at + plan.tile] = value

    write_far(plan, asked, turned, write)


def gather_far(plan, asked, turned):
    return pl.pallas_call(
        functools.partial(far_kernel, plan),
        out_shape=jax.ShapeDtypeStruct((plan.width, plan.far * plan.tile), F32),
        in_specs=[SMEM, VMEM],
        out_specs=VMEM,
        compiler_params=params(8),
        name="far",
    )(asked, turned)


def band_kernel(plan, depth, inverse, ham_t, band, staged, sems):
    size, tile = plan.size, plan.tile
    lane = lax.broadcasted_iota(jnp.int32, (size, tile), 1)

    def fetch(p):
        return pltpu.make_async_copy(
            ham_t.at[:, pl.ds(pl.multiple_of(p * tile, tile), tile)],
            staged.at[p, pl.ds(0, depth), :],
            sems.at[p],
        )

    for p in range(plan.pairs):
        fetch(p).start()
    for p in range(plan.pairs):
        staged[p, depth:, :] = jnp.zeros((size, tile), F32)

    def one_pair(p, carry):
        fetch(p).wait()

        def block(q):
            even = pl.multiple_of(inverse[2 * p, q] * size, size)
            odd = pl.multiple_of(inverse[2 * p + 1, q] * size, size)
            first = staged[p, pl.ds(even, size), :]
            second = staged[p, pl.ds(odd, size), :]
            return jnp.where(lane < size, first, second)

        def group(g, carry):
            halves = [split(block(4 * g + q)) for q in range(4)]
            for q, (high, low) in enumerate(halves):
                at = pl.multiple_of((4 * g + q) * size, size)
                band[p, pl.ds(at, size), :tile] = high
                band[p, pl.ds(at, size), tile:] = low
            return carry

        begin, end = plan.outer_range(p)
        lax.fori_loop(begin // 2, (end + 1) // 2, group, 0)
        begin, end = (plan.outer + bound for bound in plan.own_range(p))
        lax.fori_loop(begin // 2, (end + 1) // 2, group, 0)
        return carry

    lax.fori_loop(0, plan.pairs, one_pair, 0)


def make_band(plan, inverse, ham_t):
    depth, rows = ham_t.shape
    size, tile = plan.size, plan.tile
    return pl.pallas_call(
        functools.partial(band_kernel, plan, depth),
        out_shape=pltpu.VMEM((plan.pairs, plan.places * size, 2 * tile), jnp.bfloat16),
        in_specs=[SMEM, pl.BlockSpec(memory_space=pltpu.HBM)],
        out_specs=VMEM,
        scratch_shapes=[
            pltpu.VMEM((plan.pairs, depth + size, tile), F32),
            pltpu.SemaphoreType.DMA((plan.pairs,)),
        ],
        compiler_params=params(16),
        cost_estimate=cost(0, 2 * 4 * depth * rows),
        name="band",
    )(inverse, pltpu.with_memory_space_constraint(ham_t, pltpu.HBM))


def inner_kernel(plan, *refs):
    vectors, band, inner, halves = refs[:PARTS], *refs[PARTS:]
    tile, width, part = plan.tile, plan.width, plan.part
    for p in range(plan.pairs):
        at = p * tile
        for h, ref in enumerate(vectors):
            high, low = split(ref[:, at : at + tile])
            halves[h * part : (h + 1) * part, at : at + tile] = high
            halves[width + h * part : width + (h + 1) * part, at : at + tile] = low
    base = plan.outer * tile
    for p in range(plan.pairs):
        begin, end = (tile * bound for bound in plan.own_range(p))
        sums = jnp.dot(
            halves[:, begin:end],
            band[p, base + begin : base + end, :],
            preferred_element_type=F32,
        )
        inner[:, p * tile : (p + 1) * tile] = fold(sums)


def run_inner(plan, vectors, band):
    return pl.pallas_call(
        functools.partial(inner_kernel, plan),
        out_shape=pltpu.VMEM((plan.width, plan.rows), F32),
        in_specs=[VMEM] * (PARTS + 1),
        out_specs=VMEM,
        scratch_shapes=[pltpu.VMEM((2 * plan.width, plan.rows), jnp.bfloat16)],
        compiler_params=params(8),
        cost_estimate=cost(8 * plan.width * plan.rows**2, 0),
        name="inner",
    )(*vectors, band)


def outer_products(plan, h, side, away, far, near, band, halves):
    tile, part = plan.tile, plan.part
    upper = (plan.near + plan.far) * tile
    odd = side[0]
    for ref, base in ((away, odd * upper), (near, (1 - odd) * upper), (far, plan.edge)):
        rows = slice(h * part, (h + 1) * part) if ref.shape[0] > part else slice(None)
        for begin in range(0, ref.shape[1], tile):
            at = pl.ds(pl.multiple_of(base + begin, tile), tile)
            high, low = split(ref[rows, begin : begin + tile])
            halves[:part, at] = high
            halves[part:, at] = low
    for p in range(plan.pairs):
        begin, end = (tile * bound for bound in plan.outer_range(p))
        sums = jnp.dot(
            halves[:, begin:end], band[p, begin:end, :], preferred_element_type=F32
        )
        yield p * tile, fold(sums)


def first_kernel(
    plan, h, side, asked, away, far, near, band, inner, own, value, to_away, to_near, to_far, halves
):
    tile, part = plan.tile, plan.part
    rows = slice(h * part, (h + 1) * part)
    for at, product in outer_products(plan, h, side, away, far, near, band, halves):
        lanes = slice(at, at + tile)
        shifted = product + inner[rows, lanes] - CENTER * own[rows, lanes]
        value[:, lanes] = shifted * (1.0 / HALF_WIDTH)
    write_sends(plan, side, value, slice(None), to_away, to_near)

    def write(at, term):
        to_far[:, at : at + tile] = term

    write_far(plan, asked, value, write)


def run_first(plan, h, side, asked, arrived, band, inner, own):
    edge = jax.ShapeDtypeStruct((plan.part, plan.edge), F32)
    far = jax.ShapeDtypeStruct((plan.part, plan.far * plan.tile), F32)
    return pl.pallas_call(
        functools.partial(first_kernel, plan, h),
        out_shape=[pltpu.VMEM((plan.part, plan.rows), F32), edge, edge, far],
        in_specs=[SMEM] * 2 + [VMEM] * 6,
        out_specs=[VMEM] * 4,
        scratch_shapes=[pltpu.VMEM((2 * plan.part, plan.outer * plan.tile), jnp.bfloat16)],
        compiler_params=params(8),
        cost_estimate=cost(8 * plan.part * plan.rows**2, 0),
        name="first",
    )(side, asked, *arrived, band, inner, own)


def second_kernel(plan, h, side, away, far, near, band, inner, own, start, *rest):
    earlier, out, halves = rest[:-2], *rest[-2:]
    tile, part = plan.tile, plan.part
    rows = slice(h * part, (h + 1) * part)
    for at, product in outer_products(plan, h, side, away, far, near, band, halves):
        lanes = slice(at, at + tile)
        shifted = product + inner[rows, lanes] - CENTER * own[:, lanes]
        term = 2.0 / HALF_WIDTH * shifted - start[rows, lanes]
        if h < PARTS - 1:
            out[:, lanes] = term
        else:
            whole = [ref[:, lanes] for ref in earlier] + [term]
            out[lanes, :] = jnp.concatenate(whole, axis=0).T


def run_second(plan, h, side, arrived, band, inner, own, start, earlier):
    if h < PARTS - 1:
        out, earlier = pltpu.VMEM((plan.part, plan.rows), F32), []
    else:
        out = jax.ShapeDtypeStruct((plan.rows, plan.width), F32)
    return pl.pallas_call(
        functools.partial(second_kernel, plan, h),
        out_shape=out,
        in_specs=[SMEM] + [VMEM] * (7 + len(earlier)),
        out_specs=VMEM,
        scratch_shapes=[pltpu.VMEM((2 * plan.part, plan.outer * plan.tile), jnp.bfloat16)],
        compiler_params=params(8),
        cost_estimate=cost(8 * plan.part * plan.rows**2, 0),
        name="second",
    )(side, *arrived, band, inner, own, start, *earlier)


def after(value, *others):
    return lax.optimization_barrier((value, *others))[0]


def per_device(hamiltonian, subspace, block_cols, far_list):
    block_rows, entries = block_cols.shape
    size = hamiltonian.shape[1] // entries
    device_count = lax.axis_size("rows")
    first_row = lax.axis_index("rows") * block_rows
    block_total = block_rows * device_count
    swap_level = (device_count // 8).bit_length() - 1
    plan = Plan(size, block_rows * size, subspace.shape[1], far_list.shape[1])

    side = (lax.axis_index("rows") % 2).astype(jnp.int32).reshape(1)

    def exchange(to_away, to_near):
        return swap_chips(to_away, "rows"), partner(to_near, "rows", 0)

    asked = partner(far_list, "rows", swap_level)
    start, *sends = pack(plan, side, subspace)
    listed = gather_far(plan, asked, start)
    far = partner(listed, "rows", swap_level)
    arrived = []
    for h in range(PARTS):
        to_away, to_near = sends[2 * h : 2 * h + 2]
        if h > 0:
            to_away, to_near = lax.optimization_barrier((to_away, to_near, listed))[:2]
        away, near = exchange(to_away, to_near)
        arrived.append((away, far, near))

    block_cols = after(block_cols, listed)
    near, far_slots = 2 * plan.near, 2 * plan.far
    shift = (block_cols - first_row + near + block_total) % block_total
    places = jnp.where(
        block_cols >= block_total,
        near + block_cols - block_total,
        jnp.where(
            shift < near,
            shift,
            jnp.where(
                shift < near + block_rows,
                shift - near + 2 * plan.outer,
                shift - block_rows + far_slots,
            ),
        ),
    )
    every = jnp.arange(plan.places, dtype=jnp.int32)[None, None, :]
    entry = jnp.arange(entries, dtype=jnp.int32)[None, :, None]
    hit = places[:, :, None] == every
    inverse = entries + jnp.sum(jnp.where(hit, entry - entries, 0), axis=1)

    band = make_band(plan, inverse, hamiltonian.T)
    inner = run_inner(plan, [start[h * plan.part : (h + 1) * plan.part] for h in range(PARTS)], band)

    values, later = [], []
    for h in range(PARTS):
        if values:
            inner = after(inner, values[-1])
        value, to_away, to_near, listed = run_first(
            plan, h, side, asked, arrived[h], band, inner, start
        )
        values.append(value)
        far = partner(listed, "rows", swap_level)
        away, near = exchange(to_away, to_near)
        later.append((away, far, near))
    inner = run_inner(plan, values, band)
    result = []
    for h in range(PARTS):
        if result:
            inner = after(inner, result[-1])
        out = run_second(plan, h, side, later[h], band, inner, values[h], start, result)
        result.append(out)
    return result[-1]


def solution(mesh):
    placed = (P("rows", None), P("rows", None), P("rows", None), P("rows", None))
    return jax.shard_map(
        per_device, mesh=mesh, in_specs=placed, out_specs=P("rows", None), check_vma=False
    )
```

time: 48.8 us -> 43.1 us (0.88)
  starting transfers between devices: 24.7 us -> 7.82 us
  waiting for transfers between devices: 0.08 us -> 12.5 us
  local copies, waits for them, and re-layouts: 1.22 us -> 0.08 us
    ppermute x8 -> x2, starting transfers between devices: 21.5 us -> 4.73 us  [swap_chips(): return lax.ppermute(value, axis, pairs)]
    ppermute x4 -> x5, waiting for transfers between devices: 0.01 us -> 12.5 us  [partner(): return lax.ppermute(value, axis, pairs)]
    pallas_call x1 -> x2, Pallas kernels: 2.36 us -> 4.73 us  [run_inner(): pl.pallas_call(functools.partial(inner_kernel, plan), out_shape=pltpu.VME...]
    pallas_call x2, Pallas kernels: 11.2 us -> 9.57 us  [the longest x1 8.01 us: make_band(): pl.pallas_call(functools.partial(band_kernel, plan, depth), out_shape=plt...]
    unnamed x2 -> x0, local copies, waits for them, and re-layouts: 1.13 us -> none
    pallas_call x2 -> x1, Pallas kernels: 3.76 us -> 3.09 us  [run_first(): pl.pallas_call(functools.partial(first_kernel, plan, h), out_shape=[pltpu...]
    pallas_call x2 -> x1, Pallas kernels: 3.44 us -> 3.3 us  [run_second(): pl.pallas_call(functools.partial(second_kernel, plan, h), out_shape=out,...]
    ppermute x4 -> x5, starting transfers between devices: 3.18 us -> 3.09 us  [partner(): return lax.ppermute(value, axis, pairs)]
  transfers between devices with their start and end apart: 12 -> 7, of which waited for: 0 -> 2; matrix products, arithmetic and copies ran while one was open for 2% -> 2% of each run, Pallas kernels for 40% -> 35%
where the time goes in v3:
time: 43.1 us; the launch traced here: 42.9 us
  Pallas kernels  21.4 us (50%)
  waiting for transfers between devices  12.5 us (29%)
  starting transfers between devices  7.82 us (18%)
  other arithmetic  0.92 us (2%)
    ppermute x5, waiting for transfers between devices, partner(): return lax.ppermute(value, axis, pairs)  12.5 us
    pallas_call x1, Pallas kernels, make_band(): pl.pallas_call(functools.partial(band_kernel, plan, depth), out_shape=plt...  8.01 us
    pallas_call x2, Pallas kernels, run_inner(): pl.pallas_call(functools.partial(inner_kernel, plan), out_shape=pltpu.VME...  4.73 us
    ppermute x2, starting transfers between devices, swap_chips(): return lax.ppermute(value, axis, pairs)  4.73 us
    pallas_call x1, Pallas kernels, run_second(): pl.pallas_call(functools.partial(second_kernel, plan, h), out_shape=out,...  3.3 us
    ppermute x5, starting transfers between devices, partner(): return lax.ppermute(value, axis, pairs)  3.09 us
    pallas_call x1, Pallas kernels, run_first(): pl.pallas_call(functools.partial(first_kernel, plan, h), out_shape=[pltpu...  3.09 us
    pallas_call x1, Pallas kernels, pack(): pl.pallas_call(functools.partial(pack_kernel, plan, chunks), out_shape=[p...  1.56 us
  transfers between devices with their start and end apart: 7, of which 2 were waited for; matrix products, arithmetic and copies ran while one was open for 2% of the time, Pallas kernels for 35%

profile of v3, /device:TPU:0, one launch (start us, length us, event | category | flops | bytes accessed | tf_op | source)
XLA Modules:
  0.0 42.9 jit_solution(2158155508233557530)
XLA Ops:
  0.0 3.0 %collective-permute-start = (s32[1,8]{1,0:T(1,128)}, s32[1,8]{1,0:T(1,128)S(1)}, u32[]{:S(2)}, u32[]{:S(2)}) collective-permute-start(s32[1,8]{1,0:T(1,128)} %param.7), channel_id=1, source_target_pairs={{0,4},{1,5},{2,6},{3,7},{4,0},{5,1},{6,2},{7,3},{8,12},{9,13},{10,... | collective-permute-start | bytes 104 | tf_op jit(solution)/shard_map/ppermute | solution.py:22
  3.0 1.6 %pack.1 = (f32[128,1536]{1,0:T(8,128)S(1)}, f32[128,896]{1,0:T(8,128)S(1)}, f32[128,896]{1,0:T(8,128)S(1)}) custom-call(s32[1]{0:T(128)} %bitcast.side, f32[1536,128]{1,0:T(8,128)} %natural.1), custom_call_target="tpu_custom_call" | custom-call | tf_op jit(solution)/shard_map/pack/pallas_call | solution.py:122
  4.5 3.7 %collective-permute-start.1 = (f32[128,896]{1,0:T(8,128)S(1)}, f32[128,896]{1,0:T(8,128)S(1)}, u32[]{:S(2)}, u32[]{:S(2)}) collective-permute-start(f32[128,896]{1,0:T(8,128)S(1)} %get-tuple-element.13), channel_id=1, source_target_pairs={{0,31},{1,2},{2,1},{3,4},{4,3},{5,6},{6,5},{7,8},{8,7},{9,10},{10,... | collective-permute-start | bytes 1376264 | tf_op jit(solution)/shard_map/ppermute | solution.py:28
  8.2 0.0 collective-permute-start.3
  8.2 0.0 collective-permute-done.asked
  8.2 0.8 %far.1 = f32[128,512]{1,0:T(8,128)S(1)} custom-call(s32[1,8]{1,0:T(1,128)S(1)} %collective-permute-done.asked, f32[128,1536]{1,0:T(8,128)S(1)} %get-tuple-element.14.turned.refs_0_.own.start), custom_call_target="tpu_custom_call" | custom-call | tf_op jit(solution)/shard_map/far/pallas_call | solution.py:144
  9.0 0.1 collective-permute-start.2
  9.1 0.7 %fusion = s32[24,27]{1,0:T(8,128)S(1)} fusion(s32[24,27]{1,0:T(8,128)} %param.6, s32[]{:T(128)S(6)} %mul.3), kind=kLoop, calls=%fused_computation.4 | loop fusion | flops 11016 | bytes 5188 | tf_op jit(solution)/shard_map/jit(_where)/select_n | solution.py:364
  9.8 0.1 copy.5
  9.9 0.2 select_reduce_fusion
  10.1 8.0 %band.1.refs_1_ = bf16[12,3840,256]{2,1,0:T(8,128)(2,1)S(1)} custom-call(s32[24,60]{1,0:T(8,128)S(1)} %broadcast_add_fusion.inverse, f32[1728,1536]{1,0:T(8,128)} %bitcast.2), custom_call_target="tpu_custom_call" | custom-call | bytes 21233664 | tf_op jit(solution)/shard_map/band/pallas_call | solution.py:200
  18.1 2.4 %inner.2 = f32[128,1536]{1,0:T(8,128)S(1)} custom-call(f32[128,1536]{1,0:T(8,128)S(1)} %get-tuple-element.14.turned.refs_0_.own.start, bf16[12,3840,256]{2,1,0:T(8,128)(2,1)S(1)} %band.1.refs_1_), custom_call_target="tpu_custom_call" | custom-call | flops 2415919104 | tf_op jit(solution)/shard_map/inner/pallas_call | solution.py:236
  20.5 1.3 %collective-permute-done.2.far = f32[128,512]{1,0:T(8,128)S(1)} collective-permute-done((f32[128,512]{1,0:T(8,128)S(1)}, f32[128,512]{1,0:T(8,128)S(1)}, u32[]{:S(2)}, u32[]{:S(2)}) %collective-permute-start.2) | collective-permute-done | bytes 262176 | tf_op jit(solution)/shard_map/ppermute | solution.py:22
  21.8 0.0 collective-permute-done.1.away
  21.8 0.0 collective-permute-done.3.near
  21.8 3.1 %first.1 = (f32[128,1536]{1,0:T(8,128)S(1)}, f32[128,896]{1,0:T(8,128)S(1)}, f32[128,896]{1,0:T(8,128)S(1)}, f32[128,512]{1,0:T(8,128)S(1)}) custom-call(s32[1]{0:T(128)} %bitcast.side, s32[1,8]{1,0:T(1,128)S(1)} %collective-permute-done.asked, f32[128,896]{1,0:T(8,128)S(1)} %collective-permute-done.1.away, f32[128,512]{1,0:T(8,128)S(1)} %collective-permute-done.2.far, ...), custom_call_target="tpu_custom_call" | custom-call | flops 2415919104 | tf_op jit(solution)/shard_map/first/pallas_call | solution.py:287
  24.9 1.0 %collective-permute-start.4 = (f32[128,896]{1,0:T(8,128)S(1)}, f32[128,896]{1,0:T(8,128)S(1)}, u32[]{:S(2)}, u32[]{:S(2)}) collective-permute-start(f32[128,896]{1,0:T(8,128)S(1)} %get-tuple-element.17), channel_id=1, source_target_pairs={{0,31},{1,2},{2,1},{3,4},{4,3},{5,6},{6,5},{7,8},{8,7},{9,10},{10,... | collective-permute-start | bytes 1376264 | tf_op jit(solution)/shard_map/ppermute | solution.py:28
  26.0 0.0 collective-permute-start.6
  26.0 0.1 collective-permute-start.5
  26.0 2.4 %inner.3 = f32[128,1536]{1,0:T(8,128)S(1)} custom-call(f32[128,1536]{1,0:T(8,128)S(1)} %get-tuple-element.20.refs_0_.own, bf16[12,3840,256]{2,1,0:T(8,128)(2,1)S(1)} %band.1.refs_1_), custom_call_target="tpu_custom_call" | custom-call | flops 2415919104 | tf_op jit(solution)/shard_map/inner/pallas_call | solution.py:236
  28.4 11.2 %collective-permute-done.5.far = f32[128,512]{1,0:T(8,128)S(1)} collective-permute-done((f32[128,512]{1,0:T(8,128)S(1)}, f32[128,512]{1,0:T(8,128)S(1)}, u32[]{:S(2)}, u32[]{:S(2)}) %collective-permute-start.5) | collective-permute-done | bytes 262176 | tf_op jit(solution)/shard_map/ppermute | solution.py:22
  39.6 0.0 collective-permute-done.4.away
  39.6 0.0 collective-permute-done.6.near
  39.6 3.3 %second.1 = f32[1536,128]{1,0:T(8,128)} custom-call(s32[1]{0:T(128)} %bitcast.side, f32[128,896]{1,0:T(8,128)S(1)} %collective-permute-done.4.away, f32[128,512]{1,0:T(8,128)S(1)} %collective-permute-done.5.far, f32[128,896]{1,0:T(8,128)S(1)} %collective-permute-done.6.near, bf16[12,3840,256]{2,1,0:T(8,128)(2,1)S(1)} %band.1.refs_1_, f32[128,1536]{1,0:T(8,128)S(1)} %inner.3, ...), custom_call_target="tpu_custom_call" | custom-call | flops 2415919104 | tf_op jit(solution)/shard_map/second/pallas_call | solution.py:319
  (2 shorter events, 0.0 us)
Async XLA Ops:
  0.0 8.2 %collective-permute-start = (s32[1,8]{1,0:T(1,128)}, s32[1,8]{1,0:T(1,128)S(1)}, u32[]{:S(2)}, u32[]{:S(2)}) collective-permute-start(s32[1,8]{1,0:T(1,128)} %param.7), channel_id=1, source_target_pairs={{0,4},{1,5},{2,6},{3,7},{4,0},{5,1},{6,2},{7,3},{8,12},{9,13},{10,... | collective-permute-start | bytes 104 | tf_op jit(solution)/shard_map/ppermute | solution.py:22
  4.5 17.3 %collective-permute-start.1 = (f32[128,896]{1,0:T(8,128)S(1)}, f32[128,896]{1,0:T(8,128)S(1)}, u32[]{:S(2)}, u32[]{:S(2)}) collective-permute-start(f32[128,896]{1,0:T(8,128)S(1)} %get-tuple-element.13), channel_id=1, source_target_pairs={{0,31},{1,2},{2,1},{3,4},{4,3},{5,6},{6,5},{7,8},{8,7},{9,10},{10,... | collective-permute-start | bytes 1376264 | tf_op jit(solution)/shard_map/ppermute | solution.py:28
  8.2 13.6 %collective-permute-start.3 = (f32[128,896]{1,0:T(8,128)S(1)}, f32[128,896]{1,0:T(8,128)S(1)}, u32[]{:S(2)}, u32[]{:S(2)}) collective-permute-start(f32[128,896]{1,0:T(8,128)S(1)} %get-tuple-element.15), channel_id=1, source_target_pairs={{0,1},{1,0},{2,3},{3,2},{4,5},{5,4},{6,7},{7,6},{8,9},{9,8},{10,11... | collective-permute-start | bytes 1376264 | tf_op jit(solution)/shard_map/ppermute | solution.py:22
  9.0 12.8 %collective-permute-start.2 = (f32[128,512]{1,0:T(8,128)S(1)}, f32[128,512]{1,0:T(8,128)S(1)}, u32[]{:S(2)}, u32[]{:S(2)}) collective-permute-start(f32[128,512]{1,0:T(8,128)S(1)} %far.1), channel_id=1, source_target_pairs={{0,4},{1,5},{2,6},{3,7},{4,0},{5,1},{6,2},{7,3},{8,12},{9,13},{10,... | collective-permute-start | bytes 786440 | tf_op jit(solution)/shard_map/ppermute | solution.py:22
  24.9 14.7 %collective-permute-start.4 = (f32[128,896]{1,0:T(8,128)S(1)}, f32[128,896]{1,0:T(8,128)S(1)}, u32[]{:S(2)}, u32[]{:S(2)}) collective-permute-start(f32[128,896]{1,0:T(8,128)S(1)} %get-tuple-element.17), channel_id=1, source_target_pairs={{0,31},{1,2},{2,1},{3,4},{4,3},{5,6},{6,5},{7,8},{8,7},{9,10},{10,... | collective-permute-start | bytes 1376264 | tf_op jit(solution)/shard_map/ppermute | solution.py:28
  26.0 13.6 %collective-permute-start.6 = (f32[128,896]{1,0:T(8,128)S(1)}, f32[128,896]{1,0:T(8,128)S(1)}, u32[]{:S(2)}, u32[]{:S(2)}) collective-permute-start(f32[128,896]{1,0:T(8,128)S(1)} %get-tuple-element.19), channel_id=1, source_target_pairs={{0,1},{1,0},{2,3},{3,2},{4,5},{5,4},{6,7},{7,6},{8,9},{9,8},{10,11... | collective-permute-start | bytes 1376264 | tf_op jit(solution)/shard_map/ppermute | solution.py:22
  26.0 13.6 %collective-permute-start.5 = (f32[128,512]{1,0:T(8,128)S(1)}, f32[128,512]{1,0:T(8,128)S(1)}, u32[]{:S(2)}, u32[]{:S(2)}) collective-permute-start(f32[128,512]{1,0:T(8,128)S(1)} %get-tuple-element.18), channel_id=1, source_target_pairs={{0,4},{1,5},{2,6},{3,7},{4,0},{5,1},{6,2},{7,3},{8,12},{9,13},{10,... | collective-permute-start | bytes 786440 | tf_op jit(solution)/shard_map/ppermute | solution.py:22

commit v4 on v3

--- a/solution.py
+++ b/solution.py
@@ -58,45 +58,53 @@
         self.part = width // PARTS
         self.outer = 2 * self.near + self.far
         self.places = 2 * (self.outer + self.pairs)
+        self.depth = max(sum(run[2] for run in self.runs(p)) for p in range(self.pairs))
 
     def outer_range(self, p):
         extra = p + self.near - self.pairs + 1
-        if isinstance(p, int):
-            return min(p, self.near), self.near + self.far + max(0, extra)
-        return jnp.minimum(p, self.near), self.near + self.far + jnp.maximum(0, extra)
+        return min(p, self.near), self.near + self.far + max(0, extra)
 
     def own_range(self, p):
-        begin, end = p - self.near, p + self.near + 1
-        if isinstance(p, int):
-            return max(0, begin), min(self.pairs, end)
-        return jnp.maximum(0, begin), jnp.minimum(self.pairs, end)
-
-
-def write_far(plan, asked, source, write):
+        return max(0, p - self.near), min(self.pairs, p + self.near + 1)
+
+    def runs(self, p):
+        begin, end = self.outer_range(p)
+        rows = (end - begin) * self.tile
+        outer = (2 * begin, 0, rows)
+        begin, end = self.own_range(p)
+        return outer, (2 * (self.outer + begin), rows, (end - begin) * self.tile)
+
+    def mirrored(self, t, side):
+        return t + side[0] * (self.pairs - 1 - 2 * t)
+
+
+def write_far(plan, side, asked, source, write):
     tile, size = plan.tile, plan.size
     lane = lax.broadcasted_iota(jnp.int32, (source.shape[0], tile), 1)
 
     def block(slot, want):
         index = lax.rem(asked[0, slot] + 2 * plan.pairs, 2 * plan.pairs)
-        at = pl.multiple_of((index // 2) * tile, tile)
-        value = source[:, pl.ds(at, tile)]
-        return jnp.where(index % 2 == want, value, pltpu.roll(value, size, 1))
+        at = plan.mirrored(lax.div(index, 2), side) * tile
+        value = source[:, pl.ds(pl.multiple_of(at, tile), tile)]
+        return jnp.where(lax.rem(index, 2) == want, value, pltpu.roll(value, size, 1))
 
     for t in range(plan.far):
         value = jnp.where(lane < size, block(2 * t, 0), block(2 * t + 1, 1))
         write(t * tile, value)
 
 
-def write_sends(plan, side, source, rows, away, near):
+def write_sends(plan, at, value, to_away, to_near):
     skip = plan.rows - plan.edge
-    odd = side[0]
-    for ref, at in ((away, odd * skip), (near, (1 - odd) * skip)):
-        ref[...] = source[rows, pl.ds(pl.multiple_of(at, plan.tile), plan.edge)]
+    if at < plan.edge:
+        to_away[:, at : at + plan.tile] = value
+    if at >= skip:
+        to_near[:, at - skip : at - skip + plan.tile] = value
 
 
 def pack_kernel(plan, chunks, side, natural, turned, *rest):
     sends, staged, sems = rest[:-2], *rest[-2:]
-    tile, part, step = plan.tile, plan.part, plan.rows // chunks
+    tile, part, count = plan.tile, plan.part, plan.pairs // chunks
+    step = count * tile
 
     def fetch(c):
         return pltpu.make_async_copy(
@@ -109,11 +117,14 @@
         fetch(c).start()
     for c in range(chunks):
         fetch(c).wait()
-        for at in range(c * step, (c + 1) * step, tile):
-            turned[:, at : at + tile] = staged[at : at + tile, :].T
-    for h in range(PARTS):
-        rows = slice(h * part, (h + 1) * part)
-        write_sends(plan, side, turned, rows, *sends[2 * h : 2 * h + 2])
+    for t in range(plan.pairs):
+        at = pl.multiple_of(plan.mirrored(t, side) * tile, tile)
+        value = staged[pl.ds(at, tile), :].T
+        at = t * tile
+        turned[:, at : at + tile] = value
+        for h in range(PARTS):
+            rows = slice(h * part, (h + 1) * part)
+            write_sends(plan, at, value[rows], *sends[2 * h : 2 * h + 2])
 
 
 def pack(plan, side, natural):
@@ -133,103 +144,108 @@
     )(side, pltpu.with_memory_space_constraint(natural, pltpu.HBM))
 
 
-def far_kernel(plan, asked, turned, out):
+def far_kernel(plan, side, asked, turned, out):
     def write(at, value):
         out[:, at : at + plan.tile] = value
 
-    write_far(plan, asked, turned, write)
-
-
-def gather_far(plan, asked, turned):
+    write_far(plan, side, asked, turned, write)
+
+
+def gather_far(plan, side, asked, turned):
     return pl.pallas_call(
         functools.partial(far_kernel, plan),
         out_shape=jax.ShapeDtypeStruct((plan.width, plan.far * plan.tile), F32),
-        in_specs=[SMEM, VMEM],
+        in_specs=[SMEM, SMEM, VMEM],
         out_specs=VMEM,
         compiler_params=params(8),
         name="far",
-    )(asked, turned)
-
-
-def band_kernel(plan, depth, inverse, ham_t, band, staged, sems):
+    )(side, asked, turned)
+
+
+def own_halves(plan, vectors, halves):
+    tile, width, part = plan.tile, plan.width, plan.part
+    for at in range(0, plan.rows, tile):
+        for h, ref in enumerate(vectors):
+            high, low = split(ref[:, at : at + tile])
+            rows = slice(h * ref.shape[0], (h + 1) * ref.shape[0])
+            halves[rows, at : at + tile] = high
+            halves[width + rows.start : width + rows.stop, at : at + tile] = low
+
+
+def own_product(plan, p, halves, band, inner):
+    begin, end = (plan.tile * bound for bound in plan.own_range(p))
+    _, (_, row, rows) = plan.runs(p)
+    sums = jnp.dot(
+        halves[:, begin:end], band[p, row : row + rows, :], preferred_element_type=F32
+    )
+    inner[:, p * plan.tile : (p + 1) * plan.tile] = fold(sums)
+
+
+def band_kernel(plan, depth, side, inverse, ham_t, vectors, band, inner, staged, halves, sems):
     size, tile = plan.size, plan.tile
     lane = lax.broadcasted_iota(jnp.int32, (size, tile), 1)
 
     def fetch(p):
+        at = pl.multiple_of(plan.mirrored(p, side) * tile, tile)
         return pltpu.make_async_copy(
-            ham_t.at[:, pl.ds(pl.multiple_of(p * tile, tile), tile)],
-            staged.at[p, pl.ds(0, depth), :],
-            sems.at[p],
+            ham_t.at[:, pl.ds(at, tile)], staged.at[p, pl.ds(0, depth), :], sems.at[p]
         )
 
     for p in range(plan.pairs):
         fetch(p).start()
     for p in range(plan.pairs):
         staged[p, depth:, :] = jnp.zeros((size, tile), F32)
-
-    def one_pair(p, carry):
+    own_halves(plan, [vectors], halves)
+
+    for p in range(plan.pairs):
         fetch(p).wait()
+        row = 2 * plan.mirrored(p, side)
 
         def block(q):
-            even = pl.multiple_of(inverse[2 * p, q] * size, size)
-            odd = pl.multiple_of(inverse[2 * p + 1, q] * size, size)
+            even = pl.multiple_of(inverse[row, q] * size, size)
+            odd = pl.multiple_of(inverse[row + 1, q] * size, size)
             first = staged[p, pl.ds(even, size), :]
             second = staged[p, pl.ds(odd, size), :]
             return jnp.where(lane < size, first, second)
 
-        def group(g, carry):
-            halves = [split(block(4 * g + q)) for q in range(4)]
-            for q, (high, low) in enumerate(halves):
-                at = pl.multiple_of((4 * g + q) * size, size)
-                band[p, pl.ds(at, size), :tile] = high
-                band[p, pl.ds(at, size), tile:] = low
-            return carry
-
-        begin, end = plan.outer_range(p)
-        lax.fori_loop(begin // 2, (end + 1) // 2, group, 0)
-        begin, end = (plan.outer + bound for bound in plan.own_range(p))
-        lax.fori_loop(begin // 2, (end + 1) // 2, group, 0)
-        return carry
-
-    lax.fori_loop(0, plan.pairs, one_pair, 0)
-
-
-def make_band(plan, inverse, ham_t):
+        if p > 0:
+            own_product(plan, p - 1, halves, band, inner)
+        for place, at, rows in plan.runs(p):
+            for q in range(rows // size):
+                high, low = split(block(place + q))
+                lines = slice(at + q * size, at + (q + 1) * size)
+                band[p, lines, :tile] = high
+                band[p, lines, tile:] = low
+    own_product(plan, plan.pairs - 1, halves, band, inner)
+
+
+def make_band(plan, side, inverse, ham_t, vectors):
     depth, rows = ham_t.shape
     size, tile = plan.size, plan.tile
     return pl.pallas_call(
         functools.partial(band_kernel, plan, depth),
-        out_shape=pltpu.VMEM((plan.pairs, plan.places * size, 2 * tile), jnp.bfloat16),
-        in_specs=[SMEM, pl.BlockSpec(memory_space=pltpu.HBM)],
-        out_specs=VMEM,
+        out_shape=[
+            pltpu.VMEM((plan.pairs, plan.depth, 2 * tile), jnp.bfloat16),
+            pltpu.VMEM((plan.width, rows), F32),
+        ],
+        in_specs=[SMEM, SMEM, pl.BlockSpec(memory_space=pltpu.HBM), VMEM],
+        out_specs=[VMEM, VMEM],
         scratch_shapes=[
             pltpu.VMEM((plan.pairs, depth + size, tile), F32),
+            pltpu.VMEM((2 * plan.width, rows), jnp.bfloat16),
             pltpu.SemaphoreType.DMA((plan.pairs,)),
         ],
-        compiler_params=params(16),
+        compiler_params=params(14),
         cost_estimate=cost(0, 2 * 4 * depth * rows),
         name="band",
-    )(inverse, pltpu.with_memory_space_constraint(ham_t, pltpu.HBM))
+    )(side, inverse, pltpu.with_memory_space_constraint(ham_t, pltpu.HBM), vectors)
 
 
 def inner_kernel(plan, *refs):
     vectors, band, inner, halves = refs[:PARTS], *refs[PARTS:]
-    tile, width, part = plan.tile, plan.width, plan.part
+    own_halves(plan, vectors, halves)
     for p in range(plan.pairs):
-        at = p * tile
-        for h, ref in enumerate(vectors):
-            high, low = split(ref[:, at : at + tile])
-            halves[h * part : (h + 1) * part, at : at + tile] = high
-            halves[width + h * part : width + (h + 1) * part, at : at + tile] = low
-    base = plan.outer * tile
-    for p in range(plan.pairs):
-        begin, end = (tile * bound for bound in plan.own_range(p))
-        sums = jnp.dot(
-            halves[:, begin:end],
-            band[p, base + begin : base + end, :],
-            preferred_element_type=F32,
-        )
-        inner[:, p * tile : (p + 1) * tile] = fold(sums)
+        own_product(plan, p, halves, band, inner)
 
 
 def run_inner(plan, vectors, band):
@@ -245,21 +261,20 @@
     )(*vectors, band)
 
 
-def outer_products(plan, h, side, away, far, near, band, halves):
+def outer_products(plan, h, away, far, near, band, halves):
     tile, part = plan.tile, plan.part
-    upper = (plan.near + plan.far) * tile
-    odd = side[0]
-    for ref, base in ((away, odd * upper), (near, (1 - odd) * upper), (far, plan.edge)):
+    tiles = [(away, plan.near - 1 - t) for t in range(plan.near)]
+    tiles += [(far, t) for t in range(plan.far)]
+    tiles += [(near, plan.near - 1 - t) for t in range(plan.near)]
+    for t, (ref, source) in enumerate(tiles):
         rows = slice(h * part, (h + 1) * part) if ref.shape[0] > part else slice(None)
-        for begin in range(0, ref.shape[1], tile):
-            at = pl.ds(pl.multiple_of(base + begin, tile), tile)
-            high, low = split(ref[rows, begin : begin + tile])
-            halves[:part, at] = high
-            halves[part:, at] = low
+        high, low = split(ref[rows, source * tile : (source + 1) * tile])
+        halves[:part, t * tile : (t + 1) * tile] = high
+        halves[part:, t * tile : (t + 1) * tile] = low
     for p in range(plan.pairs):
         begin, end = (tile * bound for bound in plan.outer_range(p))
         sums = jnp.dot(
-            halves[:, begin:end], band[p, begin:end, :], preferred_element_type=F32
+            halves[:, begin:end], band[p, : end - begin, :], preferred_element_type=F32
         )
         yield p * tile, fold(sums)
 
@@ -269,16 +284,17 @@
 ):
     tile, part = plan.tile, plan.part
     rows = slice(h * part, (h + 1) * part)
-    for at, product in outer_products(plan, h, side, away, far, near, band, halves):
+    for at, product in outer_products(plan, h, away, far, near, band, halves):
         lanes = slice(at, at + tile)
         shifted = product + inner[rows, lanes] - CENTER * own[rows, lanes]
-        value[:, lanes] = shifted * (1.0 / HALF_WIDTH)
-    write_sends(plan, side, value, slice(None), to_away, to_near)
+        term = shifted * (1.0 / HALF_WIDTH)
+        value[:, lanes] = term
+        write_sends(plan, at, term, to_away, to_near)
 
     def write(at, term):
         to_far[:, at : at + tile] = term
 
-    write_far(plan, asked, value, write)
+    write_far(plan, side, asked, value, write)
 
 
 def run_first(plan, h, side, asked, arrived, band, inner, own):
@@ -300,7 +316,7 @@
     earlier, out, halves = rest[:-2], *rest[-2:]
     tile, part = plan.tile, plan.part
     rows = slice(h * part, (h + 1) * part)
-    for at, product in outer_products(plan, h, side, away, far, near, band, halves):
+    for at, product in outer_products(plan, h, away, far, near, band, halves):
         lanes = slice(at, at + tile)
         shifted = product + inner[rows, lanes] - CENTER * own[:, lanes]
         term = 2.0 / HALF_WIDTH * shifted - start[rows, lanes]
@@ -308,7 +324,8 @@
             out[:, lanes] = term
         else:
             whole = [ref[:, lanes] for ref in earlier] + [term]
-            out[lanes, :] = jnp.concatenate(whole, axis=0).T
+            place = pl.multiple_of(plan.mirrored(at // tile, side) * tile, tile)
+            out[pl.ds(place, tile), :] = jnp.concatenate(whole, axis=0).T
 
 
 def run_second(plan, h, side, arrived, band, inner, own, start, earlier):
@@ -348,7 +365,7 @@
 
     asked = partner(far_list, "rows", swap_level)
     start, *sends = pack(plan, side, subspace)
-    listed = gather_far(plan, asked, start)
+    listed = gather_far(plan, side, asked, start)
     far = partner(listed, "rows", swap_level)
     arrived = []
     for h in range(PARTS):
@@ -361,6 +378,8 @@
     block_cols = after(block_cols, listed)
     near, far_slots = 2 * plan.near, 2 * plan.far
     shift = (block_cols - first_row + near + block_total) % block_total
+    last = block_rows + 2 * near - 2
+    shift = shift + side[0] * (last - 4 * (shift // 2))
     places = jnp.where(
         block_cols >= block_total,
         near + block_cols - block_total,
@@ -379,8 +398,7 @@
     hit = places[:, :, None] == every
     inverse = entries + jnp.sum(jnp.where(hit, entry - entries, 0), axis=1)
 
-    band = make_band(plan, inverse, hamiltonian.T)
-    inner = run_inner(plan, [start[h * plan.part : (h + 1) * plan.part] for h in range(PARTS)], band)
+    band, inner = make_band(plan, side, inverse, hamiltonian.T, start)
 
     values, later = [], []
     for h in range(PARTS):

time: 43.1 us -> 42.6 us (0.988)
  Pallas kernels: 21.4 us -> 19.6 us
  waiting for transfers between devices: 12.5 us -> 14 us
    pallas_call x2 -> x1, Pallas kernels: 4.73 us -> 2.37 us  [run_inner(): pl.pallas_call(functools.partial(inner_kernel, plan), out_shape=pltpu.VME...]
    ppermute x5, waiting for transfers between devices: 12.5 us -> 14 us  [partner(): return lax.ppermute(value, axis, pairs)]
    pallas_call x1, Pallas kernels: 8.01 us -> 8.95 us  [make_band(): pl.pallas_call(functools.partial(band_kernel, plan, depth), out_shape=[pl...]
  transfers between devices with their start and end apart: 7 -> 7, of which waited for: 2 -> 2; matrix products, arithmetic and copies ran while one was open for 2% -> 2% of each run, Pallas kernels for 35% -> 32%
where the time goes in v4:
time: 42.6 us; the launch traced here: 42.4 us
  Pallas kernels  19.6 us (46%)
  waiting for transfers between devices  14 us (33%)
  starting transfers between devices  7.72 us (18%)
  other arithmetic  0.93 us (2%)
    ppermute x5, waiting for transfers between devices, partner(): return lax.ppermute(value, axis, pairs)  14 us
    pallas_call x1, Pallas kernels, make_band(): pl.pallas_call(functools.partial(band_kernel, plan, depth), out_shape=[pl...  8.95 us
    ppermute x2, starting transfers between devices, swap_chips(): return lax.ppermute(value, axis, pairs)  4.67 us
    pallas_call x1, Pallas kernels, run_second(): pl.pallas_call(functools.partial(second_kernel, plan, h), out_shape=out,...  3.13 us
    ppermute x5, starting transfers between devices, partner(): return lax.ppermute(value, axis, pairs)  3.05 us
    pallas_call x1, Pallas kernels, run_first(): pl.pallas_call(functools.partial(first_kernel, plan, h), out_shape=[pltpu...  2.85 us
    pallas_call x1, Pallas kernels, run_inner(): pl.pallas_call(functools.partial(inner_kernel, plan), out_shape=pltpu.VME...  2.37 us
    pallas_call x1, Pallas kernels, pack(): pl.pallas_call(functools.partial(pack_kernel, plan, chunks), out_shape=[p...  1.52 us
  transfers between devices with their start and end apart: 7, of which 2 were waited for; matrix products, arithmetic and copies ran while one was open for 2% of the time, Pallas kernels for 32%

profile of v4, /device:TPU:0, one launch (start us, length us, event | category | flops | bytes accessed | tf_op | source)
XLA Modules:
  0.0 42.4 jit_solution(1006958920577359608)
XLA Ops:
  0.0 3.0 %collective-permute-start = (s32[1,8]{1,0:T(1,128)}, s32[1,8]{1,0:T(1,128)S(1)}, u32[]{:S(2)}, u32[]{:S(2)}) collective-permute-start(s32[1,8]{1,0:T(1,128)} %param.7), channel_id=1, source_target_pairs={{0,4},{1,5},{2,6},{3,7},{4,0},{5,1},{6,2},{7,3},{8,12},{9,13},{10,... | collective-permute-start | bytes 104 | tf_op jit(solution)/shard_map/ppermute | solution.py:22
  3.0 1.5 %pack.1 = (f32[128,1536]{1,0:T(8,128)S(1)}, f32[128,896]{1,0:T(8,128)S(1)}, f32[128,896]{1,0:T(8,128)S(1)}) custom-call(s32[1]{0:T(128)} %bitcast.side, f32[1536,128]{1,0:T(8,128)} %natural.1), custom_call_target="tpu_custom_call" | custom-call | tf_op jit(solution)/shard_map/pack/pallas_call | solution.py:133
  4.5 3.7 %collective-permute-start.1 = (f32[128,896]{1,0:T(8,128)S(1)}, f32[128,896]{1,0:T(8,128)S(1)}, u32[]{:S(2)}, u32[]{:S(2)}) collective-permute-start(f32[128,896]{1,0:T(8,128)S(1)} %get-tuple-element.15), channel_id=1, source_target_pairs={{0,31},{1,2},{2,1},{3,4},{4,3},{5,6},{6,5},{7,8},{8,7},{9,10},{10,... | collective-permute-start | bytes 1376264 | tf_op jit(solution)/shard_map/ppermute | solution.py:28
  8.2 0.0 collective-permute-start.3
  8.2 0.0 collective-permute-done.asked
  8.2 0.8 %far.1 = f32[128,512]{1,0:T(8,128)S(1)} custom-call(s32[1]{0:T(128)} %bitcast.side, s32[1,8]{1,0:T(1,128)S(1)} %collective-permute-done.asked, f32[128,1536]{1,0:T(8,128)S(1)} %get-tuple-element.16.turned.vectors.own.start), custom_call_target="tpu_custom_call" | custom-call | tf_op jit(solution)/shard_map/far/pallas_call | solution.py:155
  9.0 0.1 collective-permute-start.2
  9.1 0.7 %fusion.5 = s32[24,27]{1,0:T(8,128)S(1)} fusion(s32[24,27]{1,0:T(8,128)} %param.6, s32[]{:T(128)} %select_n.31, s32[]{:T(128)S(6)} %mul.15), kind=kLoop, calls=%fused_computation.13 | loop fusion | flops 23328 | bytes 5192 | tf_op jit(solution)/shard_map/jit(_where)/select_n | solution.py:383
  9.8 0.1 copy.5
  9.9 0.2 select_reduce_fusion
  10.1 8.9 %band.1 = (bf16[12,2432,256]{2,1,0:T(8,128)(2,1)S(1)}, f32[128,1536]{1,0:T(8,128)S(1)}) custom-call(s32[1]{0:T(128)} %bitcast.side, s32[24,60]{1,0:T(8,128)S(1)} %broadcast_add_fusion.inverse, f32[1728,1536]{1,0:T(8,128)} %bitcast.2, f32[128,1536]{1,0:T(8,128)S(1)} %get-tuple-element.16.turned.vectors.own.start), custom_call_target="tpu_custom_call" | custom-call | bytes 21233664 | tf_op jit(solution)/shard_map/band/pallas_call | solution.py:225
  19.0 2.7 %collective-permute-done.2.far = f32[128,512]{1,0:T(8,128)S(1)} collective-permute-done((f32[128,512]{1,0:T(8,128)S(1)}, f32[128,512]{1,0:T(8,128)S(1)}, u32[]{:S(2)}, u32[]{:S(2)}) %collective-permute-start.2) | collective-permute-done | bytes 262176 | tf_op jit(solution)/shard_map/ppermute | solution.py:22
  21.8 0.0 collective-permute-done.1.away
  21.8 0.0 collective-permute-done.3.near
  21.8 2.8 %first.1 = (f32[128,1536]{1,0:T(8,128)S(1)}, f32[128,896]{1,0:T(8,128)S(1)}, f32[128,896]{1,0:T(8,128)S(1)}, f32[128,512]{1,0:T(8,128)S(1)}) custom-call(s32[1]{0:T(128)} %bitcast.side, s32[1,8]{1,0:T(1,128)S(1)} %collective-permute-done.asked, f32[128,896]{1,0:T(8,128)S(1)} %collective-permute-done.1.away, f32[128,512]{1,0:T(8,128)S(1)} %collective-permute-done.2.far, ...), custom_call_target="tpu_custom_call" | custom-call | flops 2415919104 | tf_op jit(solution)/shard_map/first/pallas_call | solution.py:303
  24.6 1.0 %collective-permute-start.4 = (f32[128,896]{1,0:T(8,128)S(1)}, f32[128,896]{1,0:T(8,128)S(1)}, u32[]{:S(2)}, u32[]{:S(2)}) collective-permute-start(f32[128,896]{1,0:T(8,128)S(1)} %get-tuple-element.21), channel_id=1, source_target_pairs={{0,31},{1,2},{2,1},{3,4},{4,3},{5,6},{6,5},{7,8},{8,7},{9,10},{10,... | collective-permute-start | bytes 1376264 | tf_op jit(solution)/shard_map/ppermute | solution.py:28
  25.6 0.0 collective-permute-start.6
  25.6 0.0 collective-permute-start.5
  25.6 2.4 %inner.1 = f32[128,1536]{1,0:T(8,128)S(1)} custom-call(f32[128,1536]{1,0:T(8,128)S(1)} %get-tuple-element.24.refs_0_.own, bf16[12,2432,256]{2,1,0:T(8,128)(2,1)S(1)} %get-tuple-element.19.band.refs_1_), custom_call_target="tpu_custom_call" | custom-call | flops 2415919104 | tf_op jit(solution)/shard_map/inner/pallas_call | solution.py:252
  28.0 11.2 %collective-permute-done.5.far = f32[128,512]{1,0:T(8,128)S(1)} collective-permute-done((f32[128,512]{1,0:T(8,128)S(1)}, f32[128,512]{1,0:T(8,128)S(1)}, u32[]{:S(2)}, u32[]{:S(2)}) %collective-permute-start.5) | collective-permute-done | bytes 262176 | tf_op jit(solution)/shard_map/ppermute | solution.py:22
  39.3 0.0 collective-permute-done.4.away
  39.3 0.0 collective-permute-done.6.near
  39.3 3.1 %second.1 = f32[1536,128]{1,0:T(8,128)} custom-call(s32[1]{0:T(128)} %bitcast.side, f32[128,896]{1,0:T(8,128)S(1)} %collective-permute-done.4.away, f32[128,512]{1,0:T(8,128)S(1)} %collective-permute-done.5.far, f32[128,896]{1,0:T(8,128)S(1)} %collective-permute-done.6.near, bf16[12,2432,256]{2,1,0:T(8,128)(2,1)S(1)} %get-tuple-element.19.band.refs_1_, ...), custom_call_target="tpu_custom_call" | custom-call | flops 2415919104 | tf_op jit(solution)/shard_map/second/pallas_call | solution.py:336
  (2 shorter events, 0.0 us)
Async XLA Ops:
  0.0 8.2 %collective-permute-start = (s32[1,8]{1,0:T(1,128)}, s32[1,8]{1,0:T(1,128)S(1)}, u32[]{:S(2)}, u32[]{:S(2)}) collective-permute-start(s32[1,8]{1,0:T(1,128)} %param.7), channel_id=1, source_target_pairs={{0,4},{1,5},{2,6},{3,7},{4,0},{5,1},{6,2},{7,3},{8,12},{9,13},{10,... | collective-permute-start | bytes 104 | tf_op jit(solution)/shard_map/ppermute | solution.py:22
  4.5 17.3 %collective-permute-start.1 = (f32[128,896]{1,0:T(8,128)S(1)}, f32[128,896]{1,0:T(8,128)S(1)}, u32[]{:S(2)}, u32[]{:S(2)}) collective-permute-start(f32[128,896]{1,0:T(8,128)S(1)} %get-tuple-element.15), channel_id=1, source_target_pairs={{0,31},{1,2},{2,1},{3,4},{4,3},{5,6},{6,5},{7,8},{8,7},{9,10},{10,... | collective-permute-start | bytes 1376264 | tf_op jit(solution)/shard_map/ppermute | solution.py:28
  8.2 13.6 %collective-permute-start.3 = (f32[128,896]{1,0:T(8,128)S(1)}, f32[128,896]{1,0:T(8,128)S(1)}, u32[]{:S(2)}, u32[]{:S(2)}) collective-permute-start(f32[128,896]{1,0:T(8,128)S(1)} %get-tuple-element.17), channel_id=1, source_target_pairs={{0,1},{1,0},{2,3},{3,2},{4,5},{5,4},{6,7},{7,6},{8,9},{9,8},{10,11... | collective-permute-start | bytes 1376264 | tf_op jit(solution)/shard_map/ppermute | solution.py:22
  9.0 12.8 %collective-permute-start.2 = (f32[128,512]{1,0:T(8,128)S(1)}, f32[128,512]{1,0:T(8,128)S(1)}, u32[]{:S(2)}, u32[]{:S(2)}) collective-permute-start(f32[128,512]{1,0:T(8,128)S(1)} %far.1), channel_id=1, source_target_pairs={{0,4},{1,5},{2,6},{3,7},{4,0},{5,1},{6,2},{7,3},{8,12},{9,13},{10,... | collective-permute-start | bytes 786440 | tf_op jit(solution)/shard_map/ppermute | solution.py:22
  24.6 14.6 %collective-permute-start.4 = (f32[128,896]{1,0:T(8,128)S(1)}, f32[128,896]{1,0:T(8,128)S(1)}, u32[]{:S(2)}, u32[]{:S(2)}) collective-permute-start(f32[128,896]{1,0:T(8,128)S(1)} %get-tuple-element.21), channel_id=1, source_target_pairs={{0,31},{1,2},{2,1},{3,4},{4,3},{5,6},{6,5},{7,8},{8,7},{9,10},{10,... | collective-permute-start | bytes 1376264 | tf_op jit(solution)/shard_map/ppermute | solution.py:28
  25.6 13.6 %collective-permute-start.6 = (f32[128,896]{1,0:T(8,128)S(1)}, f32[128,896]{1,0:T(8,128)S(1)}, u32[]{:S(2)}, u32[]{:S(2)}) collective-permute-start(f32[128,896]{1,0:T(8,128)S(1)} %get-tuple-element.23), channel_id=1, source_target_pairs={{0,1},{1,0},{2,3},{3,2},{4,5},{5,4},{6,7},{7,6},{8,9},{9,8},{10,11... | collective-permute-start | bytes 1376264 | tf_op jit(solution)/shard_map/ppermute | solution.py:22
  25.6 13.6 %collective-permute-start.5 = (f32[128,512]{1,0:T(8,128)S(1)}, f32[128,512]{1,0:T(8,128)S(1)}, u32[]{:S(2)}, u32[]{:S(2)}) collective-permute-start(f32[128,512]{1,0:T(8,128)S(1)} %get-tuple-element.22), channel_id=1, source_target_pairs={{0,4},{1,5},{2,6},{3,7},{4,0},{5,1},{6,2},{7,3},{8,12},{9,13},{10,... | collective-permute-start | bytes 786440 | tf_op jit(solution)/shard_map/ppermute | solution.py:22

commit v5 on v4

--- a/solution.py
+++ b/solution.py
@@ -10,7 +10,6 @@
 CENTER = 0.25
 HALF_WIDTH = 1.5
 REACH = 13
-PARTS = 1
 F32 = jnp.float32
 VMEM = pl.BlockSpec(memory_space=pltpu.VMEM)
 SMEM = pl.BlockSpec(memory_space=pltpu.SMEM)
@@ -55,7 +54,8 @@
         self.near = (REACH + 1) // 2
         self.far = slots * size // self.tile
         self.edge = self.near * self.tile
-        self.part = width // PARTS
+        self.half = width // 2
+        self.whole = self.edge - self.tile
         self.outer = 2 * self.near + self.far
         self.places = 2 * (self.outer + self.pairs)
         self.depth = max(sum(run[2] for run in self.runs(p)) for p in range(self.pairs))
@@ -93,17 +93,42 @@
         write(t * tile, value)
 
 
-def write_sends(plan, at, value, to_away, to_near):
-    skip = plan.rows - plan.edge
-    if at < plan.edge:
-        to_away[:, at : at + plan.tile] = value
+def write_sends(plan, side, at, value, sends):
+    tile, half, skip = plan.tile, plan.half, plan.rows - plan.edge
+    first, second, to_near = sends
+    if at < plan.whole:
+        first[:, at : at + tile] = value[:half]
+        second[:, at : at + tile] = value[half:]
+    elif at == plan.whole:
+        lane = lax.broadcasted_iota(jnp.int32, (half, tile), 1)
+        turned = pltpu.roll(value, plan.size, 1)
+        even = jnp.where(lane < plan.size, value[:half], turned[half:])
+        odd = jnp.where(lane < plan.size, turned[:half], value[half:])
+        first[:, at : at + tile] = jnp.where(side[0] == 0, even, odd)
     if at >= skip:
-        to_near[:, at - skip : at - skip + plan.tile] = value
+        to_near[:, at - skip : at - skip + tile] = value
+
+
+def away_tile(plan, side, first, second, t):
+    at = t * plan.tile
+    lanes = slice(at, at + plan.tile)
+    if at < plan.whole:
+        return jnp.concatenate([first[:, lanes], second[:, lanes]], axis=0)
+    packed = first[:, lanes]
+    turned = pltpu.roll(packed, plan.size, 1)
+    even = jnp.concatenate([turned, packed], axis=0)
+    odd = jnp.concatenate([packed, turned], axis=0)
+    return jnp.where(side[0] == 0, even, odd)
+
+
+def send_shapes(plan):
+    lanes = ((plan.half, plan.edge), (plan.half, plan.whole), (plan.width, plan.edge))
+    return [jax.ShapeDtypeStruct(shape, F32) for shape in lanes]
 
 
 def pack_kernel(plan, chunks, side, natural, turned, *rest):
     sends, staged, sems = rest[:-2], *rest[-2:]
-    tile, part, count = plan.tile, plan.part, plan.pairs // chunks
+    tile, count = plan.tile, plan.pairs // chunks
     step = count * tile
 
     def fetch(c):
@@ -120,21 +145,17 @@
     for t in range(plan.pairs):
         at = pl.multiple_of(plan.mirrored(t, side) * tile, tile)
         value = staged[pl.ds(at, tile), :].T
-        at = t * tile
-        turned[:, at : at + tile] = value
-        for h in range(PARTS):
-            rows = slice(h * part, (h + 1) * part)
-            write_sends(plan, at, value[rows], *sends[2 * h : 2 * h + 2])
+        turned[:, t * tile : (t + 1) * tile] = value
+        write_sends(plan, side, t * tile, value, sends)
 
 
 def pack(plan, side, natural):
-    edge = jax.ShapeDtypeStruct((plan.part, plan.edge), F32)
     chunks = 4 if plan.pairs % 4 == 0 else 1
     return pl.pallas_call(
         functools.partial(pack_kernel, plan, chunks),
-        out_shape=[pltpu.VMEM((plan.width, plan.rows), F32)] + [edge] * (2 * PARTS),
+        out_shape=[pltpu.VMEM((plan.width, plan.rows), F32)] + send_shapes(plan),
         in_specs=[SMEM, pl.BlockSpec(memory_space=pltpu.HBM)],
-        out_specs=[VMEM] * (1 + 2 * PARTS),
+        out_specs=[VMEM] * 4,
         scratch_shapes=[
             pltpu.VMEM((plan.rows, plan.width), F32),
             pltpu.SemaphoreType.DMA((chunks,)),
@@ -163,13 +184,10 @@
 
 
 def own_halves(plan, vectors, halves):
-    tile, width, part = plan.tile, plan.width, plan.part
-    for at in range(0, plan.rows, tile):
-        for h, ref in enumerate(vectors):
-            high, low = split(ref[:, at : at + tile])
-            rows = slice(h * ref.shape[0], (h + 1) * ref.shape[0])
-            halves[rows, at : at + tile] = high
-            halves[width + rows.start : width + rows.stop, at : at + tile] = low
+    for at in range(0, plan.rows, plan.tile):
+        high, low = split(vectors[:, at : at + plan.tile])
+        halves[: plan.width, at : at + plan.tile] = high
+        halves[plan.width :, at : at + plan.tile] = low
 
 
 def own_product(plan, p, halves, band, inner):
@@ -195,7 +213,7 @@
         fetch(p).start()
     for p in range(plan.pairs):
         staged[p, depth:, :] = jnp.zeros((size, tile), F32)
-    own_halves(plan, [vectors], halves)
+    own_halves(plan, vectors, halves)
 
     for p in range(plan.pairs):
         fetch(p).wait()
@@ -241,8 +259,7 @@
     )(side, inverse, pltpu.with_memory_space_constraint(ham_t, pltpu.HBM), vectors)
 
 
-def inner_kernel(plan, *refs):
-    vectors, band, inner, halves = refs[:PARTS], *refs[PARTS:]
+def inner_kernel(plan, vectors, band, inner, halves):
     own_halves(plan, vectors, halves)
     for p in range(plan.pairs):
         own_product(plan, p, halves, band, inner)
@@ -252,25 +269,24 @@
     return pl.pallas_call(
         functools.partial(inner_kernel, plan),
         out_shape=pltpu.VMEM((plan.width, plan.rows), F32),
-        in_specs=[VMEM] * (PARTS + 1),
+        in_specs=[VMEM] * 2,
         out_specs=VMEM,
         scratch_shapes=[pltpu.VMEM((2 * plan.width, plan.rows), jnp.bfloat16)],
         compiler_params=params(8),
         cost_estimate=cost(8 * plan.width * plan.rows**2, 0),
         name="inner",
-    )(*vectors, band)
-
-
-def outer_products(plan, h, away, far, near, band, halves):
-    tile, part = plan.tile, plan.part
-    tiles = [(away, plan.near - 1 - t) for t in range(plan.near)]
-    tiles += [(far, t) for t in range(plan.far)]
-    tiles += [(near, plan.near - 1 - t) for t in range(plan.near)]
-    for t, (ref, source) in enumerate(tiles):
-        rows = slice(h * part, (h + 1) * part) if ref.shape[0] > part else slice(None)
-        high, low = split(ref[rows, source * tile : (source + 1) * tile])
-        halves[:part, t * tile : (t + 1) * tile] = high
-        halves[part:, t * tile : (t + 1) * tile] = low
+    )(vectors, band)
+
+
+def outer_products(plan, side, first, second, far, near, band, halves):
+    tile, width = plan.tile, plan.width
+    tiles = [lambda t=t: away_tile(plan, side, first, second, t) for t in range(plan.near)][::-1]
+    tiles += [lambda t=t: far[:, t * tile : (t + 1) * tile] for t in range(plan.far)]
+    tiles += [lambda t=t: near[:, t * tile : (t + 1) * tile] for t in range(plan.near)][::-1]
+    for t, read in enumerate(tiles):
+        high, low = split(read())
+        halves[:width, t * tile : (t + 1) * tile] = high
+        halves[width:, t * tile : (t + 1) * tile] = low
     for p in range(plan.pairs):
         begin, end = (tile * bound for bound in plan.outer_range(p))
         sums = jnp.dot(
@@ -280,16 +296,16 @@
 
 
 def first_kernel(
-    plan, h, side, asked, away, far, near, band, inner, own, value, to_away, to_near, to_far, halves
+    plan, side, asked, first, second, far, near, band, inner, own, value, to_far, *rest
 ):
-    tile, part = plan.tile, plan.part
-    rows = slice(h * part, (h + 1) * part)
-    for at, product in outer_products(plan, h, away, far, near, band, halves):
+    sends, halves = rest[:-1], rest[-1]
+    tile = plan.tile
+    for at, product in outer_products(plan, side, first, second, far, near, band, halves):
         lanes = slice(at, at + tile)
-        shifted = product + inner[rows, lanes] - CENTER * own[rows, lanes]
+        shifted = product + inner[:, lanes] - CENTER * own[:, lanes]
         term = shifted * (1.0 / HALF_WIDTH)
         value[:, lanes] = term
-        write_sends(plan, at, term, to_away, to_near)
+        write_sends(plan, side, at, term, sends)
 
     def write(at, term):
         to_far[:, at : at + tile] = term
@@ -297,52 +313,41 @@
     write_far(plan, side, asked, value, write)
 
 
-def run_first(plan, h, side, asked, arrived, band, inner, own):
-    edge = jax.ShapeDtypeStruct((plan.part, plan.edge), F32)
-    far = jax.ShapeDtypeStruct((plan.part, plan.far * plan.tile), F32)
-    return pl.pallas_call(
-        functools.partial(first_kernel, plan, h),
-        out_shape=[pltpu.VMEM((plan.part, plan.rows), F32), edge, edge, far],
-        in_specs=[SMEM] * 2 + [VMEM] * 6,
-        out_specs=[VMEM] * 4,
-        scratch_shapes=[pltpu.VMEM((2 * plan.part, plan.outer * plan.tile), jnp.bfloat16)],
+def run_first(plan, side, asked, arrived, band, inner, own):
+    far = jax.ShapeDtypeStruct((plan.width, plan.far * plan.tile), F32)
+    return pl.pallas_call(
+        functools.partial(first_kernel, plan),
+        out_shape=[pltpu.VMEM((plan.width, plan.rows), F32), far] + send_shapes(plan),
+        in_specs=[SMEM] * 2 + [VMEM] * 7,
+        out_specs=[VMEM] * 5,
+        scratch_shapes=[pltpu.VMEM((2 * plan.width, plan.outer * plan.tile), jnp.bfloat16)],
         compiler_params=params(8),
-        cost_estimate=cost(8 * plan.part * plan.rows**2, 0),
+        cost_estimate=cost(8 * plan.width * plan.rows**2, 0),
         name="first",
     )(side, asked, *arrived, band, inner, own)
 
 
-def second_kernel(plan, h, side, away, far, near, band, inner, own, start, *rest):
-    earlier, out, halves = rest[:-2], *rest[-2:]
-    tile, part = plan.tile, plan.part
-    rows = slice(h * part, (h + 1) * part)
-    for at, product in outer_products(plan, h, away, far, near, band, halves):
+def second_kernel(plan, side, first, second, far, near, band, inner, own, start, out, halves):
+    tile = plan.tile
+    for at, product in outer_products(plan, side, first, second, far, near, band, halves):
         lanes = slice(at, at + tile)
-        shifted = product + inner[rows, lanes] - CENTER * own[:, lanes]
-        term = 2.0 / HALF_WIDTH * shifted - start[rows, lanes]
-        if h < PARTS - 1:
-            out[:, lanes] = term
-        else:
-            whole = [ref[:, lanes] for ref in earlier] + [term]
-            place = pl.multiple_of(plan.mirrored(at // tile, side) * tile, tile)
-            out[pl.ds(place, tile), :] = jnp.concatenate(whole, axis=0).T
-
-
-def run_second(plan, h, side, arrived, band, inner, own, start, earlier):
-    if h < PARTS - 1:
-        out, earlier = pltpu.VMEM((plan.part, plan.rows), F32), []
-    else:
-        out = jax.ShapeDtypeStruct((plan.rows, plan.width), F32)
-    return pl.pallas_call(
-        functools.partial(second_kernel, plan, h),
-        out_shape=out,
-        in_specs=[SMEM] + [VMEM] * (7 + len(earlier)),
+        shifted = product + inner[:, lanes] - CENTER * own[:, lanes]
+        term = 2.0 / HALF_WIDTH * shifted - start[:, lanes]
+        place = pl.multiple_of(plan.mirrored(at // tile, side) * tile, tile)
+        out[pl.ds(place, tile), :] = term.T
+
+
+def run_second(plan, side, arrived, band, inner, own, start):
+    return pl.pallas_call(
+        functools.partial(second_kernel, plan),
+        out_shape=jax.ShapeDtypeStruct((plan.rows, plan.width), F32),
+        in_specs=[SMEM] + [VMEM] * 8,
         out_specs=VMEM,
-        scratch_shapes=[pltpu.VMEM((2 * plan.part, plan.outer * plan.tile), jnp.bfloat16)],
+        scratch_shapes=[pltpu.VMEM((2 * plan.width, plan.outer * plan.tile), jnp.bfloat16)],
         compiler_params=params(8),
-        cost_estimate=cost(8 * plan.part * plan.rows**2, 0),
+        cost_estimate=cost(8 * plan.width * plan.rows**2, 0),
         name="second",
-    )(side, *arrived, band, inner, own, start, *earlier)
+    )(side, *arrived, band, inner, own, start)
 
 
 def after(value, *others):
@@ -360,20 +365,15 @@
 
     side = (lax.axis_index("rows") % 2).astype(jnp.int32).reshape(1)
 
-    def exchange(to_away, to_near):
-        return swap_chips(to_away, "rows"), partner(to_near, "rows", 0)
+    def exchange(listed, sends):
+        far = partner(listed, "rows", swap_level)
+        first, second = (swap_chips(value, "rows") for value in sends[:2])
+        return first, second, far, partner(sends[2], "rows", 0)
 
     asked = partner(far_list, "rows", swap_level)
     start, *sends = pack(plan, side, subspace)
     listed = gather_far(plan, side, asked, start)
-    far = partner(listed, "rows", swap_level)
-    arrived = []
-    for h in range(PARTS):
-        to_away, to_near = sends[2 * h : 2 * h + 2]
-        if h > 0:
-            to_away, to_near = lax.optimization_barrier((to_away, to_near, listed))[:2]
-        away, near = exchange(to_away, to_near)
-        arrived.append((away, far, near))
+    arrived = exchange(listed, sends)
 
     block_cols = after(block_cols, listed)
     near, far_slots = 2 * plan.near, 2 * plan.far
@@ -400,25 +400,10 @@
 
     band, inner = make_band(plan, side, inverse, hamiltonian.T, start)
 
-    values, later = [], []
-    for h in range(PARTS):
-        if values:
-            inner = after(inner, values[-1])
-        value, to_away, to_near, listed = run_first(
-            plan, h, side, asked, arrived[h], band, inner, start
-        )
-        values.append(value)
-        far = partner(listed, "rows", swap_level)
-        away, near = exchange(to_away, to_near)
-        later.append((away, far, near))
-    inner = run_inner(plan, values, band)
-    result = []
-    for h in range(PARTS):
-        if result:
-            inner = after(inner, result[-1])
-        out = run_second(plan, h, side, later[h], band, inner, values[h], start, result)
-        result.append(out)
-    return result[-1]
+    value, listed, *sends = run_first(plan, side, asked, arrived, band, inner, start)
+    arrived = exchange(listed, sends)
+    inner = run_inner(plan, value, band)
+    return run_second(plan, side, arrived, band, inner, value, start)
 
 
 def solution(mesh):

time: 42.6 us -> 42 us (0.986)
  waiting for transfers between devices: 14 us -> 5.9 us
  starting transfers between devices: 7.72 us -> 14.9 us
    ppermute x5, waiting for transfers between devices: 14 us -> 1.17 us  [partner(): return lax.ppermute(value, axis, pairs)]
    ppermute x2 -> x4, starting transfers between devices: 4.67 us -> 10.7 us  [swap_chips(): return lax.ppermute(value, axis, pairs)]
    ppermute x2 -> x4, waiting for transfers between devices: 0.01 us -> 4.73 us  [swap_chips(): return lax.ppermute(value, axis, pairs)]
    ppermute x5, starting transfers between devices: 3.05 us -> 4.2 us  [partner(): return lax.ppermute(value, axis, pairs)]
  transfers between devices with their start and end apart: 7 -> 9, of which waited for: 2 -> 2; matrix products, arithmetic and copies ran while one was open for 2% -> 2% of each run, Pallas kernels for 32% -> 33%
where the time goes in v5:
time: 42 us; the launch traced here: 41.8 us
  Pallas kernels  19.8 us (47%)
  starting transfers between devices  14.9 us (35%)
  waiting for transfers between devices  5.9 us (14%)
  other arithmetic  0.93 us (2%)
    ppermute x4, starting transfers between devices, swap_chips(): return lax.ppermute(value, axis, pairs)  10.7 us
    pallas_call x1, Pallas kernels, make_band(): pl.pallas_call(functools.partial(band_kernel, plan, depth), out_shape=[pl...  8.95 us
    ppermute x4, waiting for transfers between devices, swap_chips(): return lax.ppermute(value, axis, pairs)  4.73 us
    ppermute x5, starting transfers between devices, partner(): return lax.ppermute(value, axis, pairs)  4.2 us
    pallas_call x1, Pallas kernels, run_second(): pl.pallas_call(functools.partial(second_kernel, plan), out_shape=jax.Shap...  3.14 us
    pallas_call x1, Pallas kernels, run_first(): pl.pallas_call(functools.partial(first_kernel, plan), out_shape=[pltpu.VM...  2.87 us
    pallas_call x1, Pallas kernels, run_inner(): pl.pallas_call(functools.partial(inner_kernel, plan), out_shape=pltpu.VME...  2.37 us
    pallas_call x1, Pallas kernels, pack(): pl.pallas_call(functools.partial(pack_kernel, plan, chunks), out_shape=[p...  1.71 us
  transfers between devices with their start and end apart: 9, of which 2 were waited for; matrix products, arithmetic and copies ran while one was open for 2% of the time, Pallas kernels for 33%

profile of v5, /device:TPU:0, one launch (start us, length us, event | category | flops | bytes accessed | tf_op | source)
XLA Modules:
  0.0 41.8 jit_solution(9391601867072032096)
XLA Ops:
  0.0 3.0 %collective-permute-start = (s32[1,8]{1,0:T(1,128)}, s32[1,8]{1,0:T(1,128)S(1)}, u32[]{:S(2)}, u32[]{:S(2)}) collective-permute-start(s32[1,8]{1,0:T(1,128)} %param.7), channel_id=1, source_target_pairs={{0,4},{1,5},{2,6},{3,7},{4,0},{5,1},{6,2},{7,3},{8,12},{9,13},{10,... | collective-permute-start | bytes 104 | tf_op jit(solution)/shard_map/ppermute | solution.py:21
  3.0 1.7 %pack.1 = (f32[128,1536]{1,0:T(8,128)S(1)}, f32[64,896]{1,0:T(8,128)S(1)}, f32[64,768]{1,0:T(8,128)S(1)}, f32[128,896]{1,0:T(8,128)S(1)}) custom-call(s32[1]{0:T(128)} %bitcast.side, f32[1536,128]{1,0:T(8,128)} %natural.1), custom_call_target="tpu_custom_call" | custom-call | tf_op jit(solution)/shard_map/pack/pallas_call | solution.py:154
  4.7 3.7 %collective-permute-start.2 = (f32[64,768]{1,0:T(8,128)S(1)}, f32[64,768]{1,0:T(8,128)S(1)}, u32[]{:S(2)}, u32[]{:S(2)}) collective-permute-start(f32[64,768]{1,0:T(8,128)S(1)} %get-tuple-element.18), channel_id=1, source_target_pairs={{0,31},{1,2},{2,1},{3,4},{4,3},{5,6},{6,5},{7,8},{8,7},{9,10},{10,... | collective-permute-start | bytes 589832 | tf_op jit(solution)/shard_map/ppermute | solution.py:27
  8.4 1.7 %collective-permute-start.1 = (f32[64,896]{1,0:T(8,128)S(1)}, f32[64,896]{1,0:T(8,128)S(1)}, u32[]{:S(2)}, u32[]{:S(2)}) collective-permute-start(f32[64,896]{1,0:T(8,128)S(1)} %get-tuple-element.17), channel_id=1, source_target_pairs={{0,31},{1,2},{2,1},{3,4},{4,3},{5,6},{6,5},{7,8},{8,7},{9,10},{10,... | collective-permute-start | bytes 688136 | tf_op jit(solution)/shard_map/ppermute | solution.py:27
  10.1 0.0 collective-permute-start.4
  10.1 0.0 collective-permute-done.asked
  10.1 0.8 %far.1 = f32[128,512]{1,0:T(8,128)S(1)} custom-call(s32[1]{0:T(128)} %bitcast.side, s32[1,8]{1,0:T(1,128)S(1)} %collective-permute-done.asked, f32[128,1536]{1,0:T(8,128)S(1)} %get-tuple-element.19.turned.vectors.own.start), custom_call_target="tpu_custom_call" | custom-call | tf_op jit(solution)/shard_map/far/pallas_call | solution.py:176
  10.9 0.1 collective-permute-start.3
  11.0 0.7 %fusion.5 = s32[24,27]{1,0:T(8,128)S(1)} fusion(s32[24,27]{1,0:T(8,128)} %param.6, s32[]{:T(128)} %select_n.31, s32[]{:T(128)S(6)} %mul.15), kind=kLoop, calls=%fused_computation.13 | loop fusion | flops 23328 | bytes 5192 | tf_op jit(solution)/shard_map/jit(_where)/select_n | solution.py:383
  11.7 0.1 copy.5
  11.8 0.2 select_reduce_fusion
  12.0 8.9 %band.1 = (bf16[12,2432,256]{2,1,0:T(8,128)(2,1)S(1)}, f32[128,1536]{1,0:T(8,128)S(1)}) custom-call(s32[1]{0:T(128)} %bitcast.side, s32[24,60]{1,0:T(8,128)S(1)} %broadcast_add_fusion.inverse, f32[1728,1536]{1,0:T(8,128)} %bitcast.2, f32[128,1536]{1,0:T(8,128)S(1)} %get-tuple-element.19.turned.vectors.own.start), custom_call_target="tpu_custom_call" | custom-call | bytes 21233664 | tf_op jit(solution)/shard_map/band/pallas_call | solution.py:243
  20.9 0.0 collective-permute-done.2.second
  20.9 0.0 collective-permute-done.1.first
  21.0 1.2 %collective-permute-done.3.far = f32[128,512]{1,0:T(8,128)S(1)} collective-permute-done((f32[128,512]{1,0:T(8,128)S(1)}, f32[128,512]{1,0:T(8,128)S(1)}, u32[]{:S(2)}, u32[]{:S(2)}) %collective-permute-start.3) | collective-permute-done | bytes 262176 | tf_op jit(solution)/shard_map/ppermute | solution.py:21
  22.1 0.0 collective-permute-done.4.near
  22.1 2.9 %first.1 = (f32[128,1536]{1,0:T(8,128)S(1)}, f32[128,512]{1,0:T(8,128)S(1)}, f32[64,896]{1,0:T(8,128)S(1)}, f32[64,768]{1,0:T(8,128)S(1)}, f32[128,896]{1,0:T(8,128)S(1)}) custom-call(s32[1]{0:T(128)} %bitcast.side, s32[1,8]{1,0:T(1,128)S(1)} %collective-permute-done.asked, f32[64,896]{1,0:T(8,128)S(1)} %collective-permute-done.1.first, ...), custom_call_target="tpu_custom_call" | custom-call | flops 2415919104 | tf_op jit(solution)/shard_map/first/pallas_call | solution.py:318
  25.0 0.1 collective-permute-start.8
  25.1 1.1 %collective-permute-start.7 = (f32[128,512]{1,0:T(8,128)S(1)}, f32[128,512]{1,0:T(8,128)S(1)}, u32[]{:S(2)}, u32[]{:S(2)}) collective-permute-start(f32[128,512]{1,0:T(8,128)S(1)} %get-tuple-element.26), channel_id=1, source_target_pairs={{0,4},{1,5},{2,6},{3,7},{4,0},{5,1},{6,2},{7,3},{8,12},{9,13},{10,... | collective-permute-start | bytes 786440 | tf_op jit(solution)/shard_map/ppermute | solution.py:21
  26.2 3.6 %collective-permute-start.5 = (f32[64,896]{1,0:T(8,128)S(1)}, f32[64,896]{1,0:T(8,128)S(1)}, u32[]{:S(2)}, u32[]{:S(2)}) collective-permute-start(f32[64,896]{1,0:T(8,128)S(1)} %get-tuple-element.24), channel_id=1, source_target_pairs={{0,31},{1,2},{2,1},{3,4},{4,3},{5,6},{6,5},{7,8},{8,7},{9,10},{10,... | collective-permute-start | bytes 688136 | tf_op jit(solution)/shard_map/ppermute | solution.py:27
  29.8 1.7 %collective-permute-start.6 = (f32[64,768]{1,0:T(8,128)S(1)}, f32[64,768]{1,0:T(8,128)S(1)}, u32[]{:S(2)}, u32[]{:S(2)}) collective-permute-start(f32[64,768]{1,0:T(8,128)S(1)} %get-tuple-element.25), channel_id=1, source_target_pairs={{0,31},{1,2},{2,1},{3,4},{4,3},{5,6},{6,5},{7,8},{8,7},{9,10},{10,... | collective-permute-start | bytes 589832 | tf_op jit(solution)/shard_map/ppermute | solution.py:27
  31.5 2.4 %inner.1 = f32[128,1536]{1,0:T(8,128)S(1)} custom-call(f32[128,1536]{1,0:T(8,128)S(1)} %get-tuple-element.28.vectors.own, bf16[12,2432,256]{2,1,0:T(8,128)(2,1)S(1)} %get-tuple-element.22.band), custom_call_target="tpu_custom_call" | custom-call | flops 2415919104 | tf_op jit(solution)/shard_map/inner/pallas_call | solution.py:269
  33.9 4.7 %collective-permute-done.6.second = f32[64,768]{1,0:T(8,128)S(1)} collective-permute-done((f32[64,768]{1,0:T(8,128)S(1)}, f32[64,768]{1,0:T(8,128)S(1)}, u32[]{:S(2)}, u32[]{:S(2)}) %collective-permute-start.6) | collective-permute-done | bytes 196640 | tf_op jit(solution)/shard_map/ppermute | solution.py:27
  38.6 0.0 collective-permute-done.5.first
  38.6 0.0 collective-permute-done.7.far
  38.6 0.0 collective-permute-done.8.near
  38.6 3.1 %second.1 = f32[1536,128]{1,0:T(8,128)} custom-call(s32[1]{0:T(128)} %bitcast.side, f32[64,896]{1,0:T(8,128)S(1)} %collective-permute-done.5.first, f32[64,768]{1,0:T(8,128)S(1)} %collective-permute-done.6.second, f32[128,512]{1,0:T(8,128)S(1)} %collective-permute-done.7.far, f32[128,896]{1,0:T(8,128)S(1)} %collective-permute-done.8.near, ...), custom_call_target="tpu_custom_call" | custom-call | flops 2415919104 | tf_op jit(solution)/shard_map/second/pallas_call | solution.py:341
  (2 shorter events, 0.0 us)
Async XLA Ops:
  0.0 10.1 %collective-permute-start = (s32[1,8]{1,0:T(1,128)}, s32[1,8]{1,0:T(1,128)S(1)}, u32[]{:S(2)}, u32[]{:S(2)}) collective-permute-start(s32[1,8]{1,0:T(1,128)} %param.7), channel_id=1, source_target_pairs={{0,4},{1,5},{2,6},{3,7},{4,0},{5,1},{6,2},{7,3},{8,12},{9,13},{10,... | collective-permute-start | bytes 104 | tf_op jit(solution)/shard_map/ppermute | solution.py:21
  4.7 16.3 %collective-permute-start.2 = (f32[64,768]{1,0:T(8,128)S(1)}, f32[64,768]{1,0:T(8,128)S(1)}, u32[]{:S(2)}, u32[]{:S(2)}) collective-permute-start(f32[64,768]{1,0:T(8,128)S(1)} %get-tuple-element.18), channel_id=1, source_target_pairs={{0,31},{1,2},{2,1},{3,4},{4,3},{5,6},{6,5},{7,8},{8,7},{9,10},{10,... | collective-permute-start | bytes 589832 | tf_op jit(solution)/shard_map/ppermute | solution.py:27
  8.4 12.6 %collective-permute-start.1 = (f32[64,896]{1,0:T(8,128)S(1)}, f32[64,896]{1,0:T(8,128)S(1)}, u32[]{:S(2)}, u32[]{:S(2)}) collective-permute-start(f32[64,896]{1,0:T(8,128)S(1)} %get-tuple-element.17), channel_id=1, source_target_pairs={{0,31},{1,2},{2,1},{3,4},{4,3},{5,6},{6,5},{7,8},{8,7},{9,10},{10,... | collective-permute-start | bytes 688136 | tf_op jit(solution)/shard_map/ppermute | solution.py:27
  10.1 12.0 %collective-permute-start.4 = (f32[128,896]{1,0:T(8,128)S(1)}, f32[128,896]{1,0:T(8,128)S(1)}, u32[]{:S(2)}, u32[]{:S(2)}) collective-permute-start(f32[128,896]{1,0:T(8,128)S(1)} %get-tuple-element.20), channel_id=1, source_target_pairs={{0,1},{1,0},{2,3},{3,2},{4,5},{5,4},{6,7},{7,6},{8,9},{9,8},{10,11... | collective-permute-start | bytes 1376264 | tf_op jit(solution)/shard_map/ppermute | solution.py:21
  10.9 11.2 %collective-permute-start.3 = (f32[128,512]{1,0:T(8,128)S(1)}, f32[128,512]{1,0:T(8,128)S(1)}, u32[]{:S(2)}, u32[]{:S(2)}) collective-permute-start(f32[128,512]{1,0:T(8,128)S(1)} %far.1), channel_id=1, source_target_pairs={{0,4},{1,5},{2,6},{3,7},{4,0},{5,1},{6,2},{7,3},{8,12},{9,13},{10,... | collective-permute-start | bytes 786440 | tf_op jit(solution)/shard_map/ppermute | solution.py:21
  25.0 13.6 %collective-permute-start.8 = (f32[128,896]{1,0:T(8,128)S(1)}, f32[128,896]{1,0:T(8,128)S(1)}, u32[]{:S(2)}, u32[]{:S(2)}) collective-permute-start(f32[128,896]{1,0:T(8,128)S(1)} %get-tuple-element.27), channel_id=1, source_target_pairs={{0,1},{1,0},{2,3},{3,2},{4,5},{5,4},{6,7},{7,6},{8,9},{9,8},{10,11... | collective-permute-start | bytes 1376264 | tf_op jit(solution)/shard_map/ppermute | solution.py:21
  25.1 13.5 %collective-permute-start.7 = (f32[128,512]{1,0:T(8,128)S(1)}, f32[128,512]{1,0:T(8,128)S(1)}, u32[]{:S(2)}, u32[]{:S(2)}) collective-permute-start(f32[128,512]{1,0:T(8,128)S(1)} %get-tuple-element.26), channel_id=1, source_target_pairs={{0,4},{1,5},{2,6},{3,7},{4,0},{5,1},{6,2},{7,3},{8,12},{9,13},{10,... | collective-permute-start | bytes 786440 | tf_op jit(solution)/shard_map/ppermute | solution.py:21
  26.2 12.4 %collective-permute-start.5 = (f32[64,896]{1,0:T(8,128)S(1)}, f32[64,896]{1,0:T(8,128)S(1)}, u32[]{:S(2)}, u32[]{:S(2)}) collective-permute-start(f32[64,896]{1,0:T(8,128)S(1)} %get-tuple-element.24), channel_id=1, source_target_pairs={{0,31},{1,2},{2,1},{3,4},{4,3},{5,6},{6,5},{7,8},{8,7},{9,10},{10,... | collective-permute-start | bytes 688136 | tf_op jit(solution)/shard_map/ppermute | solution.py:27
  29.8 8.8 %collective-permute-start.6 = (f32[64,768]{1,0:T(8,128)S(1)}, f32[64,768]{1,0:T(8,128)S(1)}, u32[]{:S(2)}, u32[]{:S(2)}) collective-permute-start(f32[64,768]{1,0:T(8,128)S(1)} %get-tuple-element.25), channel_id=1, source_target_pairs={{0,31},{1,2},{2,1},{3,4},{4,3},{5,6},{6,5},{7,8},{8,7},{9,10},{10,... | collective-permute-start | bytes 589832 | tf_op jit(solution)/shard_map/ppermute | solution.py:27

commit v6 on v5

--- a/solution.py
+++ b/solution.py
@@ -12,6 +12,7 @@
 REACH = 13
 F32 = jnp.float32
 VMEM = pl.BlockSpec(memory_space=pltpu.VMEM)
+HBM = pl.BlockSpec(memory_space=pltpu.HBM)
 SMEM = pl.BlockSpec(memory_space=pltpu.SMEM)
 
 
@@ -95,26 +96,26 @@
 
 def write_sends(plan, side, at, value, sends):
     tile, half, skip = plan.tile, plan.half, plan.rows - plan.edge
-    first, second, to_near = sends
+    to_away, to_near = sends
     if at < plan.whole:
-        first[:, at : at + tile] = value[:half]
-        second[:, at : at + tile] = value[half:]
+        to_away[:, at : at + tile] = value[:half]
+        to_away[:, plan.edge + at : plan.edge + at + tile] = value[half:]
     elif at == plan.whole:
         lane = lax.broadcasted_iota(jnp.int32, (half, tile), 1)
         turned = pltpu.roll(value, plan.size, 1)
         even = jnp.where(lane < plan.size, value[:half], turned[half:])
         odd = jnp.where(lane < plan.size, turned[:half], value[half:])
-        first[:, at : at + tile] = jnp.where(side[0] == 0, even, odd)
+        to_away[:, at : at + tile] = jnp.where(side[0] == 0, even, odd)
     if at >= skip:
         to_near[:, at - skip : at - skip + tile] = value
 
 
-def away_tile(plan, side, first, second, t):
-    at = t * plan.tile
-    lanes = slice(at, at + plan.tile)
+def away_tile(plan, side, away, t):
+    at, tile = t * plan.tile, plan.tile
+    packed = away[:, at : at + tile]
     if at < plan.whole:
-        return jnp.concatenate([first[:, lanes], second[:, lanes]], axis=0)
-    packed = first[:, lanes]
+        rest = away[:, plan.edge + at : plan.edge + at + tile]
+        return jnp.concatenate([packed, rest], axis=0)
     turned = pltpu.roll(packed, plan.size, 1)
     even = jnp.concatenate([turned, packed], axis=0)
     odd = jnp.concatenate([packed, turned], axis=0)
@@ -122,7 +123,7 @@
 
 
 def send_shapes(plan):
-    lanes = ((plan.half, plan.edge), (plan.half, plan.whole), (plan.width, plan.edge))
+    lanes = ((plan.half, plan.edge + plan.whole), (plan.width, plan.edge))
     return [jax.ShapeDtypeStruct(shape, F32) for shape in lanes]
 
 
@@ -154,8 +155,8 @@
     return pl.pallas_call(
         functools.partial(pack_kernel, plan, chunks),
         out_shape=[pltpu.VMEM((plan.width, plan.rows), F32)] + send_shapes(plan),
-        in_specs=[SMEM, pl.BlockSpec(memory_space=pltpu.HBM)],
-        out_specs=[VMEM] * 4,
+        in_specs=[SMEM, HBM],
+        out_specs=[VMEM] * 3,
         scratch_shapes=[
             pltpu.VMEM((plan.rows, plan.width), F32),
             pltpu.SemaphoreType.DMA((chunks,)),
@@ -246,7 +247,7 @@
             pltpu.VMEM((plan.pairs, plan.depth, 2 * tile), jnp.bfloat16),
             pltpu.VMEM((plan.width, rows), F32),
         ],
-        in_specs=[SMEM, SMEM, pl.BlockSpec(memory_space=pltpu.HBM), VMEM],
+        in_specs=[SMEM, SMEM, HBM, VMEM],
         out_specs=[VMEM, VMEM],
         scratch_shapes=[
             pltpu.VMEM((plan.pairs, depth + size, tile), F32),
@@ -278,29 +279,54 @@
     )(vectors, band)
 
 
-def outer_products(plan, side, first, second, far, near, band, halves):
-    tile, width = plan.tile, plan.width
-    tiles = [lambda t=t: away_tile(plan, side, first, second, t) for t in range(plan.near)][::-1]
-    tiles += [lambda t=t: far[:, t * tile : (t + 1) * tile] for t in range(plan.far)]
-    tiles += [lambda t=t: near[:, t * tile : (t + 1) * tile] for t in range(plan.near)][::-1]
-    for t, read in enumerate(tiles):
-        high, low = split(read())
+def outer_products(plan, side, away, far, near, band, halves, near_held, sem):
+    tile, width, edge = plan.tile, plan.width, plan.near
+    copy = pltpu.make_async_copy(near.at[1 - side[0]], near_held, sem)
+    copy.start()
+
+    def put(t, value):
+        high, low = split(value)
         halves[:width, t * tile : (t + 1) * tile] = high
         halves[width:, t * tile : (t + 1) * tile] = low
+
+    for t in range(edge):
+        put(edge - 1 - t, away_tile(plan, side, away, t))
+    for t in range(plan.far):
+        put(edge + t, far[:, t * tile : (t + 1) * tile])
+    waited = False
     for p in range(plan.pairs):
-        begin, end = (tile * bound for bound in plan.outer_range(p))
+        begin, end = plan.outer_range(p)
+        if end > edge + plan.far and not waited:
+            copy.wait()
+            for t in range(edge):
+                put(plan.outer - 1 - t, near_held[:, t * tile : (t + 1) * tile])
+            waited = True
+        begin, end = begin * tile, end * tile
         sums = jnp.dot(
             halves[:, begin:end], band[p, : end - begin, :], preferred_element_type=F32
         )
         yield p * tile, fold(sums)
 
 
+def outer_scratch(plan):
+    return [
+        pltpu.VMEM((2 * plan.width, plan.outer * plan.tile), jnp.bfloat16),
+        pltpu.VMEM((plan.width, plan.edge), F32),
+        pltpu.SemaphoreType.DMA,
+    ]
+
+
+def in_hbm(arrived):
+    away, far, near = arrived
+    return away, far, pltpu.with_memory_space_constraint(near, pltpu.HBM)
+
+
 def first_kernel(
-    plan, side, asked, first, second, far, near, band, inner, own, value, to_far, *rest
+    plan, side, asked, away, far, near, band, inner, own, value, to_far, *rest
 ):
-    sends, halves = rest[:-1], rest[-1]
+    sends, held = rest[:2], rest[2:]
     tile = plan.tile
-    for at, product in outer_products(plan, side, first, second, far, near, band, halves):
+    for at, product in outer_products(plan, side, away, far, near, band, *held):
         lanes = slice(at, at + tile)
         shifted = product + inner[:, lanes] - CENTER * own[:, lanes]
         term = shifted * (1.0 / HALF_WIDTH)
@@ -318,18 +344,18 @@
     return pl.pallas_call(
         functools.partial(first_kernel, plan),
         out_shape=[pltpu.VMEM((plan.width, plan.rows), F32), far] + send_shapes(plan),
-        in_specs=[SMEM] * 2 + [VMEM] * 7,
-        out_specs=[VMEM] * 5,
-        scratch_shapes=[pltpu.VMEM((2 * plan.width, plan.outer * plan.tile), jnp.bfloat16)],
+        in_specs=[SMEM] * 2 + [VMEM] * 2 + [HBM] + [VMEM] * 3,
+        out_specs=[VMEM] * 4,
+        scratch_shapes=outer_scratch(plan),
         compiler_params=params(8),
         cost_estimate=cost(8 * plan.width * plan.rows**2, 0),
         name="first",
-    )(side, asked, *arrived, band, inner, own)
-
-
-def second_kernel(plan, side, first, second, far, near, band, inner, own, start, out, halves):
+    )(side, asked, *in_hbm(arrived), band, inner, own)
+
+
+def second_kernel(plan, side, away, far, near, band, inner, own, start, out, *held):
     tile = plan.tile
-    for at, product in outer_products(plan, side, first, second, far, near, band, halves):
+    for at, product in outer_products(plan, side, away, far, near, band, *held):
         lanes = slice(at, at + tile)
         shifted = product + inner[:, lanes] - CENTER * own[:, lanes]
         term = 2.0 / HALF_WIDTH * shifted - start[:, lanes]
@@ -341,13 +367,13 @@
     return pl.pallas_call(
         functools.partial(second_kernel, plan),
         out_shape=jax.ShapeDtypeStruct((plan.rows, plan.width), F32),
-        in_specs=[SMEM] + [VMEM] * 8,
+        in_specs=[SMEM] + [VMEM] * 2 + [HBM] + [VMEM] * 4,
         out_specs=VMEM,
-        scratch_shapes=[pltpu.VMEM((2 * plan.width, plan.outer * plan.tile), jnp.bfloat16)],
+        scratch_shapes=outer_scratch(plan),
         compiler_params=params(8),
         cost_estimate=cost(8 * plan.width * plan.rows**2, 0),
         name="second",
-    )(side, *arrived, band, inner, own, start)
+    )(side, *in_hbm(arrived), band, inner, own, start)
 
 
 def after(value, *others):
@@ -367,8 +393,10 @@
 
     def exchange(listed, sends):
         far = partner(listed, "rows", swap_level)
-        first, second = (swap_chips(value, "rows") for value in sends[:2])
-        return first, second, far, partner(sends[2], "rows", 0)
+        to_away, to_near = sends
+        pairs = [[i, i + 1] for i in range(0, device_count, 2)]
+        near = lax.all_gather(to_near, "rows", axis_index_groups=pairs)
+        return swap_chips(to_away, "rows"), far, near
 
     asked = partner(far_list, "rows", swap_level)
     start, *sends = pack(plan, side, subspace)

time: 42 us -> 43.7 us (1.040)
  blocking collectives: 0 us -> 5.18 us
  starting transfers between devices: 14.9 us -> 10.5 us
  Pallas kernels: 19.8 us -> 22.1 us
  waiting for transfers between devices: 5.9 us -> 4.55 us
    ppermute x4 -> x2, starting transfers between devices: 10.7 us -> 5.43 us  [swap_chips(): return lax.ppermute(value, axis, pairs)]
    all_gather x0 -> x2, blocking collectives: none -> 5.18 us  [exchange(): near = lax.all_gather(to_near, 'rows', axis_index_groups=pairs)]
    ppermute x4 -> x2, waiting for transfers between devices: 4.73 us -> 1.47 us  [swap_chips(): return lax.ppermute(value, axis, pairs)]
    ppermute x5 -> x3, waiting for transfers between devices: 1.17 us -> 3.09 us  [partner(): return lax.ppermute(value, axis, pairs)]
    pallas_call x1, Pallas kernels: 3.14 us -> 4.75 us  [run_second(): pl.pallas_call(functools.partial(second_kernel, plan), out_shape=jax.Shap...]
    ppermute x5 -> x3, starting transfers between devices: 4.2 us -> 5.11 us  [partner(): return lax.ppermute(value, axis, pairs)]
    pallas_call x1, Pallas kernels: 2.87 us -> 3.57 us  [run_first(): pl.pallas_call(functools.partial(first_kernel, plan), out_shape=[pltpu.VM...]
  transfers between devices with their start and end apart: 9 -> 5, of which waited for: 2 -> 2; matrix products, arithmetic and copies ran while one was open for 2% -> 2% of each run, Pallas kernels for 33% -> 32%
where the time goes in v6:
time: 43.7 us; the launch traced here: 43.5 us
  Pallas kernels  22.1 us (51%)
  starting transfers between devices  10.5 us (24%)
  blocking collectives  5.18 us (12%)
  waiting for transfers between devices  4.55 us (10%)
  other arithmetic  0.93 us (2%)
    pallas_call x1, Pallas kernels, make_band(): pl.pallas_call(functools.partial(band_kernel, plan, depth), out_shape=[pl...  8.95 us
    ppermute x2, starting transfers between devices, swap_chips(): return lax.ppermute(value, axis, pairs)  5.43 us
    all_gather x2, blocking collectives, exchange(): near = lax.all_gather(to_near, 'rows', axis_index_groups=pairs)  5.18 us
    ppermute x3, starting transfers between devices, partner(): return lax.ppermute(value, axis, pairs)  5.11 us
    pallas_call x1, Pallas kernels, run_second(): pl.pallas_call(functools.partial(second_kernel, plan), out_shape=jax.Shap...  4.75 us
    pallas_call x1, Pallas kernels, run_first(): pl.pallas_call(functools.partial(first_kernel, plan), out_shape=[pltpu.VM...  3.57 us
    ppermute x3, waiting for transfers between devices, partner(): return lax.ppermute(value, axis, pairs)  3.09 us
    pallas_call x1, Pallas kernels, run_inner(): pl.pallas_call(functools.partial(inner_kernel, plan), out_shape=pltpu.VME...  2.37 us
  transfers between devices with their start and end apart: 5, of which 2 were waited for; matrix products, arithmetic and copies ran while one was open for 2% of the time, Pallas kernels for 32%

profile of v6, /device:TPU:0, one launch (start us, length us, event | category | flops | bytes accessed | tf_op | source)
XLA Modules:
  0.0 43.5 jit_solution(8750201540579177444)
XLA Ops:
  0.0 3.0 %collective-permute-start = (s32[1,8]{1,0:T(1,128)}, s32[1,8]{1,0:T(1,128)S(1)}, u32[]{:S(2)}, u32[]{:S(2)}) collective-permute-start(s32[1,8]{1,0:T(1,128)} %param.7), channel_id=1, source_target_pairs={{0,4},{1,5},{2,6},{3,7},{4,0},{5,1},{6,2},{7,3},{8,12},{9,13},{10,... | collective-permute-start | bytes 104 | tf_op jit(solution)/shard_map/ppermute | solution.py:22
  3.0 1.7 %pack.1 = (f32[128,1536]{1,0:T(8,128)S(1)}, f32[64,1664]{1,0:T(8,128)S(1)}, f32[128,896]{1,0:T(8,128)S(1)}) custom-call(s32[1]{0:T(128)} %bitcast.side, f32[1536,128]{1,0:T(8,128)} %natural.1), custom_call_target="tpu_custom_call" | custom-call | tf_op jit(solution)/shard_map/pack/pallas_call | solution.py:155
  4.7 3.7 %collective-permute-start.1 = (f32[64,1664]{1,0:T(8,128)S(1)}, f32[64,1664]{1,0:T(8,128)S(1)}, u32[]{:S(2)}, u32[]{:S(2)}) collective-permute-start(f32[64,1664]{1,0:T(8,128)S(1)} %get-tuple-element.15), channel_id=1, source_target_pairs={{0,31},{1,2},{2,1},{3,4},{4,3},{5,6},{6,5},{7,8},{8,7},{9,10},{10,... | collective-permute-start | bytes 1277960 | tf_op jit(solution)/shard_map/ppermute | solution.py:28
  8.4 2.6 %all-gather = f32[256,896]{1,0:T(8,128)} all-gather(f32[128,896]{1,0:T(8,128)S(1)} %get-tuple-element.17), channel_id=2, replica_groups={{0,1},{2,3},{4,5},{6,7},{8,9},{10,11},{12,13},{14,15},{16,17},{18,19},{..., dimensions={0}, use_global_device_ids=true | all-gather | bytes 1376256 | tf_op jit(solution)/shard_map/all_gather | solution.py:398
  11.0 0.0 collective-permute-done.asked
  11.0 0.8 %far.1 = f32[128,512]{1,0:T(8,128)S(1)} custom-call(s32[1]{0:T(128)} %bitcast.side, s32[1,8]{1,0:T(1,128)S(1)} %collective-permute-done.asked, f32[128,1536]{1,0:T(8,128)S(1)} %get-tuple-element.16.turned.vectors.own.start), custom_call_target="tpu_custom_call" | custom-call | tf_op jit(solution)/shard_map/far/pallas_call | solution.py:177
  11.7 0.1 collective-permute-start.2
  11.8 0.7 %fusion.5 = s32[24,27]{1,0:T(8,128)S(1)} fusion(s32[24,27]{1,0:T(8,128)} %param.6, s32[]{:T(128)} %select_n.31, s32[]{:T(128)S(6)} %mul.15), kind=kLoop, calls=%fused_computation.13 | loop fusion | flops 23328 | bytes 5192 | tf_op jit(solution)/shard_map/jit(_where)/select_n | solution.py:411
  12.6 0.1 copy.5
  12.6 0.2 select_reduce_fusion
  12.8 8.9 %band.1 = (bf16[12,2432,256]{2,1,0:T(8,128)(2,1)S(1)}, f32[128,1536]{1,0:T(8,128)S(1)}) custom-call(s32[1]{0:T(128)} %bitcast.side, s32[24,60]{1,0:T(8,128)S(1)} %broadcast_add_fusion.inverse, f32[1728,1536]{1,0:T(8,128)} %bitcast.4, f32[128,1536]{1,0:T(8,128)S(1)} %get-tuple-element.16.turned.vectors.own.start), custom_call_target="tpu_custom_call" | custom-call | bytes 21233664 | tf_op jit(solution)/shard_map/band/pallas_call | solution.py:244
  21.8 0.0 collective-permute-done.2.far
  21.8 0.0 collective-permute-done.1.away
  21.8 3.6 %first.1 = (f32[128,1536]{1,0:T(8,128)S(1)}, f32[128,512]{1,0:T(8,128)S(1)}, f32[64,1664]{1,0:T(8,128)S(1)}, f32[128,896]{1,0:T(8,128)S(1)}) custom-call(s32[1]{0:T(128)} %bitcast.side, s32[1,8]{1,0:T(1,128)S(1)} %collective-permute-done.asked, f32[64,1664]{1,0:T(8,128)S(1)} %collective-permute-done.1.away, f32[128,512]{1,0:T(8,128)S(1)} %collective-permute-done.2.far, ...), custom_call_target="tpu_custom_call" | custom-call | flops 2415919104 | tf_op jit(solution)/shard_map/first/pallas_call | solution.py:344
  25.4 2.1 %collective-permute-start.4 = (f32[128,512]{1,0:T(8,128)S(1)}, f32[128,512]{1,0:T(8,128)S(1)}, u32[]{:S(2)}, u32[]{:S(2)}) collective-permute-start(f32[128,512]{1,0:T(8,128)S(1)} %get-tuple-element.22), channel_id=1, source_target_pairs={{0,4},{1,5},{2,6},{3,7},{4,0},{5,1},{6,2},{7,3},{8,12},{9,13},{10,... | collective-permute-start | bytes 786440 | tf_op jit(solution)/shard_map/ppermute | solution.py:22
  27.5 1.7 %collective-permute-start.3 = (f32[64,1664]{1,0:T(8,128)S(1)}, f32[64,1664]{1,0:T(8,128)S(1)}, u32[]{:S(2)}, u32[]{:S(2)}) collective-permute-start(f32[64,1664]{1,0:T(8,128)S(1)} %get-tuple-element.21), channel_id=1, source_target_pairs={{0,31},{1,2},{2,1},{3,4},{4,3},{5,6},{6,5},{7,8},{8,7},{9,10},{10,... | collective-permute-start | bytes 1277960 | tf_op jit(solution)/shard_map/ppermute | solution.py:28
  29.2 2.4 %inner.1 = f32[128,1536]{1,0:T(8,128)S(1)} custom-call(f32[128,1536]{1,0:T(8,128)S(1)} %get-tuple-element.24.vectors.own, bf16[12,2432,256]{2,1,0:T(8,128)(2,1)S(1)} %get-tuple-element.19.band), custom_call_target="tpu_custom_call" | custom-call | flops 2415919104 | tf_op jit(solution)/shard_map/inner/pallas_call | solution.py:270
  31.6 2.6 %all-gather.1 = f32[256,896]{1,0:T(8,128)} all-gather(f32[128,896]{1,0:T(8,128)S(1)} %get-tuple-element.23), channel_id=3, replica_groups={{0,1},{2,3},{4,5},{6,7},{8,9},{10,11},{12,13},{14,15},{16,17},{18,19},{..., dimensions={0}, use_global_device_ids=true | all-gather | bytes 1376256 | tf_op jit(solution)/shard_map/all_gather | solution.py:398
  34.2 3.1 %collective-permute-done.4.far = f32[128,512]{1,0:T(8,128)S(1)} collective-permute-done((f32[128,512]{1,0:T(8,128)S(1)}, f32[128,512]{1,0:T(8,128)S(1)}, u32[]{:S(2)}, u32[]{:S(2)}) %collective-permute-start.4) | collective-permute-done | bytes 262176 | tf_op jit(solution)/shard_map/ppermute | solution.py:22
  37.3 1.5 %collective-permute-done.3.away = f32[64,1664]{1,0:T(8,128)S(1)} collective-permute-done((f32[64,1664]{1,0:T(8,128)S(1)}, f32[64,1664]{1,0:T(8,128)S(1)}, u32[]{:S(2)}, u32[]{:S(2)}) %collective-permute-start.3) | collective-permute-done | bytes 426016 | tf_op jit(solution)/shard_map/ppermute | solution.py:28
  38.7 4.8 %second.1 = f32[1536,128]{1,0:T(8,128)} custom-call(s32[1]{0:T(128)} %bitcast.side, f32[64,1664]{1,0:T(8,128)S(1)} %collective-permute-done.3.away, f32[128,512]{1,0:T(8,128)S(1)} %collective-permute-done.4.far, f32[2,128,896]{2,1,0:T(8,128)} %bitcast.6, bf16[12,2432,256]{2,1,0:T(8,128)(2,1)S(1)} %get-tuple-element.19.band, f32[128,1536]{1,0:T(8,128)S(1)} %inner.1, ...), custom_call_target="tpu_custom_call" | custom-call | flops 2415919104 | tf_op jit(solution)/shard_map/second/pallas_call | solution.py:367
  (2 shorter events, 0.0 us)
Async XLA Ops:
  0.0 11.0 %collective-permute-start = (s32[1,8]{1,0:T(1,128)}, s32[1,8]{1,0:T(1,128)S(1)}, u32[]{:S(2)}, u32[]{:S(2)}) collective-permute-start(s32[1,8]{1,0:T(1,128)} %param.7), channel_id=1, source_target_pairs={{0,4},{1,5},{2,6},{3,7},{4,0},{5,1},{6,2},{7,3},{8,12},{9,13},{10,... | collective-permute-start | bytes 104 | tf_op jit(solution)/shard_map/ppermute | solution.py:22
  4.7 17.1 %collective-permute-start.1 = (f32[64,1664]{1,0:T(8,128)S(1)}, f32[64,1664]{1,0:T(8,128)S(1)}, u32[]{:S(2)}, u32[]{:S(2)}) collective-permute-start(f32[64,1664]{1,0:T(8,128)S(1)} %get-tuple-element.15), channel_id=1, source_target_pairs={{0,31},{1,2},{2,1},{3,4},{4,3},{5,6},{6,5},{7,8},{8,7},{9,10},{10,... | collective-permute-start | bytes 1277960 | tf_op jit(solution)/shard_map/ppermute | solution.py:28
  11.7 10.1 %collective-permute-start.2 = (f32[128,512]{1,0:T(8,128)S(1)}, f32[128,512]{1,0:T(8,128)S(1)}, u32[]{:S(2)}, u32[]{:S(2)}) collective-permute-start(f32[128,512]{1,0:T(8,128)S(1)} %far.1), channel_id=1, source_target_pairs={{0,4},{1,5},{2,6},{3,7},{4,0},{5,1},{6,2},{7,3},{8,12},{9,13},{10,... | collective-permute-start | bytes 786440 | tf_op jit(solution)/shard_map/ppermute | solution.py:22
  25.4 11.9 %collective-permute-start.4 = (f32[128,512]{1,0:T(8,128)S(1)}, f32[128,512]{1,0:T(8,128)S(1)}, u32[]{:S(2)}, u32[]{:S(2)}) collective-permute-start(f32[128,512]{1,0:T(8,128)S(1)} %get-tuple-element.22), channel_id=1, source_target_pairs={{0,4},{1,5},{2,6},{3,7},{4,0},{5,1},{6,2},{7,3},{8,12},{9,13},{10,... | collective-permute-start | bytes 786440 | tf_op jit(solution)/shard_map/ppermute | solution.py:22
  27.5 11.3 %collective-permute-start.3 = (f32[64,1664]{1,0:T(8,128)S(1)}, f32[64,1664]{1,0:T(8,128)S(1)}, u32[]{:S(2)}, u32[]{:S(2)}) collective-permute-start(f32[64,1664]{1,0:T(8,128)S(1)} %get-tuple-element.21), channel_id=1, source_target_pairs={{0,31},{1,2},{2,1},{3,4},{4,3},{5,6},{6,5},{7,8},{8,7},{9,10},{10,... | collective-permute-start | bytes 1277960 | tf_op jit(solution)/shard_map/ppermute | solution.py:28

commit v7 on v5

--- a/solution.py
+++ b/solution.py
@@ -64,6 +64,15 @@
         extra = p + self.near - self.pairs + 1
         return min(p, self.near), self.near + self.far + max(0, extra)
 
+    def spans(self, p):
+        begin, end = self.outer_range(p)
+        row = self.near - begin
+        return {
+            "away": (begin, self.near, 0),
+            "far": (0, self.far, row),
+            "near": (0, end - self.near - self.far, row + self.far),
+        }
+
     def own_range(self, p):
         return max(0, p - self.near), min(self.pairs, p + self.near + 1)
 
@@ -93,28 +102,27 @@
         write(t * tile, value)
 
 
-def write_sends(plan, side, at, value, sends):
+def write_sends(plan, side, at, value, to_away, to_near):
     tile, half, skip = plan.tile, plan.half, plan.rows - plan.edge
-    first, second, to_near = sends
     if at < plan.whole:
-        first[:, at : at + tile] = value[:half]
-        second[:, at : at + tile] = value[half:]
+        to_away[:, at : at + tile] = value[:half]
+        to_away[:, plan.edge + at : plan.edge + at + tile] = value[half:]
     elif at == plan.whole:
         lane = lax.broadcasted_iota(jnp.int32, (half, tile), 1)
         turned = pltpu.roll(value, plan.size, 1)
         even = jnp.where(lane < plan.size, value[:half], turned[half:])
         odd = jnp.where(lane < plan.size, turned[:half], value[half:])
-        first[:, at : at + tile] = jnp.where(side[0] == 0, even, odd)
+        to_away[:, at : at + tile] = jnp.where(side[0] == 0, even, odd)
     if at >= skip:
         to_near[:, at - skip : at - skip + tile] = value
 
 
-def away_tile(plan, side, first, second, t):
-    at = t * plan.tile
-    lanes = slice(at, at + plan.tile)
+def away_tile(plan, side, away, t):
+    at, tile = t * plan.tile, plan.tile
+    packed = away[:, at : at + tile]
     if at < plan.whole:
-        return jnp.concatenate([first[:, lanes], second[:, lanes]], axis=0)
-    packed = first[:, lanes]
+        rest = away[:, plan.edge + at : plan.edge + at + tile]
+        return jnp.concatenate([packed, rest], axis=0)
     turned = pltpu.roll(packed, plan.size, 1)
     even = jnp.concatenate([turned, packed], axis=0)
     odd = jnp.concatenate([packed, turned], axis=0)
@@ -122,8 +130,8 @@
 
 
 def send_shapes(plan):
-    lanes = ((plan.half, plan.edge), (plan.half, plan.whole), (plan.width, plan.edge))
-    return [jax.ShapeDtypeStruct(shape, F32) for shape in lanes]
+    shapes = ((plan.half, plan.edge + plan.whole), (plan.width, plan.edge))
+    return [jax.ShapeDtypeStruct(shape, F32) for shape in shapes]
 
 
 def pack_kernel(plan, chunks, side, natural, turned, *rest):
@@ -146,7 +154,7 @@
         at = pl.multiple_of(plan.mirrored(t, side) * tile, tile)
         value = staged[pl.ds(at, tile), :].T
         turned[:, t * tile : (t + 1) * tile] = value
-        write_sends(plan, side, t * tile, value, sends)
+        write_sends(plan, side, t * tile, value, *sends)
 
 
 def pack(plan, side, natural):
@@ -155,7 +163,7 @@
         functools.partial(pack_kernel, plan, chunks),
         out_shape=[pltpu.VMEM((plan.width, plan.rows), F32)] + send_shapes(plan),
         in_specs=[SMEM, pl.BlockSpec(memory_space=pltpu.HBM)],
-        out_specs=[VMEM] * 4,
+        out_specs=[VMEM] * 3,
         scratch_shapes=[
             pltpu.VMEM((plan.rows, plan.width), F32),
             pltpu.SemaphoreType.DMA((chunks,)),
@@ -201,29 +209,32 @@
 
 def band_kernel(plan, depth, side, inverse, ham_t, vectors, band, inner, staged, halves, sems):
     size, tile = plan.size, plan.tile
+    slots = staged.shape[0]
+    ahead = slots - 1
     lane = lax.broadcasted_iota(jnp.int32, (size, tile), 1)
 
     def fetch(p):
         at = pl.multiple_of(plan.mirrored(p, side) * tile, tile)
-        return pltpu.make_async_copy(
-            ham_t.at[:, pl.ds(at, tile)], staged.at[p, pl.ds(0, depth), :], sems.at[p]
-        )
-
-    for p in range(plan.pairs):
+        held = staged.at[p % slots, pl.ds(0, depth), :]
+        return pltpu.make_async_copy(ham_t.at[:, pl.ds(at, tile)], held, sems.at[p % slots])
+
+    for p in range(min(ahead, plan.pairs)):
         fetch(p).start()
-    for p in range(plan.pairs):
-        staged[p, depth:, :] = jnp.zeros((size, tile), F32)
+    for slot in range(slots):
+        staged[slot, depth:, :] = jnp.zeros((size, tile), F32)
     own_halves(plan, vectors, halves)
 
     for p in range(plan.pairs):
         fetch(p).wait()
+        if p + ahead < plan.pairs:
+            fetch(p + ahead).start()
         row = 2 * plan.mirrored(p, side)
 
         def block(q):
             even = pl.multiple_of(inverse[row, q] * size, size)
             odd = pl.multiple_of(inverse[row + 1, q] * size, size)
-            first = staged[p, pl.ds(even, size), :]
-            second = staged[p, pl.ds(odd, size), :]
+            first = staged[p % slots, pl.ds(even, size), :]
+            second = staged[p % slots, pl.ds(odd, size), :]
             return jnp.where(lane < size, first, second)
 
         if p > 0:
@@ -249,11 +260,11 @@
         in_specs=[SMEM, SMEM, pl.BlockSpec(memory_space=pltpu.HBM), VMEM],
         out_specs=[VMEM, VMEM],
         scratch_shapes=[
-            pltpu.VMEM((plan.pairs, depth + size, tile), F32),
+            pltpu.VMEM((4, depth + size, tile), F32),
             pltpu.VMEM((2 * plan.width, rows), jnp.bfloat16),
-            pltpu.SemaphoreType.DMA((plan.pairs,)),
+            pltpu.SemaphoreType.DMA((4,)),
         ],
-        compiler_params=params(14),
+        compiler_params=params(10),
         cost_estimate=cost(0, 2 * 4 * depth * rows),
         name="band",
     )(side, inverse, pltpu.with_memory_space_constraint(ham_t, pltpu.HBM), vectors)
@@ -278,76 +289,117 @@
     )(vectors, band)
 
 
-def outer_products(plan, side, first, second, far, near, band, halves):
-    tile, width = plan.tile, plan.width
-    tiles = [lambda t=t: away_tile(plan, side, first, second, t) for t in range(plan.near)][::-1]
-    tiles += [lambda t=t: far[:, t * tile : (t + 1) * tile] for t in range(plan.far)]
-    tiles += [lambda t=t: near[:, t * tile : (t + 1) * tile] for t in range(plan.near)][::-1]
-    for t, read in enumerate(tiles):
-        high, low = split(read())
-        halves[:width, t * tile : (t + 1) * tile] = high
-        halves[width:, t * tile : (t + 1) * tile] = low
+class Outer:
+    def __init__(self, plan, side, halves, away=None, far=None, near=None):
+        self.plan, self.halves, self.bases, tile = plan, halves, {}, plan.tile
+        tiles = []
+        if away is not None:
+            self.bases["away"] = len(tiles)
+            tiles += [away_tile(plan, side, away, t) for t in reversed(range(plan.near))]
+        if far is not None:
+            self.bases["far"] = len(tiles)
+            tiles += [far[:, t * tile : (t + 1) * tile] for t in range(plan.far)]
+        if near is not None:
+            self.bases["near"] = len(tiles)
+            order = reversed(range(plan.near))
+            tiles += [near[:, t * tile : (t + 1) * tile] for t in order]
+        for t, value in enumerate(tiles):
+            high, low = split(value)
+            halves[: plan.width, t * tile : (t + 1) * tile] = high
+            halves[plan.width :, t * tile : (t + 1) * tile] = low
+
+    def add(self, p, total, band):
+        plan, runs = self.plan, []
+        for name, (first, last, row) in plan.spans(p).items():
+            if name in self.bases and first < last:
+                first, last = first + self.bases[name], last + self.bases[name]
+                if runs and runs[-1][1] == first and sum(runs[-1][1:]) - runs[-1][0] == row:
+                    runs[-1][1] = last
+                else:
+                    runs.append([first, last, row])
+        for first, last, row in runs:
+            rows = slice(row * plan.tile, (row + last - first) * plan.tile)
+            vectors = self.halves[:, first * plan.tile : last * plan.tile]
+            total += fold(jnp.dot(vectors, band[p, rows, :], preferred_element_type=F32))
+        return total
+
+
+def outer_scratch(plan, tiles):
+    return [pltpu.VMEM((2 * plan.width, tiles * plan.tile), jnp.bfloat16)]
+
+
+def middle_kernel(plan, kind, side, other, near, band, inner, out, halves):
+    outer = Outer(plan, side, halves, near=near, **{kind: other})
     for p in range(plan.pairs):
-        begin, end = (tile * bound for bound in plan.outer_range(p))
-        sums = jnp.dot(
-            halves[:, begin:end], band[p, : end - begin, :], preferred_element_type=F32
-        )
-        yield p * tile, fold(sums)
+        lanes = slice(p * plan.tile, (p + 1) * plan.tile)
+        out[:, lanes] = outer.add(p, inner[:, lanes], band)
+
+
+def run_middle(plan, kind, side, other, near, band, inner):
+    return pl.pallas_call(
+        functools.partial(middle_kernel, plan, kind),
+        out_shape=pltpu.VMEM((plan.width, plan.rows), F32),
+        in_specs=[SMEM] + [VMEM] * 4,
+        out_specs=VMEM,
+        scratch_shapes=outer_scratch(plan, 2 * plan.near),
+        compiler_params=params(8),
+        cost_estimate=cost(8 * plan.width * plan.rows**2, 0),
+        name="middle",
+    )(side, other, near, band, inner)
 
 
 def first_kernel(
-    plan, side, asked, first, second, far, near, band, inner, own, value, to_far, *rest
+    plan, side, asked, far, band, inner, own, value, to_far, to_away, to_near, halves
 ):
-    sends, halves = rest[:-1], rest[-1]
-    tile = plan.tile
-    for at, product in outer_products(plan, side, first, second, far, near, band, halves):
-        lanes = slice(at, at + tile)
-        shifted = product + inner[:, lanes] - CENTER * own[:, lanes]
-        term = shifted * (1.0 / HALF_WIDTH)
+    outer = Outer(plan, side, halves, far=far)
+    for p in range(plan.pairs):
+        lanes = slice(p * plan.tile, (p + 1) * plan.tile)
+        product = outer.add(p, inner[:, lanes] - CENTER * own[:, lanes], band)
+        term = product * (1.0 / HALF_WIDTH)
         value[:, lanes] = term
-        write_sends(plan, side, at, term, sends)
+        write_sends(plan, side, lanes.start, term, to_away, to_near)
 
     def write(at, term):
-        to_far[:, at : at + tile] = term
+        to_far[:, at : at + plan.tile] = term
 
     write_far(plan, side, asked, value, write)
 
 
-def run_first(plan, side, asked, arrived, band, inner, own):
-    far = jax.ShapeDtypeStruct((plan.width, plan.far * plan.tile), F32)
+def run_first(plan, side, asked, far, band, inner, own):
+    shapes = [jax.ShapeDtypeStruct(far.shape, F32)] + send_shapes(plan)
     return pl.pallas_call(
         functools.partial(first_kernel, plan),
-        out_shape=[pltpu.VMEM((plan.width, plan.rows), F32), far] + send_shapes(plan),
-        in_specs=[SMEM] * 2 + [VMEM] * 7,
-        out_specs=[VMEM] * 5,
-        scratch_shapes=[pltpu.VMEM((2 * plan.width, plan.outer * plan.tile), jnp.bfloat16)],
-        compiler_params=params(8),
-        cost_estimate=cost(8 * plan.width * plan.rows**2, 0),
+        out_shape=[pltpu.VMEM((plan.width, plan.rows), F32)] + shapes,
+        in_specs=[SMEM] * 2 + [VMEM] * 4,
+        out_specs=[VMEM] * (1 + len(shapes)),
+        scratch_shapes=outer_scratch(plan, plan.far),
+        compiler_params=params(8),
+        cost_estimate=cost(2 * plan.width * plan.rows**2, 0),
         name="first",
-    )(side, asked, *arrived, band, inner, own)
-
-
-def second_kernel(plan, side, first, second, far, near, band, inner, own, start, out, halves):
-    tile = plan.tile
-    for at, product in outer_products(plan, side, first, second, far, near, band, halves):
-        lanes = slice(at, at + tile)
-        shifted = product + inner[:, lanes] - CENTER * own[:, lanes]
-        term = 2.0 / HALF_WIDTH * shifted - start[:, lanes]
-        place = pl.multiple_of(plan.mirrored(at // tile, side) * tile, tile)
-        out[pl.ds(place, tile), :] = term.T
-
-
-def run_second(plan, side, arrived, band, inner, own, start):
+    )(side, asked, far, band, inner, own)
+
+
+def second_kernel(plan, side, away, band, inner, own, start, out, halves):
+    outer = Outer(plan, side, halves, away=away)
+    for p in range(plan.pairs):
+        lanes = slice(p * plan.tile, (p + 1) * plan.tile)
+        product = outer.add(p, inner[:, lanes] - CENTER * own[:, lanes], band)
+        term = 2.0 / HALF_WIDTH * product - start[:, lanes]
+        place = pl.multiple_of(plan.mirrored(p, side) * plan.tile, plan.tile)
+        out[pl.ds(place, plan.tile), :] = term.T
+
+
+def run_second(plan, side, away, band, inner, own, start):
     return pl.pallas_call(
         functools.partial(second_kernel, plan),
         out_shape=jax.ShapeDtypeStruct((plan.rows, plan.width), F32),
-        in_specs=[SMEM] + [VMEM] * 8,
+        in_specs=[SMEM] + [VMEM] * 5,
         out_specs=VMEM,
-        scratch_shapes=[pltpu.VMEM((2 * plan.width, plan.outer * plan.tile), jnp.bfloat16)],
-        compiler_params=params(8),
-        cost_estimate=cost(8 * plan.width * plan.rows**2, 0),
+        scratch_shapes=outer_scratch(plan, plan.near),
+        compiler_params=params(8),
+        cost_estimate=cost(2 * plan.width * plan.rows**2, 0),
         name="second",
-    )(side, *arrived, band, inner, own, start)
+    )(side, away, band, inner, own, start)
 
 
 def after(value, *others):
@@ -366,29 +418,31 @@
     side = (lax.axis_index("rows") % 2).astype(jnp.int32).reshape(1)
 
     def exchange(listed, sends):
+        to_away, to_near = sends
         far = partner(listed, "rows", swap_level)
-        first, second = (swap_chips(value, "rows") for value in sends[:2])
-        return first, second, far, partner(sends[2], "rows", 0)
+        return swap_chips(to_away, "rows"), far, partner(to_near, "rows", 0)
 
     asked = partner(far_list, "rows", swap_level)
     start, *sends = pack(plan, side, subspace)
     listed = gather_far(plan, side, asked, start)
-    arrived = exchange(listed, sends)
+    away, far, near = exchange(listed, sends)
 
     block_cols = after(block_cols, listed)
-    near, far_slots = 2 * plan.near, 2 * plan.far
-    shift = (block_cols - first_row + near + block_total) % block_total
-    last = block_rows + 2 * near - 2
-    shift = shift + side[0] * (last - 4 * (shift // 2))
+    edge, far_slots = 2 * plan.near, 2 * plan.far
+    shift = block_cols - first_row + edge
+    shift = jnp.where(shift < 0, shift + block_total, shift)
+    shift = jnp.where(shift >= block_total, shift - block_total, shift)
+    last = block_rows + 2 * edge - 2
+    shift = shift + side[0] * (last - 4 * (shift >> 1))
     places = jnp.where(
         block_cols >= block_total,
-        near + block_cols - block_total,
+        edge + block_cols - block_total,
         jnp.where(
-            shift < near,
+            shift < edge,
             shift,
             jnp.where(
-                shift < near + block_rows,
-                shift - near + 2 * plan.outer,
+                shift < edge + block_rows,
+                shift - edge + 2 * plan.outer,
                 shift - block_rows + far_slots,
             ),
         ),
@@ -400,10 +454,12 @@
 
     band, inner = make_band(plan, side, inverse, hamiltonian.T, start)
 
-    value, listed, *sends = run_first(plan, side, asked, arrived, band, inner, start)
-    arrived = exchange(listed, sends)
+    inner = run_middle(plan, "away", side, away, near, band, inner)
+    value, listed, *sends = run_first(plan, side, asked, far, band, inner, start)
+    away, far, near = exchange(listed, sends)
     inner = run_inner(plan, value, band)
-    return run_second(plan, side, arrived, band, inner, value, start)
+    inner = run_middle(plan, "far", side, far, near, band, inner)
+    return run_second(plan, side, away, band, inner, value, start)
 
 
 def solution(mesh):

time: 42 us -> 40.5 us (0.964)
  starting transfers between devices: 14.9 us -> 10.6 us
  waiting for transfers between devices: 5.9 us -> 7.4 us
  Pallas kernels: 19.8 us -> 21.1 us
    ppermute x5, waiting for transfers between devices: 1.17 us -> 7.39 us  [partner(): return lax.ppermute(value, axis, pairs)]
    ppermute x4 -> x2, starting transfers between devices: 10.7 us -> 5.53 us  [swap_chips(): return lax.ppermute(value, axis, pairs)]
    ppermute x4 -> x2, waiting for transfers between devices: 4.73 us -> 0.01 us  [swap_chips(): return lax.ppermute(value, axis, pairs)]
    pallas_call x0 -> x2, Pallas kernels: none -> 2.93 us  [run_middle(): pl.pallas_call(functools.partial(middle_kernel, plan, kind), out_shape=pl...]
    pallas_call x1, Pallas kernels: 3.14 us -> 1.84 us  [run_second(): pl.pallas_call(functools.partial(second_kernel, plan), out_shape=jax.Shap...]
    pallas_call x1, Pallas kernels: 2.87 us -> 1.81 us  [run_first(): pl.pallas_call(functools.partial(first_kernel, plan), out_shape=[pltpu.VM...]
    ppermute x5, starting transfers between devices: 4.2 us -> 5.09 us  [partner(): return lax.ppermute(value, axis, pairs)]
    pallas_call x1, Pallas kernels: 8.95 us -> 9.72 us  [make_band(): pl.pallas_call(functools.partial(band_kernel, plan, depth), out_shape=[pl...]
  transfers between devices with their start and end apart: 9 -> 7, of which waited for: 2 -> 2; matrix products, arithmetic and copies ran while one was open for 2% -> 2% of each run, Pallas kernels for 33% -> 43%
where the time goes in v7:
time: 40.5 us; the launch traced here: 40.2 us
  Pallas kernels  21.1 us (52%)
  starting transfers between devices  10.6 us (26%)
  waiting for transfers between devices  7.4 us (18%)
  other arithmetic  0.92 us (2%)
    pallas_call x1, Pallas kernels, make_band(): pl.pallas_call(functools.partial(band_kernel, plan, depth), out_shape=[pl...  9.72 us
    ppermute x5, waiting for transfers between devices, partner(): return lax.ppermute(value, axis, pairs)  7.39 us
    ppermute x2, starting transfers between devices, swap_chips(): return lax.ppermute(value, axis, pairs)  5.53 us
    ppermute x5, starting transfers between devices, partner(): return lax.ppermute(value, axis, pairs)  5.09 us
    pallas_call x2, Pallas kernels, run_middle(): pl.pallas_call(functools.partial(middle_kernel, plan, kind), out_shape=pl...  2.93 us
    pallas_call x1, Pallas kernels, run_inner(): pl.pallas_call(functools.partial(inner_kernel, plan), out_shape=pltpu.VME...  2.34 us
    pallas_call x1, Pallas kernels, run_second(): pl.pallas_call(functools.partial(second_kernel, plan), out_shape=jax.Shap...  1.84 us
    pallas_call x1, Pallas kernels, run_first(): pl.pallas_call(functools.partial(first_kernel, plan), out_shape=[pltpu.VM...  1.81 us
  transfers between devices with their start and end apart: 7, of which 2 were waited for; matrix products, arithmetic and copies ran while one was open for 2% of the time, Pallas kernels for 43%

profile of v7, /device:TPU:0, one launch (start us, length us, event | category | flops | bytes accessed | tf_op | source)
XLA Modules:
  0.0 40.2 jit_solution(7546567808826142671)
XLA Ops:
  0.0 3.0 %collective-permute-start = (s32[1,8]{1,0:T(1,128)}, s32[1,8]{1,0:T(1,128)S(1)}, u32[]{:S(2)}, u32[]{:S(2)}) collective-permute-start(s32[1,8]{1,0:T(1,128)} %param.7), channel_id=1, source_target_pairs={{0,4},{1,5},{2,6},{3,7},{4,0},{5,1},{6,2},{7,3},{8,12},{9,13},{10,... | collective-permute-start | bytes 104 | tf_op jit(solution)/shard_map/ppermute | solution.py:21
  3.0 1.7 %pack.1 = (f32[128,1536]{1,0:T(8,128)S(1)}, f32[64,1664]{1,0:T(8,128)S(1)}, f32[128,896]{1,0:T(8,128)S(1)}) custom-call(s32[1]{0:T(128)} %bitcast.side, f32[1536,128]{1,0:T(8,128)} %natural.1), custom_call_target="tpu_custom_call" | custom-call | tf_op jit(solution)/shard_map/pack/pallas_call | solution.py:162
  4.7 3.7 %collective-permute-start.2 = (f32[64,1664]{1,0:T(8,128)S(1)}, f32[64,1664]{1,0:T(8,128)S(1)}, u32[]{:S(2)}, u32[]{:S(2)}) collective-permute-start(f32[64,1664]{1,0:T(8,128)S(1)} %get-tuple-element.18), channel_id=1, source_target_pairs={{0,31},{1,2},{2,1},{3,4},{4,3},{5,6},{6,5},{7,8},{8,7},{9,10},{10,... | collective-permute-start | bytes 1277960 | tf_op jit(solution)/shard_map/ppermute | solution.py:27
  8.4 0.0 collective-permute-start.3
  8.4 0.0 collective-permute-done.asked
  8.4 0.8 %far.1 = f32[128,512]{1,0:T(8,128)S(1)} custom-call(s32[1]{0:T(128)} %bitcast.side, s32[1,8]{1,0:T(1,128)S(1)} %collective-permute-done.asked, f32[128,1536]{1,0:T(8,128)S(1)} %get-tuple-element.15.turned.vectors.own.start), custom_call_target="tpu_custom_call" | custom-call | tf_op jit(solution)/shard_map/far/pallas_call | solution.py:184
  9.2 0.1 collective-permute-start.1
  9.2 0.7 %fusion = s32[24,27]{1,0:T(8,128)S(1)} fusion(s32[24,27]{1,0:T(8,128)} %param.6, s32[]{:T(128)} %select_n.27, s32[]{:T(128)S(6)} %mul.15), kind=kLoop, calls=%fused_computation.5 | loop fusion | flops 14256 | bytes 5192 | tf_op jit(solution)/shard_map/jit(_where)/select_n | solution.py:437
  10.0 0.1 copy.5
  10.1 0.2 select_reduce_fusion
  10.3 9.7 %band.1 = (bf16[12,2432,256]{2,1,0:T(8,128)(2,1)S(1)}, f32[128,1536]{1,0:T(8,128)S(1)}) custom-call(s32[1]{0:T(128)} %bitcast.side, s32[24,60]{1,0:T(8,128)S(1)} %broadcast_add_fusion.inverse, f32[1728,1536]{1,0:T(8,128)} %bitcast.2, f32[128,1536]{1,0:T(8,128)S(1)} %get-tuple-element.15.turned.vectors.own.start), custom_call_target="tpu_custom_call" | custom-call | bytes 21233664 | tf_op jit(solution)/shard_map/band/pallas_call | solution.py:254
  20.0 0.0 collective-permute-done.2.other
  20.0 0.0 collective-permute-done.3.near
  20.0 1.3 %middle.2.inner = f32[128,1536]{1,0:T(8,128)S(1)} custom-call(s32[1]{0:T(128)} %bitcast.side, f32[64,1664]{1,0:T(8,128)S(1)} %collective-permute-done.2.other, f32[128,896]{1,0:T(8,128)S(1)} %collective-permute-done.3.near, bf16[12,2432,256]{2,1,0:T(8,128)(2,1)S(1)} %get-tuple-element.17.band, f32[128,1536]{1,0:T(8,128)S(1)} %get-tuple-element.20.inner), custom_call_target="tpu_custom_call" | custom-call | flops 2415919104 | tf_op jit(solution)/shard_map/middle/pallas_call | solution.py:339
  21.4 0.3 collective-permute-done.1.far
  21.6 1.8 %first.1 = (f32[128,1536]{1,0:T(8,128)S(1)}, f32[128,512]{1,0:T(8,128)S(1)}, f32[64,1664]{1,0:T(8,128)S(1)}, f32[128,896]{1,0:T(8,128)S(1)}) custom-call(s32[1]{0:T(128)} %bitcast.side, s32[1,8]{1,0:T(1,128)S(1)} %collective-permute-done.asked, f32[128,512]{1,0:T(8,128)S(1)} %collective-permute-done.1.far, ...), custom_call_target="tpu_custom_call" | custom-call | flops 603979776 | tf_op jit(solution)/shard_map/first/pallas_call | solution.py:370
  23.4 0.3 collective-permute-start.6
  23.8 1.7 %collective-permute-start.5 = (f32[128,512]{1,0:T(8,128)S(1)}, f32[128,512]{1,0:T(8,128)S(1)}, u32[]{:S(2)}, u32[]{:S(2)}) collective-permute-start(f32[128,512]{1,0:T(8,128)S(1)} %get-tuple-element.22), channel_id=1, source_target_pairs={{0,4},{1,5},{2,6},{3,7},{4,0},{5,1},{6,2},{7,3},{8,12},{9,13},{10,... | collective-permute-start | bytes 786440 | tf_op jit(solution)/shard_map/ppermute | solution.py:21
  25.5 1.8 %collective-permute-start.4 = (f32[64,1664]{1,0:T(8,128)S(1)}, f32[64,1664]{1,0:T(8,128)S(1)}, u32[]{:S(2)}, u32[]{:S(2)}) collective-permute-start(f32[64,1664]{1,0:T(8,128)S(1)} %get-tuple-element.21), channel_id=1, source_target_pairs={{0,31},{1,2},{2,1},{3,4},{4,3},{5,6},{6,5},{7,8},{8,7},{9,10},{10,... | collective-permute-start | bytes 1277960 | tf_op jit(solution)/shard_map/ppermute | solution.py:27
  27.3 2.3 %inner.1 = f32[128,1536]{1,0:T(8,128)S(1)} custom-call(f32[128,1536]{1,0:T(8,128)S(1)} %get-tuple-element.24.vectors.own, bf16[12,2432,256]{2,1,0:T(8,128)(2,1)S(1)} %get-tuple-element.17.band), custom_call_target="tpu_custom_call" | custom-call | flops 2415919104 | tf_op jit(solution)/shard_map/inner/pallas_call | solution.py:280
  29.7 7.1 %collective-permute-done.5.other = f32[128,512]{1,0:T(8,128)S(1)} collective-permute-done((f32[128,512]{1,0:T(8,128)S(1)}, f32[128,512]{1,0:T(8,128)S(1)}, u32[]{:S(2)}, u32[]{:S(2)}) %collective-permute-start.5) | collective-permute-done | bytes 262176 | tf_op jit(solution)/shard_map/ppermute | solution.py:21
  36.8 0.0 collective-permute-done.6.near
  36.8 1.6 %middle.3.inner = f32[128,1536]{1,0:T(8,128)S(1)} custom-call(s32[1]{0:T(128)} %bitcast.side, f32[128,512]{1,0:T(8,128)S(1)} %collective-permute-done.5.other, f32[128,896]{1,0:T(8,128)S(1)} %collective-permute-done.6.near, bf16[12,2432,256]{2,1,0:T(8,128)(2,1)S(1)} %get-tuple-element.17.band, f32[128,1536]{1,0:T(8,128)S(1)} %inner.1), custom_call_target="tpu_custom_call" | custom-call | flops 2415919104 | tf_op jit(solution)/shard_map/middle/pallas_call | solution.py:339
  38.4 0.0 collective-permute-done.4.away
  38.4 1.8 %second.1 = f32[1536,128]{1,0:T(8,128)} custom-call(s32[1]{0:T(128)} %bitcast.side, f32[64,1664]{1,0:T(8,128)S(1)} %collective-permute-done.4.away, bf16[12,2432,256]{2,1,0:T(8,128)(2,1)S(1)} %get-tuple-element.17.band, f32[128,1536]{1,0:T(8,128)S(1)} %middle.3.inner, f32[128,1536]{1,0:T(8,128)S(1)} %get-tuple-element.24.vectors.own, ...), custom_call_target="tpu_custom_call" | custom-call | flops 603979776 | tf_op jit(solution)/shard_map/second/pallas_call | solution.py:393
  (2 shorter events, 0.0 us)
Async XLA Ops:
  0.0 8.4 %collective-permute-start = (s32[1,8]{1,0:T(1,128)}, s32[1,8]{1,0:T(1,128)S(1)}, u32[]{:S(2)}, u32[]{:S(2)}) collective-permute-start(s32[1,8]{1,0:T(1,128)} %param.7), channel_id=1, source_target_pairs={{0,4},{1,5},{2,6},{3,7},{4,0},{5,1},{6,2},{7,3},{8,12},{9,13},{10,... | collective-permute-start | bytes 104 | tf_op jit(solution)/shard_map/ppermute | solution.py:21
  4.7 15.3 %collective-permute-start.2 = (f32[64,1664]{1,0:T(8,128)S(1)}, f32[64,1664]{1,0:T(8,128)S(1)}, u32[]{:S(2)}, u32[]{:S(2)}) collective-permute-start(f32[64,1664]{1,0:T(8,128)S(1)} %get-tuple-element.18), channel_id=1, source_target_pairs={{0,31},{1,2},{2,1},{3,4},{4,3},{5,6},{6,5},{7,8},{8,7},{9,10},{10,... | collective-permute-start | bytes 1277960 | tf_op jit(solution)/shard_map/ppermute | solution.py:27
  8.4 11.6 %collective-permute-start.3 = (f32[128,896]{1,0:T(8,128)S(1)}, f32[128,896]{1,0:T(8,128)S(1)}, u32[]{:S(2)}, u32[]{:S(2)}) collective-permute-start(f32[128,896]{1,0:T(8,128)S(1)} %get-tuple-element.19), channel_id=1, source_target_pairs={{0,1},{1,0},{2,3},{3,2},{4,5},{5,4},{6,7},{7,6},{8,9},{9,8},{10,11... | collective-permute-start | bytes 1376264 | tf_op jit(solution)/shard_map/ppermute | solution.py:21
  9.2 12.5 %collective-permute-start.1 = (f32[128,512]{1,0:T(8,128)S(1)}, f32[128,512]{1,0:T(8,128)S(1)}, u32[]{:S(2)}, u32[]{:S(2)}) collective-permute-start(f32[128,512]{1,0:T(8,128)S(1)} %far.1), channel_id=1, source_target_pairs={{0,4},{1,5},{2,6},{3,7},{4,0},{5,1},{6,2},{7,3},{8,12},{9,13},{10,... | collective-permute-start | bytes 786440 | tf_op jit(solution)/shard_map/ppermute | solution.py:21
  23.4 13.4 %collective-permute-start.6 = (f32[128,896]{1,0:T(8,128)S(1)}, f32[128,896]{1,0:T(8,128)S(1)}, u32[]{:S(2)}, u32[]{:S(2)}) collective-permute-start(f32[128,896]{1,0:T(8,128)S(1)} %get-tuple-element.23), channel_id=1, source_target_pairs={{0,1},{1,0},{2,3},{3,2},{4,5},{5,4},{6,7},{7,6},{8,9},{9,8},{10,11... | collective-permute-start | bytes 1376264 | tf_op jit(solution)/shard_map/ppermute | solution.py:21
  23.8 13.0 %collective-permute-start.5 = (f32[128,512]{1,0:T(8,128)S(1)}, f32[128,512]{1,0:T(8,128)S(1)}, u32[]{:S(2)}, u32[]{:S(2)}) collective-permute-start(f32[128,512]{1,0:T(8,128)S(1)} %get-tuple-element.22), channel_id=1, source_target_pairs={{0,4},{1,5},{2,6},{3,7},{4,0},{5,1},{6,2},{7,3},{8,12},{9,13},{10,... | collective-permute-start | bytes 786440 | tf_op jit(solution)/shard_map/ppermute | solution.py:21
  25.5 12.9 %collective-permute-start.4 = (f32[64,1664]{1,0:T(8,128)S(1)}, f32[64,1664]{1,0:T(8,128)S(1)}, u32[]{:S(2)}, u32[]{:S(2)}) collective-permute-start(f32[64,1664]{1,0:T(8,128)S(1)} %get-tuple-element.21), channel_id=1, source_target_pairs={{0,31},{1,2},{2,1},{3,4},{4,3},{5,6},{6,5},{7,8},{8,7},{9,10},{10,... | collective-permute-start | bytes 1277960 | tf_op jit(solution)/shard_map/ppermute | solution.py:27

commit v8 on v7

--- a/solution.py
+++ b/solution.py
@@ -198,13 +198,11 @@
         halves[plan.width :, at : at + plan.tile] = low
 
 
-def own_product(plan, p, halves, band, inner):
+def own_product(plan, p, halves, band):
     begin, end = (plan.tile * bound for bound in plan.own_range(p))
     _, (_, row, rows) = plan.runs(p)
-    sums = jnp.dot(
-        halves[:, begin:end], band[p, row : row + rows, :], preferred_element_type=F32
-    )
-    inner[:, p * plan.tile : (p + 1) * plan.tile] = fold(sums)
+    vectors = halves[:, begin:end]
+    return fold(jnp.dot(vectors, band[p, row : row + rows, :], preferred_element_type=F32))
 
 
 def band_kernel(plan, depth, side, inverse, ham_t, vectors, band, inner, staged, halves, sems):
@@ -217,6 +215,10 @@
         at = pl.multiple_of(plan.mirrored(p, side) * tile, tile)
         held = staged.at[p % slots, pl.ds(0, depth), :]
         return pltpu.make_async_copy(ham_t.at[:, pl.ds(at, tile)], held, sems.at[p % slots])
+
+    def store(p, at, high, low):
+        band[p, at : at + size, :tile] = high
+        band[p, at : at + size, tile:] = low
 
     for p in range(min(ahead, plan.pairs)):
         fetch(p).start()
@@ -237,15 +239,20 @@
             second = staged[p % slots, pl.ds(odd, size), :]
             return jnp.where(lane < size, first, second)
 
+        ready = None if p == 0 else own_product(plan, p - 1, halves, band)
+        places = [(place + q, at + q * size) for place, at, rows in plan.runs(p) for q in range(rows // size)]
+        waiting = []
+        for begin in range(0, len(places), 2):
+            batch = [(at, *split(block(q))) for q, at in places[begin : begin + 2]]
+            for entry in waiting:
+                store(p, *entry)
+            waiting = batch
+        for entry in waiting:
+            store(p, *entry)
         if p > 0:
-            own_product(plan, p - 1, halves, band, inner)
-        for place, at, rows in plan.runs(p):
-            for q in range(rows // size):
-                high, low = split(block(place + q))
-                lines = slice(at + q * size, at + (q + 1) * size)
-                band[p, lines, :tile] = high
-                band[p, lines, tile:] = low
-    own_product(plan, plan.pairs - 1, halves, band, inner)
+            inner[:, (p - 1) * tile : p * tile] = ready
+    p = plan.pairs - 1
+    inner[:, p * tile : (p + 1) * tile] = own_product(plan, p, halves, band)
 
 
 def make_band(plan, side, inverse, ham_t, vectors):
@@ -270,91 +277,103 @@
     )(side, inverse, pltpu.with_memory_space_constraint(ham_t, pltpu.HBM), vectors)
 
 
-def inner_kernel(plan, vectors, band, inner, halves):
+def put_halves(plan, halves, tiles):
+    for t, value in enumerate(tiles):
+        high, low = split(value)
+        halves[: plan.width, t * plan.tile : (t + 1) * plan.tile] = high
+        halves[plan.width :, t * plan.tile : (t + 1) * plan.tile] = low
+
+
+def message_product(plan, name, p, halves, band):
+    first, last, row = plan.spans(p)[name]
+    if first == last:
+        return 0.0
+    rows = slice(row * plan.tile, (row + last - first) * plan.tile)
+    vectors = halves[:, first * plan.tile : last * plan.tile]
+    return fold(jnp.dot(vectors, band[p, rows, :], preferred_element_type=F32))
+
+
+def halves_scratch(plan, tiles):
+    return pltpu.VMEM((2 * plan.width, tiles * plan.tile), jnp.bfloat16)
+
+
+def near_tiles(plan, near):
+    tile = plan.tile
+    return [near[:, t * tile : (t + 1) * tile] for t in reversed(range(plan.near))]
+
+
+def away_tiles(plan, side, away):
+    return [away_tile(plan, side, away, t) for t in reversed(range(plan.near))]
+
+
+def near_kernel(plan, near, band, inner, out, halves):
+    put_halves(plan, halves, near_tiles(plan, near))
+    for p in range(plan.pairs):
+        lanes = slice(p * plan.tile, (p + 1) * plan.tile)
+        out[:, lanes] = inner[:, lanes] + message_product(plan, "near", p, halves, band)
+
+
+def add_near(plan, near, band, inner):
+    return pl.pallas_call(
+        functools.partial(near_kernel, plan),
+        out_shape=pltpu.VMEM((plan.width, plan.rows), F32),
+        in_specs=[VMEM] * 3,
+        out_specs=VMEM,
+        scratch_shapes=[halves_scratch(plan, plan.near)],
+        compiler_params=params(8),
+        cost_estimate=cost(2 * plan.width * plan.rows**2, 0),
+        name="near",
+    )(near, band, inner)
+
+
+def inner_kernel(plan, vectors, near, band, out, halves, near_halves):
     own_halves(plan, vectors, halves)
+    put_halves(plan, near_halves, near_tiles(plan, near))
     for p in range(plan.pairs):
-        own_product(plan, p, halves, band, inner)
-
-
-def run_inner(plan, vectors, band):
+        total = own_product(plan, p, halves, band)
+        total += message_product(plan, "near", p, near_halves, band)
+        out[:, p * plan.tile : (p + 1) * plan.tile] = total
+
+
+def run_inner(plan, vectors, near, band):
     return pl.pallas_call(
         functools.partial(inner_kernel, plan),
         out_shape=pltpu.VMEM((plan.width, plan.rows), F32),
-        in_specs=[VMEM] * 2,
+        in_specs=[VMEM] * 3,
         out_specs=VMEM,
-        scratch_shapes=[pltpu.VMEM((2 * plan.width, plan.rows), jnp.bfloat16)],
+        scratch_shapes=[halves_scratch(plan, plan.pairs), halves_scratch(plan, plan.near)],
         compiler_params=params(8),
         cost_estimate=cost(8 * plan.width * plan.rows**2, 0),
         name="inner",
-    )(vectors, band)
-
-
-class Outer:
-    def __init__(self, plan, side, halves, away=None, far=None, near=None):
-        self.plan, self.halves, self.bases, tile = plan, halves, {}, plan.tile
-        tiles = []
-        if away is not None:
-            self.bases["away"] = len(tiles)
-            tiles += [away_tile(plan, side, away, t) for t in reversed(range(plan.near))]
-        if far is not None:
-            self.bases["far"] = len(tiles)
-            tiles += [far[:, t * tile : (t + 1) * tile] for t in range(plan.far)]
-        if near is not None:
-            self.bases["near"] = len(tiles)
-            order = reversed(range(plan.near))
-            tiles += [near[:, t * tile : (t + 1) * tile] for t in order]
-        for t, value in enumerate(tiles):
-            high, low = split(value)
-            halves[: plan.width, t * tile : (t + 1) * tile] = high
-            halves[plan.width :, t * tile : (t + 1) * tile] = low
-
-    def add(self, p, total, band):
-        plan, runs = self.plan, []
-        for name, (first, last, row) in plan.spans(p).items():
-            if name in self.bases and first < last:
-                first, last = first + self.bases[name], last + self.bases[name]
-                if runs and runs[-1][1] == first and sum(runs[-1][1:]) - runs[-1][0] == row:
-                    runs[-1][1] = last
-                else:
-                    runs.append([first, last, row])
-        for first, last, row in runs:
-            rows = slice(row * plan.tile, (row + last - first) * plan.tile)
-            vectors = self.halves[:, first * plan.tile : last * plan.tile]
-            total += fold(jnp.dot(vectors, band[p, rows, :], preferred_element_type=F32))
-        return total
-
-
-def outer_scratch(plan, tiles):
-    return [pltpu.VMEM((2 * plan.width, tiles * plan.tile), jnp.bfloat16)]
-
-
-def middle_kernel(plan, kind, side, other, near, band, inner, out, halves):
-    outer = Outer(plan, side, halves, near=near, **{kind: other})
+    )(vectors, near, band)
+
+
+def far_split_kernel(plan, far, halves):
+    tile = plan.tile
+    put_halves(plan, halves, [far[:, t * tile : (t + 1) * tile] for t in range(plan.far)])
+
+
+def split_far(plan, far):
+    return pl.pallas_call(
+        functools.partial(far_split_kernel, plan),
+        out_shape=halves_scratch(plan, plan.far),
+        in_specs=[VMEM],
+        out_specs=VMEM,
+        compiler_params=params(8),
+        cost_estimate=cost(16 * plan.width * plan.rows**2, 0),
+        name="split",
+    )(far)
+
+
+def first_kernel(
+    plan, side, asked, away, far, band, inner, own, value, to_far, to_away, to_near, halves
+):
+    put_halves(plan, halves, away_tiles(plan, side, away))
     for p in range(plan.pairs):
         lanes = slice(p * plan.tile, (p + 1) * plan.tile)
-        out[:, lanes] = outer.add(p, inner[:, lanes], band)
-
-
-def run_middle(plan, kind, side, other, near, band, inner):
-    return pl.pallas_call(
-        functools.partial(middle_kernel, plan, kind),
-        out_shape=pltpu.VMEM((plan.width, plan.rows), F32),
-        in_specs=[SMEM] + [VMEM] * 4,
-        out_specs=VMEM,
-        scratch_shapes=outer_scratch(plan, 2 * plan.near),
-        compiler_params=params(8),
-        cost_estimate=cost(8 * plan.width * plan.rows**2, 0),
-        name="middle",
-    )(side, other, near, band, inner)
-
-
-def first_kernel(
-    plan, side, asked, far, band, inner, own, value, to_far, to_away, to_near, halves
-):
-    outer = Outer(plan, side, halves, far=far)
-    for p in range(plan.pairs):
-        lanes = slice(p * plan.tile, (p + 1) * plan.tile)
-        product = outer.add(p, inner[:, lanes] - CENTER * own[:, lanes], band)
+        product = inner[:, lanes] - CENTER * own[:, lanes]
+        product += message_product(plan, "far", p, far, band)
+        product += message_product(plan, "away", p, halves, band)
         term = product * (1.0 / HALF_WIDTH)
         value[:, lanes] = term
         write_sends(plan, side, lanes.start, term, to_away, to_near)
@@ -365,41 +384,44 @@
     write_far(plan, side, asked, value, write)
 
 
-def run_first(plan, side, asked, far, band, inner, own):
-    shapes = [jax.ShapeDtypeStruct(far.shape, F32)] + send_shapes(plan)
+def run_first(plan, side, asked, away, far, band, inner, own):
+    to_far = jax.ShapeDtypeStruct((plan.width, plan.far * plan.tile), F32)
+    shapes = [to_far] + send_shapes(plan)
     return pl.pallas_call(
         functools.partial(first_kernel, plan),
         out_shape=[pltpu.VMEM((plan.width, plan.rows), F32)] + shapes,
-        in_specs=[SMEM] * 2 + [VMEM] * 4,
+        in_specs=[SMEM] * 2 + [VMEM] * 5,
         out_specs=[VMEM] * (1 + len(shapes)),
-        scratch_shapes=outer_scratch(plan, plan.far),
+        scratch_shapes=[halves_scratch(plan, plan.near)],
         compiler_params=params(8),
         cost_estimate=cost(2 * plan.width * plan.rows**2, 0),
         name="first",
-    )(side, asked, far, band, inner, own)
-
-
-def second_kernel(plan, side, away, band, inner, own, start, out, halves):
-    outer = Outer(plan, side, halves, away=away)
+    )(side, asked, away, far, band, inner, own)
+
+
+def second_kernel(plan, side, away, far, band, inner, own, start, out, halves):
+    put_halves(plan, halves, away_tiles(plan, side, away))
     for p in range(plan.pairs):
         lanes = slice(p * plan.tile, (p + 1) * plan.tile)
-        product = outer.add(p, inner[:, lanes] - CENTER * own[:, lanes], band)
+        product = inner[:, lanes] - CENTER * own[:, lanes]
+        product += message_product(plan, "far", p, far, band)
+        product += message_product(plan, "away", p, halves, band)
         term = 2.0 / HALF_WIDTH * product - start[:, lanes]
         place = pl.multiple_of(plan.mirrored(p, side) * plan.tile, plan.tile)
         out[pl.ds(place, plan.tile), :] = term.T
 
 
-def run_second(plan, side, away, band, inner, own, start):
+def run_second(plan, side, away, far, band, inner, own, start):
     return pl.pallas_call(
         functools.partial(second_kernel, plan),
         out_shape=jax.ShapeDtypeStruct((plan.rows, plan.width), F32),
-        in_specs=[SMEM] + [VMEM] * 5,
+        in_specs=[SMEM] + [VMEM] * 6,
         out_specs=VMEM,
-        scratch_shapes=outer_scratch(plan, plan.near),
+        scratch_shapes=[halves_scratch(plan, plan.near)],
         compiler_params=params(8),
         cost_estimate=cost(2 * plan.width * plan.rows**2, 0),
         name="second",
-    )(side, away, band, inner, own, start)
+    )(side, away, far, band, inner, own, start)
 
 
 def after(value, *others):
@@ -425,7 +447,8 @@
     asked = partner(far_list, "rows", swap_level)
     start, *sends = pack(plan, side, subspace)
     listed = gather_far(plan, side, asked, start)
-    away, far, near = exchange(listed, sends)
+    to_away, to_near, _ = lax.optimization_barrier((*sends, listed))
+    away, far, near = exchange(listed, (to_away, to_near))
 
     block_cols = after(block_cols, listed)
     edge, far_slots = 2 * plan.near, 2 * plan.far
@@ -454,12 +477,14 @@
 
     band, inner = make_band(plan, side, inverse, hamiltonian.T, start)
 
-    inner = run_middle(plan, "away", side, away, near, band, inner)
-    value, listed, *sends = run_first(plan, side, asked, far, band, inner, start)
+    inner = add_near(plan, near, band, inner)
+    value, listed, *sends = run_first(
+        plan, side, asked, away, split_far(plan, after(far, inner)), band, inner, start
+    )
     away, far, near = exchange(listed, sends)
-    inner = run_inner(plan, value, band)
-    inner = run_middle(plan, "far", side, far, near, band, inner)
-    return run_second(plan, side, away, band, inner, value, start)
+    inner = run_inner(plan, value, near, band)
+    far = split_far(plan, after(far, inner))
+    return run_second(plan, side, away, far, band, inner, value, start)
 
 
 def solution(mesh):

time: 40.5 us -> 42.6 us (1.052)
  starting transfers between devices: 10.6 us -> 12 us
  waiting for transfers between devices: 7.4 us -> 8.01 us
    pallas_call x2 -> x3, Pallas kernels: 2.93 us -> 0.86 us  [the longest x1 0.77 us: add_near(): pl.pallas_call(functools.partial(near_kernel, plan), out_shape=pltpu.VMEM...]
    ppermute x2, starting transfers between devices: 5.53 us -> 6.85 us  [swap_chips(): return lax.ppermute(value, axis, pairs)]
    pallas_call x1, Pallas kernels: 1.84 us -> 2.65 us  [run_second(): pl.pallas_call(functools.partial(second_kernel, plan), out_shape=jax.Shap...]
    ppermute x5, waiting for transfers between devices: 7.39 us -> 8.01 us  [partner(): return lax.ppermute(value, axis, pairs)]
    pallas_call x1, Pallas kernels: 2.34 us -> 2.94 us  [run_inner(): pl.pallas_call(functools.partial(inner_kernel, plan), out_shape=pltpu.VME...]
    pallas_call x1, Pallas kernels: 1.81 us -> 2.39 us  [run_first(): pl.pallas_call(functools.partial(first_kernel, plan), out_shape=[pltpu.VM...]
  transfers between devices with their start and end apart: 7 -> 7, of which waited for: 2 -> 1; matrix products, arithmetic and copies ran while one was open for 2% -> 2% of each run, Pallas kernels for 43% -> 36%
where the time goes in v8:
time: 42.6 us; the launch traced here: 42.4 us
  Pallas kernels  21.3 us (50%)
  starting transfers between devices  12 us (28%)
  waiting for transfers between devices  8.01 us (19%)
  other arithmetic  0.91 us (2%)
    pallas_call x1, Pallas kernels, make_band(): pl.pallas_call(functools.partial(band_kernel, plan, depth), out_shape=[pl...  9.95 us
    ppermute x5, waiting for transfers between devices, partner(): return lax.ppermute(value, axis, pairs)  8.01 us
    ppermute x2, starting transfers between devices, swap_chips(): return lax.ppermute(value, axis, pairs)  6.85 us
    ppermute x5, starting transfers between devices, partner(): return lax.ppermute(value, axis, pairs)  5.12 us
    pallas_call x1, Pallas kernels, run_inner(): pl.pallas_call(functools.partial(inner_kernel, plan), out_shape=pltpu.VME...  2.94 us
    pallas_call x1, Pallas kernels, run_second(): pl.pallas_call(functools.partial(second_kernel, plan), out_shape=jax.Shap...  2.65 us
    pallas_call x1, Pallas kernels, run_first(): pl.pallas_call(functools.partial(first_kernel, plan), out_shape=[pltpu.VM...  2.39 us
    pallas_call x1, Pallas kernels, pack(): pl.pallas_call(functools.partial(pack_kernel, plan, chunks), out_shape=[p...  1.71 us
  transfers between devices with their start and end apart: 7, of which 1 were waited for; matrix products, arithmetic and copies ran while one was open for 2% of the time, Pallas kernels for 36%

profile of v8, /device:TPU:0, one launch (start us, length us, event | category | flops | bytes accessed | tf_op | source)
XLA Modules:
  0.0 42.4 jit_solution(15252040102263829276)
XLA Ops:
  0.0 3.0 %collective-permute-start = (s32[1,8]{1,0:T(1,128)}, s32[1,8]{1,0:T(1,128)S(1)}, u32[]{:S(2)}, u32[]{:S(2)}) collective-permute-start(s32[1,8]{1,0:T(1,128)} %param.7), channel_id=1, source_target_pairs={{0,4},{1,5},{2,6},{3,7},{4,0},{5,1},{6,2},{7,3},{8,12},{9,13},{10,... | collective-permute-start | bytes 104 | tf_op jit(solution)/shard_map/ppermute | solution.py:21
  3.0 1.7 %pack.1 = (f32[128,1536]{1,0:T(8,128)S(1)}, f32[64,1664]{1,0:T(8,128)S(1)}, f32[128,896]{1,0:T(8,128)S(1)}) custom-call(s32[1]{0:T(128)} %bitcast.side, f32[1536,128]{1,0:T(8,128)} %natural.1), custom_call_target="tpu_custom_call" | custom-call | tf_op jit(solution)/shard_map/pack/pallas_call | solution.py:162
  4.7 0.0 collective-permute-done.asked
  4.7 0.8 %far.1 = f32[128,512]{1,0:T(8,128)S(1)} custom-call(s32[1]{0:T(128)} %bitcast.side, s32[1,8]{1,0:T(1,128)S(1)} %collective-permute-done.asked, f32[128,1536]{1,0:T(8,128)S(1)} %get-tuple-element.21.turned.vectors.own.start), custom_call_target="tpu_custom_call" | custom-call | tf_op jit(solution)/shard_map/far/pallas_call | solution.py:184
  5.5 2.0 %collective-permute-start.2 = (f32[128,512]{1,0:T(8,128)S(1)}, f32[128,512]{1,0:T(8,128)S(1)}, u32[]{:S(2)}, u32[]{:S(2)}) collective-permute-start(f32[128,512]{1,0:T(8,128)S(1)} %far.1), channel_id=1, source_target_pairs={{0,4},{1,5},{2,6},{3,7},{4,0},{5,1},{6,2},{7,3},{8,12},{9,13},{10,... | collective-permute-start | bytes 786440 | tf_op jit(solution)/shard_map/ppermute | solution.py:21
  7.5 0.0 collective-permute-start.3
  7.5 0.7 %fusion = s32[24,27]{1,0:T(8,128)S(1)} fusion(s32[24,27]{1,0:T(8,128)} %param.6, s32[]{:T(128)} %select_n.27, s32[]{:T(128)S(6)} %mul.15), kind=kLoop, calls=%fused_computation.5 | loop fusion | flops 14256 | bytes 5192 | tf_op jit(solution)/shard_map/jit(_where)/select_n | solution.py:460
  8.2 0.1 copy.5
  8.3 4.6 %collective-permute-start.1 = (f32[64,1664]{1,0:T(8,128)S(1)}, f32[64,1664]{1,0:T(8,128)S(1)}, u32[]{:S(2)}, u32[]{:S(2)}) collective-permute-start(f32[64,1664]{1,0:T(8,128)S(1)} %get-tuple-element.22), channel_id=1, source_target_pairs={{0,31},{1,2},{2,1},{3,4},{4,3},{5,6},{6,5},{7,8},{8,7},{9,10},{10,... | collective-permute-start | bytes 1277960 | tf_op jit(solution)/shard_map/ppermute | solution.py:27
  12.9 0.2 select_reduce_fusion
  13.1 10.0 %band.1 = (bf16[12,2432,256]{2,1,0:T(8,128)(2,1)S(1)}, f32[128,1536]{1,0:T(8,128)S(1)}) custom-call(s32[1]{0:T(128)} %bitcast.side, s32[24,60]{1,0:T(8,128)S(1)} %broadcast_add_fusion.inverse, f32[1728,1536]{1,0:T(8,128)} %bitcast.2, f32[128,1536]{1,0:T(8,128)S(1)} %get-tuple-element.21.turned.vectors.own.start), custom_call_target="tpu_custom_call" | custom-call | bytes 21233664 | tf_op jit(solution)/shard_map/band/pallas_call | solution.py:261
  23.0 0.0 collective-permute-done.3.near
  23.0 0.8 %near.1.inner = f32[128,1536]{1,0:T(8,128)S(1)} custom-call(f32[128,896]{1,0:T(8,128)S(1)} %collective-permute-done.3.near, bf16[12,2432,256]{2,1,0:T(8,128)(2,1)S(1)} %get-tuple-element.25.band, f32[128,1536]{1,0:T(8,128)S(1)} %get-tuple-element.26.inner), custom_call_target="tpu_custom_call" | custom-call | flops 603979776 | tf_op jit(solution)/shard_map/near/pallas_call | solution.py:317
  23.8 0.0 collective-permute-done.2.far
  23.9 0.0 collective-permute-done.1.away
  23.9 2.4 %first.1 = (f32[128,1536]{1,0:T(8,128)S(1)}, f32[128,512]{1,0:T(8,128)S(1)}, f32[64,1664]{1,0:T(8,128)S(1)}, f32[128,896]{1,0:T(8,128)S(1)}) custom-call(s32[1]{0:T(128)} %bitcast.side, s32[1,8]{1,0:T(1,128)S(1)} %collective-permute-done.asked, f32[64,1664]{1,0:T(8,128)S(1)} %collective-permute-done.1.away, bf16[256,512]{1,0:T(8,128)(2,1)S(1)} %split.2.far, ...), custom_call_target="tpu_custom_call" | custom-call | flops 603979776 | tf_op jit(solution)/shard_map/first/pallas_call | solution.py:390
  26.3 0.1 collective-permute-start.6
  26.4 0.1 collective-permute-start.5
  26.5 2.3 %collective-permute-start.4 = (f32[64,1664]{1,0:T(8,128)S(1)}, f32[64,1664]{1,0:T(8,128)S(1)}, u32[]{:S(2)}, u32[]{:S(2)}) collective-permute-start(f32[64,1664]{1,0:T(8,128)S(1)} %get-tuple-element.28), channel_id=1, source_target_pairs={{0,31},{1,2},{2,1},{3,4},{4,3},{5,6},{6,5},{7,8},{8,7},{9,10},{10,... | collective-permute-start | bytes 1277960 | tf_op jit(solution)/shard_map/ppermute | solution.py:27
  28.7 0.0 collective-permute-done.6.near
  28.7 2.9 %inner.1 = f32[128,1536]{1,0:T(8,128)S(1)} custom-call(f32[128,1536]{1,0:T(8,128)S(1)} %get-tuple-element.30.vectors.own, f32[128,896]{1,0:T(8,128)S(1)} %collective-permute-done.6.near, bf16[12,2432,256]{2,1,0:T(8,128)(2,1)S(1)} %get-tuple-element.25.band), custom_call_target="tpu_custom_call" | custom-call | flops 2415919104 | tf_op jit(solution)/shard_map/inner/pallas_call | solution.py:339
  31.7 8.0 %collective-permute-done.5.far = f32[128,512]{1,0:T(8,128)S(1)} collective-permute-done((f32[128,512]{1,0:T(8,128)S(1)}, f32[128,512]{1,0:T(8,128)S(1)}, u32[]{:S(2)}, u32[]{:S(2)}) %collective-permute-start.5) | collective-permute-done | bytes 262176 | tf_op jit(solution)/shard_map/ppermute | solution.py:21
  39.7 0.0 collective-permute-done.4.away
  39.7 2.6 %second.1 = f32[1536,128]{1,0:T(8,128)} custom-call(s32[1]{0:T(128)} %bitcast.side, f32[64,1664]{1,0:T(8,128)S(1)} %collective-permute-done.4.away, bf16[256,512]{1,0:T(8,128)(2,1)S(1)} %split.3.far, bf16[12,2432,256]{2,1,0:T(8,128)(2,1)S(1)} %get-tuple-element.25.band, f32[128,1536]{1,0:T(8,128)S(1)} %inner.1, ...), custom_call_target="tpu_custom_call" | custom-call | flops 603979776 | tf_op jit(solution)/shard_map/second/pallas_call | solution.py:415
  (4 shorter events, 0.1 us)
Async XLA Ops:
  0.0 4.7 %collective-permute-start = (s32[1,8]{1,0:T(1,128)}, s32[1,8]{1,0:T(1,128)S(1)}, u32[]{:S(2)}, u32[]{:S(2)}) collective-permute-start(s32[1,8]{1,0:T(1,128)} %param.7), channel_id=1, source_target_pairs={{0,4},{1,5},{2,6},{3,7},{4,0},{5,1},{6,2},{7,3},{8,12},{9,13},{10,... | collective-permute-start | bytes 104 | tf_op jit(solution)/shard_map/ppermute | solution.py:21
  5.5 18.4 %collective-permute-start.2 = (f32[128,512]{1,0:T(8,128)S(1)}, f32[128,512]{1,0:T(8,128)S(1)}, u32[]{:S(2)}, u32[]{:S(2)}) collective-permute-start(f32[128,512]{1,0:T(8,128)S(1)} %far.1), channel_id=1, source_target_pairs={{0,4},{1,5},{2,6},{3,7},{4,0},{5,1},{6,2},{7,3},{8,12},{9,13},{10,... | collective-permute-start | bytes 786440 | tf_op jit(solution)/shard_map/ppermute | solution.py:21
  7.5 15.6 %collective-permute-start.3 = (f32[128,896]{1,0:T(8,128)S(1)}, f32[128,896]{1,0:T(8,128)S(1)}, u32[]{:S(2)}, u32[]{:S(2)}) collective-permute-start(f32[128,896]{1,0:T(8,128)S(1)} %get-tuple-element.23), channel_id=1, source_target_pairs={{0,1},{1,0},{2,3},{3,2},{4,5},{5,4},{6,7},{7,6},{8,9},{9,8},{10,11... | collective-permute-start | bytes 1376264 | tf_op jit(solution)/shard_map/ppermute | solution.py:21
  8.3 15.6 %collective-permute-start.1 = (f32[64,1664]{1,0:T(8,128)S(1)}, f32[64,1664]{1,0:T(8,128)S(1)}, u32[]{:S(2)}, u32[]{:S(2)}) collective-permute-start(f32[64,1664]{1,0:T(8,128)S(1)} %get-tuple-element.22), channel_id=1, source_target_pairs={{0,31},{1,2},{2,1},{3,4},{4,3},{5,6},{6,5},{7,8},{8,7},{9,10},{10,... | collective-permute-start | bytes 1277960 | tf_op jit(solution)/shard_map/ppermute | solution.py:27
  26.3 2.4 %collective-permute-start.6 = (f32[128,896]{1,0:T(8,128)S(1)}, f32[128,896]{1,0:T(8,128)S(1)}, u32[]{:S(2)}, u32[]{:S(2)}) collective-permute-start(f32[128,896]{1,0:T(8,128)S(1)} %get-tuple-element.31), channel_id=1, source_target_pairs={{0,1},{1,0},{2,3},{3,2},{4,5},{5,4},{6,7},{7,6},{8,9},{9,8},{10,11... | collective-permute-start | bytes 1376264 | tf_op jit(solution)/shard_map/ppermute | solution.py:21
  26.4 13.3 %collective-permute-start.5 = (f32[128,512]{1,0:T(8,128)S(1)}, f32[128,512]{1,0:T(8,128)S(1)}, u32[]{:S(2)}, u32[]{:S(2)}) collective-permute-start(f32[128,512]{1,0:T(8,128)S(1)} %get-tuple-element.29), channel_id=1, source_target_pairs={{0,4},{1,5},{2,6},{3,7},{4,0},{5,1},{6,2},{7,3},{8,12},{9,13},{10,... | collective-permute-start | bytes 786440 | tf_op jit(solution)/shard_map/ppermute | solution.py:21
  26.5 13.3 %collective-permute-start.4 = (f32[64,1664]{1,0:T(8,128)S(1)}, f32[64,1664]{1,0:T(8,128)S(1)}, u32[]{:S(2)}, u32[]{:S(2)}) collective-permute-start(f32[64,1664]{1,0:T(8,128)S(1)} %get-tuple-element.28), channel_id=1, source_target_pairs={{0,31},{1,2},{2,1},{3,4},{4,3},{5,6},{6,5},{7,8},{8,7},{9,10},{10,... | collective-permute-start | bytes 1277960 | tf_op jit(solution)/shard_map/ppermute | solution.py:27

commit v9 on v8

--- a/solution.py
+++ b/solution.py
@@ -12,6 +12,7 @@
 REACH = 13
 F32 = jnp.float32
 VMEM = pl.BlockSpec(memory_space=pltpu.VMEM)
+HBM = pl.BlockSpec(memory_space=pltpu.HBM)
 SMEM = pl.BlockSpec(memory_space=pltpu.SMEM)
 
 
@@ -134,7 +135,7 @@
     return [jax.ShapeDtypeStruct(shape, F32) for shape in shapes]
 
 
-def pack_kernel(plan, chunks, side, natural, turned, *rest):
+def pack_kernel(plan, chunks, side, natural, codes, turned, held, *rest):
     sends, staged, sems = rest[:-2], *rest[-2:]
     tile, count = plan.tile, plan.pairs // chunks
     step = count * tile
@@ -148,6 +149,8 @@
 
     for c in range(chunks):
         fetch(c).start()
+    copy = pltpu.make_async_copy(codes, held, sems.at[chunks])
+    copy.start()
     for c in range(chunks):
         fetch(c).wait()
     for t in range(plan.pairs):
@@ -155,22 +158,27 @@
         value = staged[pl.ds(at, tile), :].T
         turned[:, t * tile : (t + 1) * tile] = value
         write_sends(plan, side, t * tile, value, *sends)
-
-
-def pack(plan, side, natural):
+    copy.wait()
+
+
+def pack(plan, side, natural, codes):
     chunks = 4 if plan.pairs % 4 == 0 else 1
     return pl.pallas_call(
         functools.partial(pack_kernel, plan, chunks),
-        out_shape=[pltpu.VMEM((plan.width, plan.rows), F32)] + send_shapes(plan),
-        in_specs=[SMEM, pl.BlockSpec(memory_space=pltpu.HBM)],
-        out_specs=[VMEM] * 3,
+        out_shape=[
+            pltpu.VMEM((plan.width, plan.rows), F32),
+            pltpu.VMEM(codes.shape, codes.dtype),
+        ]
+        + send_shapes(plan),
+        in_specs=[SMEM, HBM, HBM],
+        out_specs=[VMEM] * 4,
         scratch_shapes=[
             pltpu.VMEM((plan.rows, plan.width), F32),
-            pltpu.SemaphoreType.DMA((chunks,)),
+            pltpu.SemaphoreType.DMA((chunks + 1,)),
         ],
         compiler_params=params(8),
         name="pack",
-    )(side, pltpu.with_memory_space_constraint(natural, pltpu.HBM))
+    )(side, *(pltpu.with_memory_space_constraint(x, pltpu.HBM) for x in (natural, codes)))
 
 
 def far_kernel(plan, side, asked, turned, out):
@@ -207,36 +215,38 @@
 
 def band_kernel(plan, depth, side, inverse, ham_t, vectors, band, inner, staged, halves, sems):
     size, tile = plan.size, plan.tile
-    slots = staged.shape[0]
-    ahead = slots - 1
+    group = staged.shape[2] // tile
+    units = plan.pairs // group
     lane = lax.broadcasted_iota(jnp.int32, (size, tile), 1)
 
-    def fetch(p):
-        at = pl.multiple_of(plan.mirrored(p, side) * tile, tile)
-        held = staged.at[p % slots, pl.ds(0, depth), :]
-        return pltpu.make_async_copy(ham_t.at[:, pl.ds(at, tile)], held, sems.at[p % slots])
+    def fetch(u):
+        natural = u + side[0] * (units - 1 - 2 * u)
+        at = pl.multiple_of(natural * group * tile, group * tile)
+        held = staged.at[u, pl.ds(0, depth), :]
+        return pltpu.make_async_copy(ham_t.at[:, pl.ds(at, group * tile)], held, sems.at[u])
 
     def store(p, at, high, low):
         band[p, at : at + size, :tile] = high
         band[p, at : at + size, tile:] = low
 
-    for p in range(min(ahead, plan.pairs)):
-        fetch(p).start()
-    for slot in range(slots):
-        staged[slot, depth:, :] = jnp.zeros((size, tile), F32)
+    for u in range(units):
+        fetch(u).start()
+    for u in range(units):
+        staged[u, depth:, :] = jnp.zeros((size, group * tile), F32)
     own_halves(plan, vectors, halves)
 
     for p in range(plan.pairs):
-        fetch(p).wait()
-        if p + ahead < plan.pairs:
-            fetch(p + ahead).start()
+        u, t = p // group, p % group
+        if t == 0:
+            fetch(u).wait()
+        lanes = pl.multiple_of((t + side[0] * (group - 1 - 2 * t)) * tile, tile)
         row = 2 * plan.mirrored(p, side)
 
         def block(q):
             even = pl.multiple_of(inverse[row, q] * size, size)
             odd = pl.multiple_of(inverse[row + 1, q] * size, size)
-            first = staged[p % slots, pl.ds(even, size), :]
-            second = staged[p % slots, pl.ds(odd, size), :]
+            first = staged[u, pl.ds(even, size), pl.ds(lanes, tile)]
+            second = staged[u, pl.ds(odd, size), pl.ds(lanes, tile)]
             return jnp.where(lane < size, first, second)
 
         ready = None if p == 0 else own_product(plan, p - 1, halves, band)
@@ -258,20 +268,21 @@
 def make_band(plan, side, inverse, ham_t, vectors):
     depth, rows = ham_t.shape
     size, tile = plan.size, plan.tile
+    group = 2 if plan.pairs % 2 == 0 else 1
     return pl.pallas_call(
         functools.partial(band_kernel, plan, depth),
         out_shape=[
             pltpu.VMEM((plan.pairs, plan.depth, 2 * tile), jnp.bfloat16),
             pltpu.VMEM((plan.width, rows), F32),
         ],
-        in_specs=[SMEM, SMEM, pl.BlockSpec(memory_space=pltpu.HBM), VMEM],
+        in_specs=[SMEM, SMEM, HBM, VMEM],
         out_specs=[VMEM, VMEM],
         scratch_shapes=[
-            pltpu.VMEM((4, depth + size, tile), F32),
+            pltpu.VMEM((plan.pairs // group, depth + size, group * tile), F32),
             pltpu.VMEM((2 * plan.width, rows), jnp.bfloat16),
-            pltpu.SemaphoreType.DMA((4,)),
+            pltpu.SemaphoreType.DMA((plan.pairs // group,)),
         ],
-        compiler_params=params(10),
+        compiler_params=params(14),
         cost_estimate=cost(0, 2 * 4 * depth * rows),
         name="band",
     )(side, inverse, pltpu.with_memory_space_constraint(ham_t, pltpu.HBM), vectors)
@@ -306,24 +317,26 @@
     return [away_tile(plan, side, away, t) for t in reversed(range(plan.near))]
 
 
-def near_kernel(plan, near, band, inner, out, halves):
-    put_halves(plan, halves, near_tiles(plan, near))
+def middle_kernel(plan, side, away, near, band, inner, out, away_halves, near_halves):
+    put_halves(plan, away_halves, away_tiles(plan, side, away))
+    put_halves(plan, near_halves, near_tiles(plan, near))
     for p in range(plan.pairs):
         lanes = slice(p * plan.tile, (p + 1) * plan.tile)
-        out[:, lanes] = inner[:, lanes] + message_product(plan, "near", p, halves, band)
-
-
-def add_near(plan, near, band, inner):
-    return pl.pallas_call(
-        functools.partial(near_kernel, plan),
+        total = inner[:, lanes] + message_product(plan, "away", p, away_halves, band)
+        out[:, lanes] = total + message_product(plan, "near", p, near_halves, band)
+
+
+def run_middle(plan, side, away, near, band, inner):
+    return pl.pallas_call(
+        functools.partial(middle_kernel, plan),
         out_shape=pltpu.VMEM((plan.width, plan.rows), F32),
-        in_specs=[VMEM] * 3,
+        in_specs=[SMEM] + [VMEM] * 4,
         out_specs=VMEM,
-        scratch_shapes=[halves_scratch(plan, plan.near)],
-        compiler_params=params(8),
-        cost_estimate=cost(2 * plan.width * plan.rows**2, 0),
-        name="near",
-    )(near, band, inner)
+        scratch_shapes=[halves_scratch(plan, plan.near)] * 2,
+        compiler_params=params(8),
+        cost_estimate=cost(8 * plan.width * plan.rows**2, 0),
+        name="middle",
+    )(side, away, near, band, inner)
 
 
 def inner_kernel(plan, vectors, near, band, out, halves, near_halves):
@@ -348,9 +361,12 @@
     )(vectors, near, band)
 
 
+def far_tiles(plan, far):
+    return [far[:, t * plan.tile : (t + 1) * plan.tile] for t in range(plan.far)]
+
+
 def far_split_kernel(plan, far, halves):
-    tile = plan.tile
-    put_halves(plan, halves, [far[:, t * tile : (t + 1) * tile] for t in range(plan.far)])
+    put_halves(plan, halves, far_tiles(plan, far))
 
 
 def split_far(plan, far):
@@ -366,14 +382,13 @@
 
 
 def first_kernel(
-    plan, side, asked, away, far, band, inner, own, value, to_far, to_away, to_near, halves
+    plan, side, asked, far, band, inner, own, value, to_far, to_away, to_near, halves
 ):
-    put_halves(plan, halves, away_tiles(plan, side, away))
+    put_halves(plan, halves, far_tiles(plan, far))
     for p in range(plan.pairs):
         lanes = slice(p * plan.tile, (p + 1) * plan.tile)
         product = inner[:, lanes] - CENTER * own[:, lanes]
-        product += message_product(plan, "far", p, far, band)
-        product += message_product(plan, "away", p, halves, band)
+        product += message_product(plan, "far", p, halves, band)
         term = product * (1.0 / HALF_WIDTH)
         value[:, lanes] = term
         write_sends(plan, side, lanes.start, term, to_away, to_near)
@@ -384,23 +399,23 @@
     write_far(plan, side, asked, value, write)
 
 
-def run_first(plan, side, asked, away, far, band, inner, own):
-    to_far = jax.ShapeDtypeStruct((plan.width, plan.far * plan.tile), F32)
-    shapes = [to_far] + send_shapes(plan)
+def run_first(plan, side, asked, far, band, inner, own):
+    shapes = [jax.ShapeDtypeStruct(far.shape, F32)] + send_shapes(plan)
     return pl.pallas_call(
         functools.partial(first_kernel, plan),
         out_shape=[pltpu.VMEM((plan.width, plan.rows), F32)] + shapes,
-        in_specs=[SMEM] * 2 + [VMEM] * 5,
+        in_specs=[SMEM] * 2 + [VMEM] * 4,
         out_specs=[VMEM] * (1 + len(shapes)),
-        scratch_shapes=[halves_scratch(plan, plan.near)],
+        scratch_shapes=[halves_scratch(plan, plan.far)],
         compiler_params=params(8),
         cost_estimate=cost(2 * plan.width * plan.rows**2, 0),
         name="first",
-    )(side, asked, away, far, band, inner, own)
-
-
-def second_kernel(plan, side, away, far, band, inner, own, start, out, halves):
+    )(side, asked, far, band, inner, own)
+
+
+def second_kernel(plan, side, away, far, band, inner, own, start, out, halves, held, sems):
     put_halves(plan, halves, away_tiles(plan, side, away))
+    copies = []
     for p in range(plan.pairs):
         lanes = slice(p * plan.tile, (p + 1) * plan.tile)
         product = inner[:, lanes] - CENTER * own[:, lanes]
@@ -408,7 +423,13 @@
         product += message_product(plan, "away", p, halves, band)
         term = 2.0 / HALF_WIDTH * product - start[:, lanes]
         place = pl.multiple_of(plan.mirrored(p, side) * plan.tile, plan.tile)
-        out[pl.ds(place, plan.tile), :] = term.T
+        held[p] = term.T
+        copies.append(
+            pltpu.make_async_copy(held.at[p], out.at[pl.ds(place, plan.tile), :], sems.at[p])
+        )
+        copies[-1].start()
+    for copy in copies:
+        copy.wait()
 
 
 def run_second(plan, side, away, far, band, inner, own, start):
@@ -416,8 +437,12 @@
         functools.partial(second_kernel, plan),
         out_shape=jax.ShapeDtypeStruct((plan.rows, plan.width), F32),
         in_specs=[SMEM] + [VMEM] * 6,
-        out_specs=VMEM,
-        scratch_shapes=[halves_scratch(plan, plan.near)],
+        out_specs=HBM,
+        scratch_shapes=[
+            halves_scratch(plan, plan.near),
+            pltpu.VMEM((plan.pairs, plan.tile, plan.width), F32),
+            pltpu.SemaphoreType.DMA((plan.pairs,)),
+        ],
         compiler_params=params(8),
         cost_estimate=cost(2 * plan.width * plan.rows**2, 0),
         name="second",
@@ -445,10 +470,9 @@
         return swap_chips(to_away, "rows"), far, partner(to_near, "rows", 0)
 
     asked = partner(far_list, "rows", swap_level)
-    start, *sends = pack(plan, side, subspace)
+    start, block_cols, *sends = pack(plan, side, subspace, block_cols)
     listed = gather_far(plan, side, asked, start)
-    to_away, to_near, _ = lax.optimization_barrier((*sends, listed))
-    away, far, near = exchange(listed, (to_away, to_near))
+    away, far, near = exchange(listed, sends)
 
     block_cols = after(block_cols, listed)
     edge, far_slots = 2 * plan.near, 2 * plan.far
@@ -477,10 +501,8 @@
 
     band, inner = make_band(plan, side, inverse, hamiltonian.T, start)
 
-    inner = add_near(plan, near, band, inner)
-    value, listed, *sends = run_first(
-        plan, side, asked, away, split_far(plan, after(far, inner)), band, inner, start
-    )
+    inner = run_middle(plan, side, away, near, band, inner)
+    value, listed, *sends = run_first(plan, side, asked, far, band, inner, start)
     away, far, near = exchange(listed, sends)
     inner = run_inner(plan, value, near, band)
     far = split_far(plan, after(far, inner))

time: 42.6 us -> 39.5 us (0.927)
  starting transfers between devices: 12 us -> 9.75 us
  Pallas kernels: 21.3 us -> 19.1 us
  waiting for transfers between devices: 8.01 us -> 10.1 us
  other arithmetic: 0.91 us -> 0.21 us
    ppermute x5, waiting for transfers between devices: 8.01 us -> 10.1 us  [partner(): return lax.ppermute(value, axis, pairs)]
    ppermute x5, starting transfers between devices: 5.12 us -> 3.19 us  [partner(): return lax.ppermute(value, axis, pairs)]
    pallas_call x1, Pallas kernels: 9.95 us -> 8.08 us  [make_band(): pl.pallas_call(functools.partial(band_kernel, plan, depth), out_shape=[pl...]
    select_n x1, other arithmetic: 0.72 us -> 0.02 us  [per_device(): jnp.where(block_cols >= block_total, edge + block_cols - block_total, jnp...]
    pallas_call x1, Pallas kernels: 2.39 us -> 1.76 us  [run_first(): pl.pallas_call(functools.partial(first_kernel, plan), out_shape=[pltpu.VM...]
    pallas_call x1, Pallas kernels: 0.77 us -> 1.31 us  [run_middle(): pl.pallas_call(functools.partial(middle_kernel, plan), out_shape=pltpu.VM...]
  transfers between devices with their start and end apart: 7 -> 7, of which waited for: 1 -> 2; matrix products, arithmetic and copies ran while one was open for 2% -> 1% of each run, Pallas kernels for 36% -> 38%
where the time goes in v9:
time: 39.5 us; the launch traced here: 39.3 us
  Pallas kernels  19.1 us (48%)
  waiting for transfers between devices  10.1 us (26%)
  starting transfers between devices  9.75 us (25%)
    ppermute x5, waiting for transfers between devices, partner(): return lax.ppermute(value, axis, pairs)  10.1 us
    pallas_call x1, Pallas kernels, make_band(): pl.pallas_call(functools.partial(band_kernel, plan, depth), out_shape=[pl...  8.08 us
    ppermute x2, starting transfers between devices, swap_chips(): return lax.ppermute(value, axis, pairs)  6.56 us
    ppermute x5, starting transfers between devices, partner(): return lax.ppermute(value, axis, pairs)  3.19 us
    pallas_call x1, Pallas kernels, run_inner(): pl.pallas_call(functools.partial(inner_kernel, plan), out_shape=pltpu.VME...  2.91 us
    pallas_call x1, Pallas kernels, run_second(): pl.pallas_call(functools.partial(second_kernel, plan), out_shape=jax.Shap...  2.51 us
    pallas_call x1, Pallas kernels, run_first(): pl.pallas_call(functools.partial(first_kernel, plan), out_shape=[pltpu.VM...  1.76 us
    pallas_call x1, Pallas kernels, pack(): pl.pallas_call(functools.partial(pack_kernel, plan, chunks), out_shape=[p...  1.72 us
  transfers between devices with their start and end apart: 7, of which 2 were waited for; matrix products, arithmetic and copies ran while one was open for 1% of the time, Pallas kernels for 38%

profile of v9, /device:TPU:0, one launch (start us, length us, event | category | flops | bytes accessed | tf_op | source)
XLA Modules:
  0.0 39.3 jit_solution(3760607110907699995)
XLA Ops:
  0.0 3.0 %collective-permute-start = (s32[1,8]{1,0:T(1,128)}, s32[1,8]{1,0:T(1,128)S(1)}, u32[]{:S(2)}, u32[]{:S(2)}) collective-permute-start(s32[1,8]{1,0:T(1,128)} %param.7), channel_id=1, source_target_pairs={{0,4},{1,5},{2,6},{3,7},{4,0},{5,1},{6,2},{7,3},{8,12},{9,13},{10,... | collective-permute-start | bytes 104 | tf_op jit(solution)/shard_map/ppermute | solution.py:22
  3.0 1.7 %pack.1 = (f32[128,1536]{1,0:T(8,128)S(1)}, s32[24,27]{1,0:T(8,128)S(1)}, f32[64,1664]{1,0:T(8,128)S(1)}, f32[128,896]{1,0:T(8,128)S(1)}) custom-call(s32[1]{0:T(128)} %bitcast.side, f32[1536,128]{1,0:T(8,128)} %natural.1, s32[24,27]{1,0:T(8,128)} %codes.1), custom_call_target="tpu_custom_call" | custom-call | tf_op jit(solution)/shard_map/pack/pallas_call | solution.py:166
  4.7 3.7 %collective-permute-start.2 = (f32[64,1664]{1,0:T(8,128)S(1)}, f32[64,1664]{1,0:T(8,128)S(1)}, u32[]{:S(2)}, u32[]{:S(2)}) collective-permute-start(f32[64,1664]{1,0:T(8,128)S(1)} %get-tuple-element.21), channel_id=1, source_target_pairs={{0,31},{1,2},{2,1},{3,4},{4,3},{5,6},{6,5},{7,8},{8,7},{9,10},{10,... | collective-permute-start | bytes 1277960 | tf_op jit(solution)/shard_map/ppermute | solution.py:28
  8.4 0.0 collective-permute-start.3
  8.4 0.0 collective-permute-done.asked
  8.4 0.8 %far.1 = f32[128,512]{1,0:T(8,128)S(1)} custom-call(s32[1]{0:T(128)} %bitcast.side, s32[1,8]{1,0:T(1,128)S(1)} %collective-permute-done.asked, f32[128,1536]{1,0:T(8,128)S(1)} %get-tuple-element.17.turned.vectors.own.start), custom_call_target="tpu_custom_call" | custom-call | tf_op jit(solution)/shard_map/far/pallas_call | solution.py:192
  9.2 0.1 collective-permute-start.1
  9.3 0.1 copy.5
  9.4 0.2 select_reduce_fusion
  9.6 8.1 %band.1 = (bf16[12,2432,256]{2,1,0:T(8,128)(2,1)S(1)}, f32[128,1536]{1,0:T(8,128)S(1)}) custom-call(s32[1]{0:T(128)} %bitcast.side, s32[24,60]{1,0:T(8,128)S(1)} %broadcast_add_fusion.inverse, f32[1728,1536]{1,0:T(8,128)} %bitcast.2, f32[128,1536]{1,0:T(8,128)S(1)} %get-tuple-element.17.turned.vectors.own.start), custom_call_target="tpu_custom_call" | custom-call | bytes 21233664 | tf_op jit(solution)/shard_map/band/pallas_call | solution.py:272
  17.7 0.0 collective-permute-done.2.away
  17.7 0.0 collective-permute-done.3.near
  17.7 1.3 %middle.1.inner = f32[128,1536]{1,0:T(8,128)S(1)} custom-call(s32[1]{0:T(128)} %bitcast.side, f32[64,1664]{1,0:T(8,128)S(1)} %collective-permute-done.2.away, f32[128,896]{1,0:T(8,128)S(1)} %collective-permute-done.3.near, bf16[12,2432,256]{2,1,0:T(8,128)(2,1)S(1)} %get-tuple-element.20.band, f32[128,1536]{1,0:T(8,128)S(1)} %get-tuple-element.23.inner), custom_call_target="tpu_custom_call" | custom-call | flops 2415919104 | tf_op jit(solution)/shard_map/middle/pallas_call | solution.py:330
  19.0 2.6 %collective-permute-done.1.far = f32[128,512]{1,0:T(8,128)S(1)} collective-permute-done((f32[128,512]{1,0:T(8,128)S(1)}, f32[128,512]{1,0:T(8,128)S(1)}, u32[]{:S(2)}, u32[]{:S(2)}) %collective-permute-start.1) | collective-permute-done | bytes 262176 | tf_op jit(solution)/shard_map/ppermute | solution.py:22
  21.6 1.8 %first.1 = (f32[128,1536]{1,0:T(8,128)S(1)}, f32[128,512]{1,0:T(8,128)S(1)}, f32[64,1664]{1,0:T(8,128)S(1)}, f32[128,896]{1,0:T(8,128)S(1)}) custom-call(s32[1]{0:T(128)} %bitcast.side, s32[1,8]{1,0:T(1,128)S(1)} %collective-permute-done.asked, f32[128,512]{1,0:T(8,128)S(1)} %collective-permute-done.1.far, ...), custom_call_target="tpu_custom_call" | custom-call | flops 603979776 | tf_op jit(solution)/shard_map/first/pallas_call | solution.py:404
  23.4 0.1 collective-permute-start.6
  23.5 0.0 collective-permute-start.5
  23.6 2.9 %collective-permute-start.4 = (f32[64,1664]{1,0:T(8,128)S(1)}, f32[64,1664]{1,0:T(8,128)S(1)}, u32[]{:S(2)}, u32[]{:S(2)}) collective-permute-start(f32[64,1664]{1,0:T(8,128)S(1)} %get-tuple-element.24), channel_id=1, source_target_pairs={{0,31},{1,2},{2,1},{3,4},{4,3},{5,6},{6,5},{7,8},{8,7},{9,10},{10,... | collective-permute-start | bytes 1277960 | tf_op jit(solution)/shard_map/ppermute | solution.py:28
  26.4 0.0 collective-permute-done.6.near
  26.4 2.9 %inner.1 = f32[128,1536]{1,0:T(8,128)S(1)} custom-call(f32[128,1536]{1,0:T(8,128)S(1)} %get-tuple-element.26.vectors.own, f32[128,896]{1,0:T(8,128)S(1)} %collective-permute-done.6.near, bf16[12,2432,256]{2,1,0:T(8,128)(2,1)S(1)} %get-tuple-element.20.band), custom_call_target="tpu_custom_call" | custom-call | flops 2415919104 | tf_op jit(solution)/shard_map/inner/pallas_call | solution.py:352
  29.3 7.4 %collective-permute-done.5.far = f32[128,512]{1,0:T(8,128)S(1)} collective-permute-done((f32[128,512]{1,0:T(8,128)S(1)}, f32[128,512]{1,0:T(8,128)S(1)}, u32[]{:S(2)}, u32[]{:S(2)}) %collective-permute-start.5) | collective-permute-done | bytes 262176 | tf_op jit(solution)/shard_map/ppermute | solution.py:22
  36.8 0.0 collective-permute-done.4.away
  36.8 2.5 %second.1 = f32[1536,128]{1,0:T(8,128)} custom-call(s32[1]{0:T(128)} %bitcast.side, f32[64,1664]{1,0:T(8,128)S(1)} %collective-permute-done.4.away, bf16[256,512]{1,0:T(8,128)(2,1)S(1)} %split.1.far, bf16[12,2432,256]{2,1,0:T(8,128)(2,1)S(1)} %get-tuple-element.20.band, f32[128,1536]{1,0:T(8,128)S(1)} %inner.1, ...), custom_call_target="tpu_custom_call" | custom-call | flops 603979776 | tf_op jit(solution)/shard_map/second/pallas_call | solution.py:436
  (4 shorter events, 0.1 us)
Async XLA Ops:
  0.0 8.4 %collective-permute-start = (s32[1,8]{1,0:T(1,128)}, s32[1,8]{1,0:T(1,128)S(1)}, u32[]{:S(2)}, u32[]{:S(2)}) collective-permute-start(s32[1,8]{1,0:T(1,128)} %param.7), channel_id=1, source_target_pairs={{0,4},{1,5},{2,6},{3,7},{4,0},{5,1},{6,2},{7,3},{8,12},{9,13},{10,... | collective-permute-start | bytes 104 | tf_op jit(solution)/shard_map/ppermute | solution.py:22
  4.7 13.0 %collective-permute-start.2 = (f32[64,1664]{1,0:T(8,128)S(1)}, f32[64,1664]{1,0:T(8,128)S(1)}, u32[]{:S(2)}, u32[]{:S(2)}) collective-permute-start(f32[64,1664]{1,0:T(8,128)S(1)} %get-tuple-element.21), channel_id=1, source_target_pairs={{0,31},{1,2},{2,1},{3,4},{4,3},{5,6},{6,5},{7,8},{8,7},{9,10},{10,... | collective-permute-start | bytes 1277960 | tf_op jit(solution)/shard_map/ppermute | solution.py:28
  8.4 9.3 %collective-permute-start.3 = (f32[128,896]{1,0:T(8,128)S(1)}, f32[128,896]{1,0:T(8,128)S(1)}, u32[]{:S(2)}, u32[]{:S(2)}) collective-permute-start(f32[128,896]{1,0:T(8,128)S(1)} %get-tuple-element.22), channel_id=1, source_target_pairs={{0,1},{1,0},{2,3},{3,2},{4,5},{5,4},{6,7},{7,6},{8,9},{9,8},{10,11... | collective-permute-start | bytes 1376264 | tf_op jit(solution)/shard_map/ppermute | solution.py:22
  9.2 12.5 %collective-permute-start.1 = (f32[128,512]{1,0:T(8,128)S(1)}, f32[128,512]{1,0:T(8,128)S(1)}, u32[]{:S(2)}, u32[]{:S(2)}) collective-permute-start(f32[128,512]{1,0:T(8,128)S(1)} %far.1), channel_id=1, source_target_pairs={{0,4},{1,5},{2,6},{3,7},{4,0},{5,1},{6,2},{7,3},{8,12},{9,13},{10,... | collective-permute-start | bytes 786440 | tf_op jit(solution)/shard_map/ppermute | solution.py:22
  23.4 3.0 %collective-permute-start.6 = (f32[128,896]{1,0:T(8,128)S(1)}, f32[128,896]{1,0:T(8,128)S(1)}, u32[]{:S(2)}, u32[]{:S(2)}) collective-permute-start(f32[128,896]{1,0:T(8,128)S(1)} %get-tuple-element.27), channel_id=1, source_target_pairs={{0,1},{1,0},{2,3},{3,2},{4,5},{5,4},{6,7},{7,6},{8,9},{9,8},{10,11... | collective-permute-start | bytes 1376264 | tf_op jit(solution)/shard_map/ppermute | solution.py:22
  23.5 13.2 %collective-permute-start.5 = (f32[128,512]{1,0:T(8,128)S(1)}, f32[128,512]{1,0:T(8,128)S(1)}, u32[]{:S(2)}, u32[]{:S(2)}) collective-permute-start(f32[128,512]{1,0:T(8,128)S(1)} %get-tuple-element.25), channel_id=1, source_target_pairs={{0,4},{1,5},{2,6},{3,7},{4,0},{5,1},{6,2},{7,3},{8,12},{9,13},{10,... | collective-permute-start | bytes 786440 | tf_op jit(solution)/shard_map/ppermute | solution.py:22
  23.6 13.3 %collective-permute-start.4 = (f32[64,1664]{1,0:T(8,128)S(1)}, f32[64,1664]{1,0:T(8,128)S(1)}, u32[]{:S(2)}, u32[]{:S(2)}) collective-permute-start(f32[64,1664]{1,0:T(8,128)S(1)} %get-tuple-element.24), channel_id=1, source_target_pairs={{0,31},{1,2},{2,1},{3,4},{4,3},{5,6},{6,5},{7,8},{8,7},{9,10},{10,... | collective-permute-start | bytes 1277960 | tf_op jit(solution)/shard_map/ppermute | solution.py:28

commit v10 on v9

--- a/solution.py
+++ b/solution.py
@@ -469,10 +469,10 @@
         far = partner(listed, "rows", swap_level)
         return swap_chips(to_away, "rows"), far, partner(to_near, "rows", 0)
 
-    asked = partner(far_list, "rows", swap_level)
     start, block_cols, *sends = pack(plan, side, subspace, block_cols)
+    asked = partner(after(far_list, start), "rows", swap_level)
     listed = gather_far(plan, side, asked, start)
-    away, far, near = exchange(listed, sends)
+    away, far, near = exchange(listed, (sends[0], after(sends[1], listed)))
 
     block_cols = after(block_cols, listed)
     edge, far_slots = 2 * plan.near, 2 * plan.far

time: 39.5 us -> 37.8 us (0.957)
  waiting for transfers between devices: 10.1 us -> 6.27 us
  starting transfers between devices: 9.75 us -> 11.9 us
    ppermute x5, waiting for transfers between devices: 10.1 us -> 6.26 us  [partner(): return lax.ppermute(value, axis, pairs)]
    ppermute x5, starting transfers between devices: 3.19 us -> 4.88 us  [partner(): return lax.ppermute(value, axis, pairs)]
    ppermute x2, starting transfers between devices: 6.56 us -> 7.04 us  [swap_chips(): return lax.ppermute(value, axis, pairs)]
  transfers between devices with their start and end apart: 7 -> 7, of which waited for: 2 -> 2; matrix products, arithmetic and copies ran while one was open for 1% -> 1% of each run, Pallas kernels for 38% -> 35%
where the time goes in v10:
time: 37.8 us; the launch traced here: 37.7 us
  Pallas kernels  19.1 us (51%)
  starting transfers between devices  11.9 us (31%)
  waiting for transfers between devices  6.27 us (17%)
    pallas_call x1, Pallas kernels, make_band(): pl.pallas_call(functools.partial(band_kernel, plan, depth), out_shape=[pl...  8.08 us
    ppermute x2, starting transfers between devices, swap_chips(): return lax.ppermute(value, axis, pairs)  7.04 us
    ppermute x5, waiting for transfers between devices, partner(): return lax.ppermute(value, axis, pairs)  6.26 us
    ppermute x5, starting transfers between devices, partner(): return lax.ppermute(value, axis, pairs)  4.88 us
    pallas_call x1, Pallas kernels, run_inner(): pl.pallas_call(functools.partial(inner_kernel, plan), out_shape=pltpu.VME...  2.91 us
    pallas_call x1, Pallas kernels, run_second(): pl.pallas_call(functools.partial(second_kernel, plan), out_shape=jax.Shap...  2.51 us
    pallas_call x1, Pallas kernels, run_first(): pl.pallas_call(functools.partial(first_kernel, plan), out_shape=[pltpu.VM...  1.76 us
    pallas_call x1, Pallas kernels, pack(): pl.pallas_call(functools.partial(pack_kernel, plan, chunks), out_shape=[p...  1.72 us
  transfers between devices with their start and end apart: 7, of which 2 were waited for; matrix products, arithmetic and copies ran while one was open for 1% of the time, Pallas kernels for 35%

profile of v10, /device:TPU:0, one launch (start us, length us, event | category | flops | bytes accessed | tf_op | source)
XLA Modules:
  0.0 37.7 jit_solution(1244431294740063046)
XLA Ops:
  0.0 1.7 %pack.1 = (f32[128,1536]{1,0:T(8,128)S(1)}, s32[24,27]{1,0:T(8,128)S(1)}, f32[64,1664]{1,0:T(8,128)S(1)}, f32[128,896]{1,0:T(8,128)S(1)}) custom-call(s32[1]{0:T(128)} %bitcast.side, f32[1536,128]{1,0:T(8,128)} %natural.1, s32[24,27]{1,0:T(8,128)} %codes.1), custom_call_target="tpu_custom_call" | custom-call | tf_op jit(solution)/shard_map/pack/pallas_call | solution.py:166
  1.7 3.0 %collective-permute-start = (s32[1,8]{1,0:T(1,128)}, s32[1,8]{1,0:T(1,128)S(1)}, u32[]{:S(2)}, u32[]{:S(2)}) collective-permute-start(s32[1,8]{1,0:T(1,128)} %param.7), channel_id=1, source_target_pairs={{0,4},{1,5},{2,6},{3,7},{4,0},{5,1},{6,2},{7,3},{8,12},{9,13},{10,... | collective-permute-start | bytes 104 | tf_op jit(solution)/shard_map/ppermute | solution.py:22
  4.8 3.6 %collective-permute-start.2 = (f32[64,1664]{1,0:T(8,128)S(1)}, f32[64,1664]{1,0:T(8,128)S(1)}, u32[]{:S(2)}, u32[]{:S(2)}) collective-permute-start(f32[64,1664]{1,0:T(8,128)S(1)} %get-tuple-element.24), channel_id=1, source_target_pairs={{0,31},{1,2},{2,1},{3,4},{4,3},{5,6},{6,5},{7,8},{8,7},{9,10},{10,... | collective-permute-start | bytes 1277960 | tf_op jit(solution)/shard_map/ppermute | solution.py:28
  8.4 0.0 collective-permute-done.asked
  8.4 0.8 %far.1 = f32[128,512]{1,0:T(8,128)S(1)} custom-call(s32[1]{0:T(128)} %bitcast.side, s32[1,8]{1,0:T(1,128)S(1)} %collective-permute-done.asked, f32[128,1536]{1,0:T(8,128)S(1)} %get-tuple-element.19.turned.vectors.own.start), custom_call_target="tpu_custom_call" | custom-call | tf_op jit(solution)/shard_map/far/pallas_call | solution.py:192
  9.2 0.1 collective-permute-start.1
  9.3 0.0 collective-permute-start.3
  9.3 0.1 copy.5
  9.4 0.2 select_reduce_fusion
  9.6 8.1 %band.1 = (bf16[12,2432,256]{2,1,0:T(8,128)(2,1)S(1)}, f32[128,1536]{1,0:T(8,128)S(1)}) custom-call(s32[1]{0:T(128)} %bitcast.side, s32[24,60]{1,0:T(8,128)S(1)} %broadcast_add_fusion.inverse, f32[1728,1536]{1,0:T(8,128)} %bitcast.2, f32[128,1536]{1,0:T(8,128)S(1)} %get-tuple-element.19.turned.vectors.own.start), custom_call_target="tpu_custom_call" | custom-call | bytes 21233664 | tf_op jit(solution)/shard_map/band/pallas_call | solution.py:272
  17.7 0.0 collective-permute-done.2.away
  17.7 0.0 collective-permute-done.3.near
  17.7 1.3 %middle.1.inner = f32[128,1536]{1,0:T(8,128)S(1)} custom-call(s32[1]{0:T(128)} %bitcast.side, f32[64,1664]{1,0:T(8,128)S(1)} %collective-permute-done.2.away, f32[128,896]{1,0:T(8,128)S(1)} %collective-permute-done.3.near, bf16[12,2432,256]{2,1,0:T(8,128)(2,1)S(1)} %get-tuple-element.23.band, f32[128,1536]{1,0:T(8,128)S(1)} %get-tuple-element.27.inner), custom_call_target="tpu_custom_call" | custom-call | flops 2415919104 | tf_op jit(solution)/shard_map/middle/pallas_call | solution.py:330
  19.1 0.9 %collective-permute-done.1.far = f32[128,512]{1,0:T(8,128)S(1)} collective-permute-done((f32[128,512]{1,0:T(8,128)S(1)}, f32[128,512]{1,0:T(8,128)S(1)}, u32[]{:S(2)}, u32[]{:S(2)}) %collective-permute-start.1) | collective-permute-done | bytes 262176 | tf_op jit(solution)/shard_map/ppermute | solution.py:22
  20.0 1.8 %first.1 = (f32[128,1536]{1,0:T(8,128)S(1)}, f32[128,512]{1,0:T(8,128)S(1)}, f32[64,1664]{1,0:T(8,128)S(1)}, f32[128,896]{1,0:T(8,128)S(1)}) custom-call(s32[1]{0:T(128)} %bitcast.side, s32[1,8]{1,0:T(1,128)S(1)} %collective-permute-done.asked, f32[128,512]{1,0:T(8,128)S(1)} %collective-permute-done.1.far, ...), custom_call_target="tpu_custom_call" | custom-call | flops 603979776 | tf_op jit(solution)/shard_map/first/pallas_call | solution.py:404
  21.8 0.1 collective-permute-start.6
  21.8 1.6 %collective-permute-start.5 = (f32[128,512]{1,0:T(8,128)S(1)}, f32[128,512]{1,0:T(8,128)S(1)}, u32[]{:S(2)}, u32[]{:S(2)}) collective-permute-start(f32[128,512]{1,0:T(8,128)S(1)} %get-tuple-element.29), channel_id=1, source_target_pairs={{0,4},{1,5},{2,6},{3,7},{4,0},{5,1},{6,2},{7,3},{8,12},{9,13},{10,... | collective-permute-start | bytes 786440 | tf_op jit(solution)/shard_map/ppermute | solution.py:22
  23.5 3.4 %collective-permute-start.4 = (f32[64,1664]{1,0:T(8,128)S(1)}, f32[64,1664]{1,0:T(8,128)S(1)}, u32[]{:S(2)}, u32[]{:S(2)}) collective-permute-start(f32[64,1664]{1,0:T(8,128)S(1)} %get-tuple-element.28), channel_id=1, source_target_pairs={{0,31},{1,2},{2,1},{3,4},{4,3},{5,6},{6,5},{7,8},{8,7},{9,10},{10,... | collective-permute-start | bytes 1277960 | tf_op jit(solution)/shard_map/ppermute | solution.py:28
  26.9 0.0 collective-permute-done.6.near
  26.9 2.9 %inner.1 = f32[128,1536]{1,0:T(8,128)S(1)} custom-call(f32[128,1536]{1,0:T(8,128)S(1)} %get-tuple-element.30.vectors.own, f32[128,896]{1,0:T(8,128)S(1)} %collective-permute-done.6.near, bf16[12,2432,256]{2,1,0:T(8,128)(2,1)S(1)} %get-tuple-element.23.band), custom_call_target="tpu_custom_call" | custom-call | flops 2415919104 | tf_op jit(solution)/shard_map/inner/pallas_call | solution.py:352
  29.8 5.3 %collective-permute-done.5.far = f32[128,512]{1,0:T(8,128)S(1)} collective-permute-done((f32[128,512]{1,0:T(8,128)S(1)}, f32[128,512]{1,0:T(8,128)S(1)}, u32[]{:S(2)}, u32[]{:S(2)}) %collective-permute-start.5) | collective-permute-done | bytes 262176 | tf_op jit(solution)/shard_map/ppermute | solution.py:22
  35.2 0.0 collective-permute-done.4.away
  35.2 2.5 %second.1 = f32[1536,128]{1,0:T(8,128)} custom-call(s32[1]{0:T(128)} %bitcast.side, f32[64,1664]{1,0:T(8,128)S(1)} %collective-permute-done.4.away, bf16[256,512]{1,0:T(8,128)(2,1)S(1)} %split.1.far, bf16[12,2432,256]{2,1,0:T(8,128)(2,1)S(1)} %get-tuple-element.23.band, f32[128,1536]{1,0:T(8,128)S(1)} %inner.1, ...), custom_call_target="tpu_custom_call" | custom-call | flops 603979776 | tf_op jit(solution)/shard_map/second/pallas_call | solution.py:436
  (4 shorter events, 0.1 us)
Async XLA Ops:
  1.7 6.7 %collective-permute-start = (s32[1,8]{1,0:T(1,128)}, s32[1,8]{1,0:T(1,128)S(1)}, u32[]{:S(2)}, u32[]{:S(2)}) collective-permute-start(s32[1,8]{1,0:T(1,128)} %param.7), channel_id=1, source_target_pairs={{0,4},{1,5},{2,6},{3,7},{4,0},{5,1},{6,2},{7,3},{8,12},{9,13},{10,... | collective-permute-start | bytes 104 | tf_op jit(solution)/shard_map/ppermute | solution.py:22
  4.8 13.0 %collective-permute-start.2 = (f32[64,1664]{1,0:T(8,128)S(1)}, f32[64,1664]{1,0:T(8,128)S(1)}, u32[]{:S(2)}, u32[]{:S(2)}) collective-permute-start(f32[64,1664]{1,0:T(8,128)S(1)} %get-tuple-element.24), channel_id=1, source_target_pairs={{0,31},{1,2},{2,1},{3,4},{4,3},{5,6},{6,5},{7,8},{8,7},{9,10},{10,... | collective-permute-start | bytes 1277960 | tf_op jit(solution)/shard_map/ppermute | solution.py:28
  9.2 10.8 %collective-permute-start.1 = (f32[128,512]{1,0:T(8,128)S(1)}, f32[128,512]{1,0:T(8,128)S(1)}, u32[]{:S(2)}, u32[]{:S(2)}) collective-permute-start(f32[128,512]{1,0:T(8,128)S(1)} %far.1), channel_id=1, source_target_pairs={{0,4},{1,5},{2,6},{3,7},{4,0},{5,1},{6,2},{7,3},{8,12},{9,13},{10,... | collective-permute-start | bytes 786440 | tf_op jit(solution)/shard_map/ppermute | solution.py:22
  9.3 8.5 %collective-permute-start.3 = (f32[128,896]{1,0:T(8,128)S(1)}, f32[128,896]{1,0:T(8,128)S(1)}, u32[]{:S(2)}, u32[]{:S(2)}) collective-permute-start(f32[128,896]{1,0:T(8,128)S(1)} %get-tuple-element.26), channel_id=1, source_target_pairs={{0,1},{1,0},{2,3},{3,2},{4,5},{5,4},{6,7},{7,6},{8,9},{9,8},{10,11... | collective-permute-start | bytes 1376264 | tf_op jit(solution)/shard_map/ppermute | solution.py:22
  21.8 5.1 %collective-permute-start.6 = (f32[128,896]{1,0:T(8,128)S(1)}, f32[128,896]{1,0:T(8,128)S(1)}, u32[]{:S(2)}, u32[]{:S(2)}) collective-permute-start(f32[128,896]{1,0:T(8,128)S(1)} %get-tuple-element.31), channel_id=1, source_target_pairs={{0,1},{1,0},{2,3},{3,2},{4,5},{5,4},{6,7},{7,6},{8,9},{9,8},{10,11... | collective-permute-start | bytes 1376264 | tf_op jit(solution)/shard_map/ppermute | solution.py:22
  21.8 13.3 %collective-permute-start.5 = (f32[128,512]{1,0:T(8,128)S(1)}, f32[128,512]{1,0:T(8,128)S(1)}, u32[]{:S(2)}, u32[]{:S(2)}) collective-permute-start(f32[128,512]{1,0:T(8,128)S(1)} %get-tuple-element.29), channel_id=1, source_target_pairs={{0,4},{1,5},{2,6},{3,7},{4,0},{5,1},{6,2},{7,3},{8,12},{9,13},{10,... | collective-permute-start | bytes 786440 | tf_op jit(solution)/shard_map/ppermute | solution.py:22
  23.5 11.7 %collective-permute-start.4 = (f32[64,1664]{1,0:T(8,128)S(1)}, f32[64,1664]{1,0:T(8,128)S(1)}, u32[]{:S(2)}, u32[]{:S(2)}) collective-permute-start(f32[64,1664]{1,0:T(8,128)S(1)} %get-tuple-element.28), channel_id=1, source_target_pairs={{0,31},{1,2},{2,1},{3,4},{4,3},{5,6},{6,5},{7,8},{8,7},{9,10},{10,... | collective-permute-start | bytes 1277960 | tf_op jit(solution)/shard_map/ppermute | solution.py:28

commit v11 on v10

--- a/solution.py
+++ b/solution.py
@@ -135,8 +135,9 @@
     return [jax.ShapeDtypeStruct(shape, F32) for shape in shapes]
 
 
-def pack_kernel(plan, chunks, side, natural, codes, turned, held, *rest):
+def pack_kernel(plan, chunks, natural, codes, turned, held, *rest):
     sends, staged, sems = rest[:-2], *rest[-2:]
+    side = parity()
     tile, count = plan.tile, plan.pairs // chunks
     step = count * tile
 
@@ -161,7 +162,7 @@
     copy.wait()
 
 
-def pack(plan, side, natural, codes):
+def pack(plan, natural, codes):
     chunks = 4 if plan.pairs % 4 == 0 else 1
     return pl.pallas_call(
         functools.partial(pack_kernel, plan, chunks),
@@ -170,7 +171,7 @@
             pltpu.VMEM(codes.shape, codes.dtype),
         ]
         + send_shapes(plan),
-        in_specs=[SMEM, HBM, HBM],
+        in_specs=[HBM, HBM],
         out_specs=[VMEM] * 4,
         scratch_shapes=[
             pltpu.VMEM((plan.rows, plan.width), F32),
@@ -178,25 +179,25 @@
         ],
         compiler_params=params(8),
         name="pack",
-    )(side, *(pltpu.with_memory_space_constraint(x, pltpu.HBM) for x in (natural, codes)))
-
-
-def far_kernel(plan, side, asked, turned, out):
+    )(*(pltpu.with_memory_space_constraint(x, pltpu.HBM) for x in (natural, codes)))
+
+
+def far_kernel(plan, asked, turned, out):
     def write(at, value):
         out[:, at : at + plan.tile] = value
 
-    write_far(plan, side, asked, turned, write)
-
-
-def gather_far(plan, side, asked, turned):
+    write_far(plan, parity(), asked, turned, write)
+
+
+def gather_far(plan, asked, turned):
     return pl.pallas_call(
         functools.partial(far_kernel, plan),
         out_shape=jax.ShapeDtypeStruct((plan.width, plan.far * plan.tile), F32),
-        in_specs=[SMEM, SMEM, VMEM],
+        in_specs=[SMEM, VMEM],
         out_specs=VMEM,
         compiler_params=params(8),
         name="far",
-    )(side, asked, turned)
+    )(asked, turned)
 
 
 def own_halves(plan, vectors, halves):
@@ -213,8 +214,11 @@
     return fold(jnp.dot(vectors, band[p, row : row + rows, :], preferred_element_type=F32))
 
 
-def band_kernel(plan, depth, side, inverse, ham_t, vectors, band, inner, staged, halves, sems):
+def band_kernel(
+    plan, depth, table, ham_t, vectors, band, inner, staged, halves, inverse, sems
+):
     size, tile = plan.size, plan.tile
+    side = parity()
     group = staged.shape[2] // tile
     units = plan.pairs // group
     lane = lax.broadcasted_iota(jnp.int32, (size, tile), 1)
@@ -229,11 +233,14 @@
         band[p, at : at + size, :tile] = high
         band[p, at : at + size, tile:] = low
 
+    copy = pltpu.make_async_copy(table, inverse, sems.at[units])
+    copy.start()
     for u in range(units):
         fetch(u).start()
     for u in range(units):
         staged[u, depth:, :] = jnp.zeros((size, group * tile), F32)
     own_halves(plan, vectors, halves)
+    copy.wait()
 
     for p in range(plan.pairs):
         u, t = p // group, p % group
@@ -265,7 +272,7 @@
     inner[:, p * tile : (p + 1) * tile] = own_product(plan, p, halves, band)
 
 
-def make_band(plan, side, inverse, ham_t, vectors):
+def make_band(plan, inverse, ham_t, vectors):
     depth, rows = ham_t.shape
     size, tile = plan.size, plan.tile
     group = 2 if plan.pairs % 2 == 0 else 1
@@ -275,17 +282,18 @@
             pltpu.VMEM((plan.pairs, plan.depth, 2 * tile), jnp.bfloat16),
             pltpu.VMEM((plan.width, rows), F32),
         ],
-        in_specs=[SMEM, SMEM, HBM, VMEM],
+        in_specs=[VMEM, HBM, VMEM],
         out_specs=[VMEM, VMEM],
         scratch_shapes=[
             pltpu.VMEM((plan.pairs // group, depth + size, group * tile), F32),
             pltpu.VMEM((2 * plan.width, rows), jnp.bfloat16),
-            pltpu.SemaphoreType.DMA((plan.pairs // group,)),
+            pltpu.SMEM(inverse.shape, inverse.dtype),
+            pltpu.SemaphoreType.DMA((plan.pairs // group + 1,)),
         ],
         compiler_params=params(14),
         cost_estimate=cost(0, 2 * 4 * depth * rows),
         name="band",
-    )(side, inverse, pltpu.with_memory_space_constraint(ham_t, pltpu.HBM), vectors)
+    )(inverse, pltpu.with_memory_space_constraint(ham_t, pltpu.HBM), vectors)
 
 
 def put_halves(plan, halves, tiles):
@@ -317,8 +325,8 @@
     return [away_tile(plan, side, away, t) for t in reversed(range(plan.near))]
 
 
-def middle_kernel(plan, side, away, near, band, inner, out, away_halves, near_halves):
-    put_halves(plan, away_halves, away_tiles(plan, side, away))
+def middle_kernel(plan, away, near, band, inner, out, away_halves, near_halves):
+    put_halves(plan, away_halves, away_tiles(plan, parity(), away))
     put_halves(plan, near_halves, near_tiles(plan, near))
     for p in range(plan.pairs):
         lanes = slice(p * plan.tile, (p + 1) * plan.tile)
@@ -326,17 +334,17 @@
         out[:, lanes] = total + message_product(plan, "near", p, near_halves, band)
 
 
-def run_middle(plan, side, away, near, band, inner):
+def run_middle(plan, away, near, band, inner):
     return pl.pallas_call(
         functools.partial(middle_kernel, plan),
         out_shape=pltpu.VMEM((plan.width, plan.rows), F32),
-        in_specs=[SMEM] + [VMEM] * 4,
+        in_specs=[VMEM] * 4,
         out_specs=VMEM,
         scratch_shapes=[halves_scratch(plan, plan.near)] * 2,
         compiler_params=params(8),
         cost_estimate=cost(8 * plan.width * plan.rows**2, 0),
         name="middle",
-    )(side, away, near, band, inner)
+    )(away, near, band, inner)
 
 
 def inner_kernel(plan, vectors, near, band, out, halves, near_halves):
@@ -382,8 +390,11 @@
 
 
 def first_kernel(
-    plan, side, asked, far, band, inner, own, value, to_far, to_away, to_near, halves
+    plan, listed, far, band, inner, own, value, to_far, to_away, to_near, halves, asked, sem
 ):
+    copy = pltpu.make_async_copy(listed, asked, sem)
+    copy.start()
+    side = parity()
     put_halves(plan, halves, far_tiles(plan, far))
     for p in range(plan.pairs):
         lanes = slice(p * plan.tile, (p + 1) * plan.tile)
@@ -396,24 +407,30 @@
     def write(at, term):
         to_far[:, at : at + plan.tile] = term
 
+    copy.wait()
     write_far(plan, side, asked, value, write)
 
 
-def run_first(plan, side, asked, far, band, inner, own):
+def run_first(plan, asked, far, band, inner, own):
     shapes = [jax.ShapeDtypeStruct(far.shape, F32)] + send_shapes(plan)
     return pl.pallas_call(
         functools.partial(first_kernel, plan),
         out_shape=[pltpu.VMEM((plan.width, plan.rows), F32)] + shapes,
-        in_specs=[SMEM] * 2 + [VMEM] * 4,
+        in_specs=[VMEM] * 5,
         out_specs=[VMEM] * (1 + len(shapes)),
-        scratch_shapes=[halves_scratch(plan, plan.far)],
+        scratch_shapes=[
+            halves_scratch(plan, plan.far),
+            pltpu.SMEM(asked.shape, asked.dtype),
+            pltpu.SemaphoreType.DMA,
+        ],
         compiler_params=params(8),
         cost_estimate=cost(2 * plan.width * plan.rows**2, 0),
         name="first",
-    )(side, asked, far, band, inner, own)
-
-
-def second_kernel(plan, side, away, far, band, inner, own, start, out, halves, held, sems):
+    )(asked, far, band, inner, own)
+
+
+def second_kernel(plan, away, far, band, inner, own, start, out, halves, held, sems):
+    side = parity()
     put_halves(plan, halves, away_tiles(plan, side, away))
     copies = []
     for p in range(plan.pairs):
@@ -432,11 +449,11 @@
         copy.wait()
 
 
-def run_second(plan, side, away, far, band, inner, own, start):
+def run_second(plan, away, far, band, inner, own, start):
     return pl.pallas_call(
         functools.partial(second_kernel, plan),
         out_shape=jax.ShapeDtypeStruct((plan.rows, plan.width), F32),
-        in_specs=[SMEM] + [VMEM] * 6,
+        in_specs=[VMEM] * 6,
         out_specs=HBM,
         scratch_shapes=[
             halves_scratch(plan, plan.near),
@@ -446,7 +463,11 @@
         compiler_params=params(8),
         cost_estimate=cost(2 * plan.width * plan.rows**2, 0),
         name="second",
-    )(side, away, far, band, inner, own, start)
+    )(away, far, band, inner, own, start)
+
+
+def parity():
+    return (lax.rem(lax.axis_index("rows"), 2),)
 
 
 def after(value, *others):
@@ -469,9 +490,9 @@
         far = partner(listed, "rows", swap_level)
         return swap_chips(to_away, "rows"), far, partner(to_near, "rows", 0)
 
-    start, block_cols, *sends = pack(plan, side, subspace, block_cols)
+    start, block_cols, *sends = pack(plan, subspace, block_cols)
     asked = partner(after(far_list, start), "rows", swap_level)
-    listed = gather_far(plan, side, asked, start)
+    listed = gather_far(plan, asked, start)
     away, far, near = exchange(listed, (sends[0], after(sends[1], listed)))
 
     block_cols = after(block_cols, listed)
@@ -499,14 +520,14 @@
     hit = places[:, :, None] == every
     inverse = entries + jnp.sum(jnp.where(hit, entry - entries, 0), axis=1)
 
-    band, inner = make_band(plan, side, inverse, hamiltonian.T, start)
-
-    inner = run_middle(plan, side, away, near, band, inner)
-    value, listed, *sends = run_first(plan, side, asked, far, band, inner, start)
+    band, inner = make_band(plan, inverse, hamiltonian.T, start)
+
+    inner = run_middle(plan, away, near, band, inner)
+    value, listed, *sends = run_first(plan, asked, far, band, inner, start)
     away, far, near = exchange(listed, sends)
     inner = run_inner(plan, value, near, band)
     far = split_far(plan, after(far, inner))
-    return run_second(plan, side, away, far, band, inner, value, start)
+    return run_second(plan, away, far, band, inner, value, start)
 
 
 def solution(mesh):

time: 37.8 us -> 37.3 us (0.987)
  Pallas kernels: 19.1 us -> 18 us
  waiting for transfers between devices: 6.27 us -> 7.11 us
    ppermute x5, waiting for transfers between devices: 6.26 us -> 7.11 us  [partner(): return lax.ppermute(value, axis, pairs)]
    pallas_call x1, Pallas kernels: 8.08 us -> 7.37 us  [make_band(): pl.pallas_call(functools.partial(band_kernel, plan, depth), out_shape=[pl...]
    ppermute x5, starting transfers between devices: 4.88 us -> 4.37 us  [partner(): return lax.ppermute(value, axis, pairs)]
    pallas_call x1, Pallas kernels: 1.76 us -> 1.26 us  [run_first(): pl.pallas_call(functools.partial(first_kernel, plan), out_shape=[pltpu.VM...]
  transfers between devices with their start and end apart: 7 -> 7, of which waited for: 2 -> 2; matrix products, arithmetic and copies ran while one was open for 1% -> 1% of each run, Pallas kernels for 35% -> 34%
where the time goes in v11:
time: 37.3 us; the launch traced here: 37.2 us
  Pallas kernels  18 us (48%)
  starting transfers between devices  11.7 us (31%)
  waiting for transfers between devices  7.11 us (19%)
    pallas_call x1, Pallas kernels, make_band(): pl.pallas_call(functools.partial(band_kernel, plan, depth), out_shape=[pl...  7.37 us
    ppermute x2, starting transfers between devices, swap_chips(): return lax.ppermute(value, axis, pairs)  7.33 us
    ppermute x5, waiting for transfers between devices, partner(): return lax.ppermute(value, axis, pairs)  7.11 us
    ppermute x5, starting transfers between devices, partner(): return lax.ppermute(value, axis, pairs)  4.37 us
    pallas_call x1, Pallas kernels, run_inner(): pl.pallas_call(functools.partial(inner_kernel, plan), out_shape=pltpu.VME...  2.95 us
    pallas_call x1, Pallas kernels, run_second(): pl.pallas_call(functools.partial(second_kernel, plan), out_shape=jax.Shap...  2.5 us
    pallas_call x1, Pallas kernels, pack(): pl.pallas_call(functools.partial(pack_kernel, plan, chunks), out_shape=[p...  1.72 us
    pallas_call x1, Pallas kernels, run_middle(): pl.pallas_call(functools.partial(middle_kernel, plan), out_shape=pltpu.VM...  1.35 us
  transfers between devices with their start and end apart: 7, of which 2 were waited for; matrix products, arithmetic and copies ran while one was open for 1% of the time, Pallas kernels for 34%

profile of v11, /device:TPU:0, one launch (start us, length us, event | category | flops | bytes accessed | tf_op | source)
XLA Modules:
  0.0 37.2 jit_solution(10960523096704174576)
XLA Ops:
  0.0 1.7 %pack.1 = (f32[128,1536]{1,0:T(8,128)S(1)}, s32[24,27]{1,0:T(8,128)S(1)}, f32[64,1664]{1,0:T(8,128)S(1)}, f32[128,896]{1,0:T(8,128)S(1)}) custom-call(f32[1536,128]{1,0:T(8,128)} %natural.1, s32[24,27]{1,0:T(8,128)} %codes.1), custom_call_target="tpu_custom_call" | custom-call | tf_op jit(solution)/shard_map/pack/pallas_call | solution.py:167
  1.7 3.0 %collective-permute-start = (s32[1,8]{1,0:T(1,128)}, s32[1,8]{1,0:T(1,128)S(1)}, u32[]{:S(2)}, u32[]{:S(2)}) collective-permute-start(s32[1,8]{1,0:T(1,128)} %param.7), channel_id=1, source_target_pairs={{0,4},{1,5},{2,6},{3,7},{4,0},{5,1},{6,2},{7,3},{8,12},{9,13},{10,... | collective-permute-start | bytes 104 | tf_op jit(solution)/shard_map/ppermute | solution.py:22
  4.8 3.6 %collective-permute-start.2 = (f32[64,1664]{1,0:T(8,128)S(1)}, f32[64,1664]{1,0:T(8,128)S(1)}, u32[]{:S(2)}, u32[]{:S(2)}) collective-permute-start(f32[64,1664]{1,0:T(8,128)S(1)} %get-tuple-element.24), channel_id=1, source_target_pairs={{0,31},{1,2},{2,1},{3,4},{4,3},{5,6},{6,5},{7,8},{8,7},{9,10},{10,... | collective-permute-start | bytes 1277960 | tf_op jit(solution)/shard_map/ppermute | solution.py:28
  8.4 0.0 collective-permute-done.asked.listed
  8.4 0.8 %far.1 = f32[128,512]{1,0:T(8,128)S(1)} custom-call(s32[1,8]{1,0:T(1,128)S(1)} %collective-permute-done.asked.listed, f32[128,1536]{1,0:T(8,128)S(1)} %get-tuple-element.19.turned.vectors.own.start), custom_call_target="tpu_custom_call" | custom-call | tf_op jit(solution)/shard_map/far/pallas_call | solution.py:193
  9.2 0.1 collective-permute-start.1
  9.3 0.0 collective-permute-start.3
  9.4 0.1 copy.5
  9.4 0.2 select_reduce_fusion
  9.6 7.4 %band.1 = (bf16[12,2432,256]{2,1,0:T(8,128)(2,1)S(1)}, f32[128,1536]{1,0:T(8,128)S(1)}) custom-call(s32[24,60]{1,0:T(8,128)S(1)} %broadcast_add_fusion.table, f32[1728,1536]{1,0:T(8,128)} %bitcast.1, f32[128,1536]{1,0:T(8,128)S(1)} %get-tuple-element.19.turned.vectors.own.start), custom_call_target="tpu_custom_call" | custom-call | bytes 21233664 | tf_op jit(solution)/shard_map/band/pallas_call | solution.py:279
  17.0 0.0 collective-permute-done.2.away
  17.0 0.0 collective-permute-done.3.near
  17.0 1.4 %middle.1.inner = f32[128,1536]{1,0:T(8,128)S(1)} custom-call(f32[64,1664]{1,0:T(8,128)S(1)} %collective-permute-done.2.away, f32[128,896]{1,0:T(8,128)S(1)} %collective-permute-done.3.near, bf16[12,2432,256]{2,1,0:T(8,128)(2,1)S(1)} %get-tuple-element.23.band, f32[128,1536]{1,0:T(8,128)S(1)} %get-tuple-element.27.inner), custom_call_target="tpu_custom_call" | custom-call | flops 2415919104 | tf_op jit(solution)/shard_map/middle/pallas_call | solution.py:338
  18.4 1.6 %collective-permute-done.1.far = f32[128,512]{1,0:T(8,128)S(1)} collective-permute-done((f32[128,512]{1,0:T(8,128)S(1)}, f32[128,512]{1,0:T(8,128)S(1)}, u32[]{:S(2)}, u32[]{:S(2)}) %collective-permute-start.1) | collective-permute-done | bytes 262176 | tf_op jit(solution)/shard_map/ppermute | solution.py:22
  20.0 1.3 %first.1 = (f32[128,1536]{1,0:T(8,128)S(1)}, f32[128,512]{1,0:T(8,128)S(1)}, f32[64,1664]{1,0:T(8,128)S(1)}, f32[128,896]{1,0:T(8,128)S(1)}) custom-call(s32[1,8]{1,0:T(1,128)S(1)} %collective-permute-done.asked.listed, f32[128,512]{1,0:T(8,128)S(1)} %collective-permute-done.1.far, bf16[12,2432,256]{2,1,0:T(8,128)(2,1)S(1)} %get-tuple-element.23.band, ...), custom_call_target="tpu_custom_call" | custom-call | flops 603979776 | tf_op jit(solution)/shard_map/first/pallas_call | solution.py:416
  21.3 0.1 collective-permute-start.6
  21.3 1.1 %collective-permute-start.5 = (f32[128,512]{1,0:T(8,128)S(1)}, f32[128,512]{1,0:T(8,128)S(1)}, u32[]{:S(2)}, u32[]{:S(2)}) collective-permute-start(f32[128,512]{1,0:T(8,128)S(1)} %get-tuple-element.29), channel_id=1, source_target_pairs={{0,4},{1,5},{2,6},{3,7},{4,0},{5,1},{6,2},{7,3},{8,12},{9,13},{10,... | collective-permute-start | bytes 786440 | tf_op jit(solution)/shard_map/ppermute | solution.py:22
  22.4 3.7 %collective-permute-start.4 = (f32[64,1664]{1,0:T(8,128)S(1)}, f32[64,1664]{1,0:T(8,128)S(1)}, u32[]{:S(2)}, u32[]{:S(2)}) collective-permute-start(f32[64,1664]{1,0:T(8,128)S(1)} %get-tuple-element.28), channel_id=1, source_target_pairs={{0,31},{1,2},{2,1},{3,4},{4,3},{5,6},{6,5},{7,8},{8,7},{9,10},{10,... | collective-permute-start | bytes 1277960 | tf_op jit(solution)/shard_map/ppermute | solution.py:28
  26.1 0.0 collective-permute-done.6.near
  26.2 3.0 %inner.1 = f32[128,1536]{1,0:T(8,128)S(1)} custom-call(f32[128,1536]{1,0:T(8,128)S(1)} %get-tuple-element.30.vectors.own, f32[128,896]{1,0:T(8,128)S(1)} %collective-permute-done.6.near, bf16[12,2432,256]{2,1,0:T(8,128)(2,1)S(1)} %get-tuple-element.23.band), custom_call_target="tpu_custom_call" | custom-call | flops 2415919104 | tf_op jit(solution)/shard_map/inner/pallas_call | solution.py:360
  29.1 5.5 %collective-permute-done.5.far = f32[128,512]{1,0:T(8,128)S(1)} collective-permute-done((f32[128,512]{1,0:T(8,128)S(1)}, f32[128,512]{1,0:T(8,128)S(1)}, u32[]{:S(2)}, u32[]{:S(2)}) %collective-permute-start.5) | collective-permute-done | bytes 262176 | tf_op jit(solution)/shard_map/ppermute | solution.py:22
  34.7 0.0 collective-permute-done.4.away
  34.7 2.5 %second.1 = f32[1536,128]{1,0:T(8,128)} custom-call(f32[64,1664]{1,0:T(8,128)S(1)} %collective-permute-done.4.away, bf16[256,512]{1,0:T(8,128)(2,1)S(1)} %split.1.far, bf16[12,2432,256]{2,1,0:T(8,128)(2,1)S(1)} %get-tuple-element.23.band, f32[128,1536]{1,0:T(8,128)S(1)} %inner.1, f32[128,1536]{1,0:T(8,128)S(1)} %get-tuple-element.30.vectors.own, ...), custom_call_target="tpu_custom_call" | custom-call | flops 603979776 | tf_op jit(solution)/shard_map/second/pallas_call | solution.py:453
  (4 shorter events, 0.1 us)
Async XLA Ops:
  1.7 6.7 %collective-permute-start = (s32[1,8]{1,0:T(1,128)}, s32[1,8]{1,0:T(1,128)S(1)}, u32[]{:S(2)}, u32[]{:S(2)}) collective-permute-start(s32[1,8]{1,0:T(1,128)} %param.7), channel_id=1, source_target_pairs={{0,4},{1,5},{2,6},{3,7},{4,0},{5,1},{6,2},{7,3},{8,12},{9,13},{10,... | collective-permute-start | bytes 104 | tf_op jit(solution)/shard_map/ppermute | solution.py:22
  4.8 12.3 %collective-permute-start.2 = (f32[64,1664]{1,0:T(8,128)S(1)}, f32[64,1664]{1,0:T(8,128)S(1)}, u32[]{:S(2)}, u32[]{:S(2)}) collective-permute-start(f32[64,1664]{1,0:T(8,128)S(1)} %get-tuple-element.24), channel_id=1, source_target_pairs={{0,31},{1,2},{2,1},{3,4},{4,3},{5,6},{6,5},{7,8},{8,7},{9,10},{10,... | collective-permute-start | bytes 1277960 | tf_op jit(solution)/shard_map/ppermute | solution.py:28
  9.2 10.8 %collective-permute-start.1 = (f32[128,512]{1,0:T(8,128)S(1)}, f32[128,512]{1,0:T(8,128)S(1)}, u32[]{:S(2)}, u32[]{:S(2)}) collective-permute-start(f32[128,512]{1,0:T(8,128)S(1)} %far.1), channel_id=1, source_target_pairs={{0,4},{1,5},{2,6},{3,7},{4,0},{5,1},{6,2},{7,3},{8,12},{9,13},{10,... | collective-permute-start | bytes 786440 | tf_op jit(solution)/shard_map/ppermute | solution.py:22
  9.3 7.8 %collective-permute-start.3 = (f32[128,896]{1,0:T(8,128)S(1)}, f32[128,896]{1,0:T(8,128)S(1)}, u32[]{:S(2)}, u32[]{:S(2)}) collective-permute-start(f32[128,896]{1,0:T(8,128)S(1)} %get-tuple-element.26), channel_id=1, source_target_pairs={{0,1},{1,0},{2,3},{3,2},{4,5},{5,4},{6,7},{7,6},{8,9},{9,8},{10,11... | collective-permute-start | bytes 1376264 | tf_op jit(solution)/shard_map/ppermute | solution.py:22
  21.3 4.9 %collective-permute-start.6 = (f32[128,896]{1,0:T(8,128)S(1)}, f32[128,896]{1,0:T(8,128)S(1)}, u32[]{:S(2)}, u32[]{:S(2)}) collective-permute-start(f32[128,896]{1,0:T(8,128)S(1)} %get-tuple-element.31), channel_id=1, source_target_pairs={{0,1},{1,0},{2,3},{3,2},{4,5},{5,4},{6,7},{7,6},{8,9},{9,8},{10,11... | collective-permute-start | bytes 1376264 | tf_op jit(solution)/shard_map/ppermute | solution.py:22
  21.3 13.3 %collective-permute-start.5 = (f32[128,512]{1,0:T(8,128)S(1)}, f32[128,512]{1,0:T(8,128)S(1)}, u32[]{:S(2)}, u32[]{:S(2)}) collective-permute-start(f32[128,512]{1,0:T(8,128)S(1)} %get-tuple-element.29), channel_id=1, source_target_pairs={{0,4},{1,5},{2,6},{3,7},{4,0},{5,1},{6,2},{7,3},{8,12},{9,13},{10,... | collective-permute-start | bytes 786440 | tf_op jit(solution)/shard_map/ppermute | solution.py:22
  22.4 12.2 %collective-permute-start.4 = (f32[64,1664]{1,0:T(8,128)S(1)}, f32[64,1664]{1,0:T(8,128)S(1)}, u32[]{:S(2)}, u32[]{:S(2)}) collective-permute-start(f32[64,1664]{1,0:T(8,128)S(1)} %get-tuple-element.28), channel_id=1, source_target_pairs={{0,31},{1,2},{2,1},{3,4},{4,3},{5,6},{6,5},{7,8},{8,7},{9,10},{10,... | collective-permute-start | bytes 1277960 | tf_op jit(solution)/shard_map/ppermute | solution.py:28

commit v12 on v11

--- a/solution.py
+++ b/solution.py
@@ -142,20 +142,21 @@
     step = count * tile
 
     def fetch(c):
+        at = pl.multiple_of((c + side[0] * (chunks - 1 - 2 * c)) * step, step)
         return pltpu.make_async_copy(
-            natural.at[pl.ds(c * step, step), :],
-            staged.at[pl.ds(c * step, step), :],
-            sems.at[c],
+            natural.at[pl.ds(at, step), :], staged.at[pl.ds(c * step, step), :], sems.at[c]
         )
 
     for c in range(chunks):
         fetch(c).start()
     copy = pltpu.make_async_copy(codes, held, sems.at[chunks])
     copy.start()
-    for c in range(chunks):
-        fetch(c).wait()
     for t in range(plan.pairs):
-        at = pl.multiple_of(plan.mirrored(t, side) * tile, tile)
+        c, u = t // count, t % count
+        if u == 0:
+            fetch(c).wait()
+        at = c * step + (u + side[0] * (count - 1 - 2 * u)) * tile
+        at = pl.multiple_of(at, tile)
         value = staged[pl.ds(at, tile), :].T
         turned[:, t * tile : (t + 1) * tile] = value
         write_sends(plan, side, t * tile, value, *sends)
@@ -432,12 +433,15 @@
 def second_kernel(plan, away, far, band, inner, own, start, out, halves, held, sems):
     side = parity()
     put_halves(plan, halves, away_tiles(plan, side, away))
+    halves[:, plan.edge :] = far[...]
     copies = []
-    for p in range(plan.pairs):
+    for p in reversed(range(plan.pairs)):
         lanes = slice(p * plan.tile, (p + 1) * plan.tile)
         product = inner[:, lanes] - CENTER * own[:, lanes]
-        product += message_product(plan, "far", p, far, band)
-        product += message_product(plan, "away", p, halves, band)
+        begin = plan.outer_range(p)[0] * plan.tile
+        vectors = far[...] if begin == plan.edge else halves[:, begin:]
+        rows = band[p, : vectors.shape[1], :]
+        product += fold(jnp.dot(vectors, rows, preferred_element_type=F32))
         term = 2.0 / HALF_WIDTH * product - start[:, lanes]
         place = pl.multiple_of(plan.mirrored(p, side) * plan.tile, plan.tile)
         held[p] = term.T
@@ -456,7 +460,7 @@
         in_specs=[VMEM] * 6,
         out_specs=HBM,
         scratch_shapes=[
-            halves_scratch(plan, plan.near),
+            halves_scratch(plan, plan.near + plan.far),
             pltpu.VMEM((plan.pairs, plan.tile, plan.width), F32),
             pltpu.SemaphoreType.DMA((plan.pairs,)),
         ],

time: 37.3 us -> 37.2 us (level)
  no operation moved by 1% of the time
where the time goes in v12:
time: 37.2 us; the launch traced here: 37 us
  Pallas kernels  17.8 us (48%)
  starting transfers between devices  11.7 us (31%)
  waiting for transfers between devices  7.11 us (19%)
    pallas_call x1, Pallas kernels, make_band(): pl.pallas_call(functools.partial(band_kernel, plan, depth), out_shape=[pl...  7.37 us
    ppermute x2, starting transfers between devices, swap_chips(): return lax.ppermute(value, axis, pairs)  7.34 us
    ppermute x5, waiting for transfers between devices, partner(): return lax.ppermute(value, axis, pairs)  7.11 us
    ppermute x5, starting transfers between devices, partner(): return lax.ppermute(value, axis, pairs)  4.36 us
    pallas_call x1, Pallas kernels, run_inner(): pl.pallas_call(functools.partial(inner_kernel, plan), out_shape=pltpu.VME...  2.95 us
    pallas_call x1, Pallas kernels, run_second(): pl.pallas_call(functools.partial(second_kernel, plan), out_shape=jax.Shap...  2.49 us
    pallas_call x1, Pallas kernels, pack(): pl.pallas_call(functools.partial(pack_kernel, plan, chunks), out_shape=[p...  1.6 us
    pallas_call x1, Pallas kernels, run_middle(): pl.pallas_call(functools.partial(middle_kernel, plan), out_shape=pltpu.VM...  1.35 us
  transfers between devices with their start and end apart: 7, of which 2 were waited for; matrix products, arithmetic and copies ran while one was open for 1% of the time, Pallas kernels for 34%

profile of v12, /device:TPU:0, one launch (start us, length us, event | category | flops | bytes accessed | tf_op | source)
XLA Modules:
  0.0 37.0 jit_solution(9536709165948587090)
XLA Ops:
  0.0 1.6 %pack.1 = (f32[128,1536]{1,0:T(8,128)S(1)}, s32[24,27]{1,0:T(8,128)S(1)}, f32[64,1664]{1,0:T(8,128)S(1)}, f32[128,896]{1,0:T(8,128)S(1)}) custom-call(f32[1536,128]{1,0:T(8,128)} %natural.1, s32[24,27]{1,0:T(8,128)} %codes.1), custom_call_target="tpu_custom_call" | custom-call | tf_op jit(solution)/shard_map/pack/pallas_call | solution.py:168
  1.6 3.0 %collective-permute-start = (s32[1,8]{1,0:T(1,128)}, s32[1,8]{1,0:T(1,128)S(1)}, u32[]{:S(2)}, u32[]{:S(2)}) collective-permute-start(s32[1,8]{1,0:T(1,128)} %param.7), channel_id=1, source_target_pairs={{0,4},{1,5},{2,6},{3,7},{4,0},{5,1},{6,2},{7,3},{8,12},{9,13},{10,... | collective-permute-start | bytes 104 | tf_op jit(solution)/shard_map/ppermute | solution.py:22
  4.6 3.6 %collective-permute-start.2 = (f32[64,1664]{1,0:T(8,128)S(1)}, f32[64,1664]{1,0:T(8,128)S(1)}, u32[]{:S(2)}, u32[]{:S(2)}) collective-permute-start(f32[64,1664]{1,0:T(8,128)S(1)} %get-tuple-element.24), channel_id=1, source_target_pairs={{0,31},{1,2},{2,1},{3,4},{4,3},{5,6},{6,5},{7,8},{8,7},{9,10},{10,... | collective-permute-start | bytes 1277960 | tf_op jit(solution)/shard_map/ppermute | solution.py:28
  8.3 0.0 collective-permute-done.asked.listed
  8.3 0.8 %far.1 = f32[128,512]{1,0:T(8,128)S(1)} custom-call(s32[1,8]{1,0:T(1,128)S(1)} %collective-permute-done.asked.listed, f32[128,1536]{1,0:T(8,128)S(1)} %get-tuple-element.19.turned.vectors.own.start), custom_call_target="tpu_custom_call" | custom-call | tf_op jit(solution)/shard_map/far/pallas_call | solution.py:194
  9.0 0.1 collective-permute-start.1
  9.1 0.0 collective-permute-start.3
  9.2 0.1 copy.5
  9.3 0.2 select_reduce_fusion
  9.5 7.4 %band.1 = (bf16[12,2432,256]{2,1,0:T(8,128)(2,1)S(1)}, f32[128,1536]{1,0:T(8,128)S(1)}) custom-call(s32[24,60]{1,0:T(8,128)S(1)} %broadcast_add_fusion.table, f32[1728,1536]{1,0:T(8,128)} %bitcast.1, f32[128,1536]{1,0:T(8,128)S(1)} %get-tuple-element.19.turned.vectors.own.start), custom_call_target="tpu_custom_call" | custom-call | bytes 21233664 | tf_op jit(solution)/shard_map/band/pallas_call | solution.py:280
  16.9 0.0 collective-permute-done.2.away
  16.9 0.0 collective-permute-done.3.near
  16.9 1.3 %middle.1.inner = f32[128,1536]{1,0:T(8,128)S(1)} custom-call(f32[64,1664]{1,0:T(8,128)S(1)} %collective-permute-done.2.away, f32[128,896]{1,0:T(8,128)S(1)} %collective-permute-done.3.near, bf16[12,2432,256]{2,1,0:T(8,128)(2,1)S(1)} %get-tuple-element.23.band, f32[128,1536]{1,0:T(8,128)S(1)} %get-tuple-element.27.inner), custom_call_target="tpu_custom_call" | custom-call | flops 2415919104 | tf_op jit(solution)/shard_map/middle/pallas_call | solution.py:339
  18.3 1.6 %collective-permute-done.1.far = f32[128,512]{1,0:T(8,128)S(1)} collective-permute-done((f32[128,512]{1,0:T(8,128)S(1)}, f32[128,512]{1,0:T(8,128)S(1)}, u32[]{:S(2)}, u32[]{:S(2)}) %collective-permute-start.1) | collective-permute-done | bytes 262176 | tf_op jit(solution)/shard_map/ppermute | solution.py:22
  19.9 1.3 %first.1 = (f32[128,1536]{1,0:T(8,128)S(1)}, f32[128,512]{1,0:T(8,128)S(1)}, f32[64,1664]{1,0:T(8,128)S(1)}, f32[128,896]{1,0:T(8,128)S(1)}) custom-call(s32[1,8]{1,0:T(1,128)S(1)} %collective-permute-done.asked.listed, f32[128,512]{1,0:T(8,128)S(1)} %collective-permute-done.1.far, bf16[12,2432,256]{2,1,0:T(8,128)(2,1)S(1)} %get-tuple-element.23.band, ...), custom_call_target="tpu_custom_call" | custom-call | flops 603979776 | tf_op jit(solution)/shard_map/first/pallas_call | solution.py:417
  21.1 0.1 collective-permute-start.6
  21.2 1.1 %collective-permute-start.5 = (f32[128,512]{1,0:T(8,128)S(1)}, f32[128,512]{1,0:T(8,128)S(1)}, u32[]{:S(2)}, u32[]{:S(2)}) collective-permute-start(f32[128,512]{1,0:T(8,128)S(1)} %get-tuple-element.29), channel_id=1, source_target_pairs={{0,4},{1,5},{2,6},{3,7},{4,0},{5,1},{6,2},{7,3},{8,12},{9,13},{10,... | collective-permute-start | bytes 786440 | tf_op jit(solution)/shard_map/ppermute | solution.py:22
  22.3 3.7 %collective-permute-start.4 = (f32[64,1664]{1,0:T(8,128)S(1)}, f32[64,1664]{1,0:T(8,128)S(1)}, u32[]{:S(2)}, u32[]{:S(2)}) collective-permute-start(f32[64,1664]{1,0:T(8,128)S(1)} %get-tuple-element.28), channel_id=1, source_target_pairs={{0,31},{1,2},{2,1},{3,4},{4,3},{5,6},{6,5},{7,8},{8,7},{9,10},{10,... | collective-permute-start | bytes 1277960 | tf_op jit(solution)/shard_map/ppermute | solution.py:28
  26.0 0.0 collective-permute-done.6.near
  26.0 3.0 %inner.1 = f32[128,1536]{1,0:T(8,128)S(1)} custom-call(f32[128,1536]{1,0:T(8,128)S(1)} %get-tuple-element.30.vectors.own, f32[128,896]{1,0:T(8,128)S(1)} %collective-permute-done.6.near, bf16[12,2432,256]{2,1,0:T(8,128)(2,1)S(1)} %get-tuple-element.23.band), custom_call_target="tpu_custom_call" | custom-call | flops 2415919104 | tf_op jit(solution)/shard_map/inner/pallas_call | solution.py:361
  29.0 5.5 %collective-permute-done.5.far = f32[128,512]{1,0:T(8,128)S(1)} collective-permute-done((f32[128,512]{1,0:T(8,128)S(1)}, f32[128,512]{1,0:T(8,128)S(1)}, u32[]{:S(2)}, u32[]{:S(2)}) %collective-permute-start.5) | collective-permute-done | bytes 262176 | tf_op jit(solution)/shard_map/ppermute | solution.py:22
  34.6 0.0 collective-permute-done.4.away
  34.6 2.5 %second.1 = f32[1536,128]{1,0:T(8,128)} custom-call(f32[64,1664]{1,0:T(8,128)S(1)} %collective-permute-done.4.away, bf16[256,512]{1,0:T(8,128)(2,1)S(1)} %split.1.far, bf16[12,2432,256]{2,1,0:T(8,128)(2,1)S(1)} %get-tuple-element.23.band, f32[128,1536]{1,0:T(8,128)S(1)} %inner.1, f32[128,1536]{1,0:T(8,128)S(1)} %get-tuple-element.30.vectors.own, ...), custom_call_target="tpu_custom_call" | custom-call | flops 603979776 | tf_op jit(solution)/shard_map/second/pallas_call | solution.py:457
  (4 shorter events, 0.1 us)
Async XLA Ops:
  1.6 6.7 %collective-permute-start = (s32[1,8]{1,0:T(1,128)}, s32[1,8]{1,0:T(1,128)S(1)}, u32[]{:S(2)}, u32[]{:S(2)}) collective-permute-start(s32[1,8]{1,0:T(1,128)} %param.7), channel_id=1, source_target_pairs={{0,4},{1,5},{2,6},{3,7},{4,0},{5,1},{6,2},{7,3},{8,12},{9,13},{10,... | collective-permute-start | bytes 104 | tf_op jit(solution)/shard_map/ppermute | solution.py:22
  4.6 12.3 %collective-permute-start.2 = (f32[64,1664]{1,0:T(8,128)S(1)}, f32[64,1664]{1,0:T(8,128)S(1)}, u32[]{:S(2)}, u32[]{:S(2)}) collective-permute-start(f32[64,1664]{1,0:T(8,128)S(1)} %get-tuple-element.24), channel_id=1, source_target_pairs={{0,31},{1,2},{2,1},{3,4},{4,3},{5,6},{6,5},{7,8},{8,7},{9,10},{10,... | collective-permute-start | bytes 1277960 | tf_op jit(solution)/shard_map/ppermute | solution.py:28
  9.0 10.8 %collective-permute-start.1 = (f32[128,512]{1,0:T(8,128)S(1)}, f32[128,512]{1,0:T(8,128)S(1)}, u32[]{:S(2)}, u32[]{:S(2)}) collective-permute-start(f32[128,512]{1,0:T(8,128)S(1)} %far.1), channel_id=1, source_target_pairs={{0,4},{1,5},{2,6},{3,7},{4,0},{5,1},{6,2},{7,3},{8,12},{9,13},{10,... | collective-permute-start | bytes 786440 | tf_op jit(solution)/shard_map/ppermute | solution.py:22
  9.1 7.8 %collective-permute-start.3 = (f32[128,896]{1,0:T(8,128)S(1)}, f32[128,896]{1,0:T(8,128)S(1)}, u32[]{:S(2)}, u32[]{:S(2)}) collective-permute-start(f32[128,896]{1,0:T(8,128)S(1)} %get-tuple-element.26), channel_id=1, source_target_pairs={{0,1},{1,0},{2,3},{3,2},{4,5},{5,4},{6,7},{7,6},{8,9},{9,8},{10,11... | collective-permute-start | bytes 1376264 | tf_op jit(solution)/shard_map/ppermute | solution.py:22
  21.1 4.9 %collective-permute-start.6 = (f32[128,896]{1,0:T(8,128)S(1)}, f32[128,896]{1,0:T(8,128)S(1)}, u32[]{:S(2)}, u32[]{:S(2)}) collective-permute-start(f32[128,896]{1,0:T(8,128)S(1)} %get-tuple-element.31), channel_id=1, source_target_pairs={{0,1},{1,0},{2,3},{3,2},{4,5},{5,4},{6,7},{7,6},{8,9},{9,8},{10,11... | collective-permute-start | bytes 1376264 | tf_op jit(solution)/shard_map/ppermute | solution.py:22
  21.2 13.3 %collective-permute-start.5 = (f32[128,512]{1,0:T(8,128)S(1)}, f32[128,512]{1,0:T(8,128)S(1)}, u32[]{:S(2)}, u32[]{:S(2)}) collective-permute-start(f32[128,512]{1,0:T(8,128)S(1)} %get-tuple-element.29), channel_id=1, source_target_pairs={{0,4},{1,5},{2,6},{3,7},{4,0},{5,1},{6,2},{7,3},{8,12},{9,13},{10,... | collective-permute-start | bytes 786440 | tf_op jit(solution)/shard_map/ppermute | solution.py:22
  22.3 12.2 %collective-permute-start.4 = (f32[64,1664]{1,0:T(8,128)S(1)}, f32[64,1664]{1,0:T(8,128)S(1)}, u32[]{:S(2)}, u32[]{:S(2)}) collective-permute-start(f32[64,1664]{1,0:T(8,128)S(1)} %get-tuple-element.28), channel_id=1, source_target_pairs={{0,31},{1,2},{2,1},{3,4},{4,3},{5,6},{6,5},{7,8},{8,7},{9,10},{10,... | collective-permute-start | bytes 1277960 | tf_op jit(solution)/shard_map/ppermute | solution.py:28

commit v13 on v12

--- a/solution.py
+++ b/solution.py
@@ -348,26 +348,43 @@
     )(away, near, band, inner)
 
 
-def inner_kernel(plan, vectors, near, band, out, halves, near_halves):
+def inner_kernel(plan, vectors, band, out, halves):
     own_halves(plan, vectors, halves)
-    put_halves(plan, near_halves, near_tiles(plan, near))
     for p in range(plan.pairs):
-        total = own_product(plan, p, halves, band)
-        total += message_product(plan, "near", p, near_halves, band)
-        out[:, p * plan.tile : (p + 1) * plan.tile] = total
-
-
-def run_inner(plan, vectors, near, band):
+        out[:, p * plan.tile : (p + 1) * plan.tile] = own_product(plan, p, halves, band)
+
+
+def run_inner(plan, vectors, band):
     return pl.pallas_call(
         functools.partial(inner_kernel, plan),
+        out_shape=pltpu.VMEM((plan.width, plan.rows), F32),
+        in_specs=[VMEM] * 2,
+        out_specs=VMEM,
+        scratch_shapes=[halves_scratch(plan, plan.pairs)],
+        compiler_params=params(8),
+        cost_estimate=cost(8 * plan.width * plan.rows**2, 0),
+        name="inner",
+    )(vectors, band)
+
+
+def near_kernel(plan, near, band, inner, out, halves):
+    put_halves(plan, halves, near_tiles(plan, near))
+    for p in range(plan.pairs):
+        lanes = slice(p * plan.tile, (p + 1) * plan.tile)
+        out[:, lanes] = inner[:, lanes] + message_product(plan, "near", p, halves, band)
+
+
+def add_near(plan, near, band, inner):
+    return pl.pallas_call(
+        functools.partial(near_kernel, plan),
         out_shape=pltpu.VMEM((plan.width, plan.rows), F32),
         in_specs=[VMEM] * 3,
         out_specs=VMEM,
-        scratch_shapes=[halves_scratch(plan, plan.pairs), halves_scratch(plan, plan.near)],
-        compiler_params=params(8),
-        cost_estimate=cost(8 * plan.width * plan.rows**2, 0),
-        name="inner",
-    )(vectors, near, band)
+        scratch_shapes=[halves_scratch(plan, plan.near)],
+        compiler_params=params(8),
+        cost_estimate=cost(2 * plan.width * plan.rows**2, 0),
+        name="near",
+    )(near, band, inner)
 
 
 def far_tiles(plan, far):
@@ -527,9 +544,13 @@
     band, inner = make_band(plan, inverse, hamiltonian.T, start)
 
     inner = run_middle(plan, away, near, band, inner)
-    value, listed, *sends = run_first(plan, asked, far, band, inner, start)
-    away, far, near = exchange(listed, sends)
-    inner = run_inner(plan, value, near, band)
+    value, listed, to_away, to_near = run_first(plan, asked, far, band, inner, start)
+    far, away = partner(listed, "rows", swap_level), swap_chips(to_away, "rows")
+    inner = run_inner(plan, value, band)
+    cores = [[i, i + 1] for i in range(0, device_count, 2)]
+    both = lax.all_gather(to_near, "rows", axis_index_groups=cores)
+    near = lax.dynamic_index_in_dim(both, 1 - side[0], keepdims=False)
+    inner = add_near(plan, near, band, inner)
     far = split_far(plan, after(far, inner))
     return run_second(plan, away, far, band, inner, value, start)
 

time: 37.2 us -> 38.1 us (1.024)
  blocking collectives: 0 us -> 2.63 us
  starting transfers between devices: 11.7 us -> 10.1 us
  waiting for transfers between devices: 7.11 us -> 6.64 us
    all_gather x0 -> x1, blocking collectives: none -> 2.63 us  [per_device(): both = lax.all_gather(to_near, 'rows', axis_index_groups=cores)]
    ppermute x5 -> x4, starting transfers between devices: 4.36 us -> 3.18 us  [partner(): return lax.ppermute(value, axis, pairs)]
    pallas_call x0 -> x1, Pallas kernels: none -> 0.76 us  [add_near(): pl.pallas_call(functools.partial(near_kernel, plan), out_shape=pltpu.VMEM...]
    pallas_call x1, Pallas kernels: 2.95 us -> 2.37 us  [run_inner(): pl.pallas_call(functools.partial(inner_kernel, plan), out_shape=pltpu.VME...]
    ppermute x5 -> x4, waiting for transfers between devices: 7.11 us -> 6.64 us  [partner(): return lax.ppermute(value, axis, pairs)]
    ppermute x2, starting transfers between devices: 7.34 us -> 6.9 us  [swap_chips(): return lax.ppermute(value, axis, pairs)]
  transfers between devices with their start and end apart: 7 -> 6, of which waited for: 2 -> 2; matrix products, arithmetic and copies ran while one was open for 1% -> 1% of each run, Pallas kernels for 34% -> 33%
where the time goes in v13:
time: 38.1 us; the launch traced here: 38 us
  Pallas kernels  18 us (47%)
  starting transfers between devices  10.1 us (27%)
  waiting for transfers between devices  6.64 us (17%)
  blocking collectives  2.63 us (7%)
    pallas_call x1, Pallas kernels, make_band(): pl.pallas_call(functools.partial(band_kernel, plan, depth), out_shape=[pl...  7.37 us
    ppermute x2, starting transfers between devices, swap_chips(): return lax.ppermute(value, axis, pairs)  6.9 us
    ppermute x4, waiting for transfers between devices, partner(): return lax.ppermute(value, axis, pairs)  6.64 us
    ppermute x4, starting transfers between devices, partner(): return lax.ppermute(value, axis, pairs)  3.18 us
    all_gather x1, blocking collectives, per_device(): both = lax.all_gather(to_near, 'rows', axis_index_groups=cores)  2.63 us
    pallas_call x1, Pallas kernels, run_second(): pl.pallas_call(functools.partial(second_kernel, plan), out_shape=jax.Shap...  2.51 us
    pallas_call x1, Pallas kernels, run_inner(): pl.pallas_call(functools.partial(inner_kernel, plan), out_shape=pltpu.VME...  2.37 us
    pallas_call x1, Pallas kernels, pack(): pl.pallas_call(functools.partial(pack_kernel, plan, chunks), out_shape=[p...  1.6 us
  transfers between devices with their start and end apart: 6, of which 2 were waited for; matrix products, arithmetic and copies ran while one was open for 1% of the time, Pallas kernels for 33%

profile of v13, /device:TPU:0, one launch (start us, length us, event | category | flops | bytes accessed | tf_op | source)
XLA Modules:
  0.0 38.0 jit_solution(16424839648691604562)
XLA Ops:
  0.0 1.6 %pack.1 = (f32[128,1536]{1,0:T(8,128)S(1)}, s32[24,27]{1,0:T(8,128)S(1)}, f32[64,1664]{1,0:T(8,128)S(1)}, f32[128,896]{1,0:T(8,128)S(1)}) custom-call(f32[1536,128]{1,0:T(8,128)} %natural.1, s32[24,27]{1,0:T(8,128)} %codes.1), custom_call_target="tpu_custom_call" | custom-call | tf_op jit(solution)/shard_map/pack/pallas_call | solution.py:168
  1.6 3.0 %collective-permute-start = (s32[1,8]{1,0:T(1,128)}, s32[1,8]{1,0:T(1,128)S(1)}, u32[]{:S(2)}, u32[]{:S(2)}) collective-permute-start(s32[1,8]{1,0:T(1,128)} %param.7), channel_id=1, source_target_pairs={{0,4},{1,5},{2,6},{3,7},{4,0},{5,1},{6,2},{7,3},{8,12},{9,13},{10,... | collective-permute-start | bytes 104 | tf_op jit(solution)/shard_map/ppermute | solution.py:22
  4.6 3.6 %collective-permute-start.2 = (f32[64,1664]{1,0:T(8,128)S(1)}, f32[64,1664]{1,0:T(8,128)S(1)}, u32[]{:S(2)}, u32[]{:S(2)}) collective-permute-start(f32[64,1664]{1,0:T(8,128)S(1)} %get-tuple-element.24), channel_id=1, source_target_pairs={{0,31},{1,2},{2,1},{3,4},{4,3},{5,6},{6,5},{7,8},{8,7},{9,10},{10,... | collective-permute-start | bytes 1277960 | tf_op jit(solution)/shard_map/ppermute | solution.py:28
  8.3 0.0 collective-permute-done.asked.listed
  8.3 0.8 %far.1 = f32[128,512]{1,0:T(8,128)S(1)} custom-call(s32[1,8]{1,0:T(1,128)S(1)} %collective-permute-done.asked.listed, f32[128,1536]{1,0:T(8,128)S(1)} %get-tuple-element.19.turned.vectors.own.start), custom_call_target="tpu_custom_call" | custom-call | tf_op jit(solution)/shard_map/far/pallas_call | solution.py:194
  9.0 0.1 collective-permute-start.1
  9.1 0.0 collective-permute-start.3
  9.2 0.1 copy.5
  9.3 0.2 select_reduce_fusion
  9.5 7.4 %band.1 = (bf16[12,2432,256]{2,1,0:T(8,128)(2,1)S(1)}, f32[128,1536]{1,0:T(8,128)S(1)}) custom-call(s32[24,60]{1,0:T(8,128)S(1)} %broadcast_add_fusion.table, f32[1728,1536]{1,0:T(8,128)} %bitcast.4, f32[128,1536]{1,0:T(8,128)S(1)} %get-tuple-element.19.turned.vectors.own.start), custom_call_target="tpu_custom_call" | custom-call | bytes 21233664 | tf_op jit(solution)/shard_map/band/pallas_call | solution.py:280
  16.9 0.0 collective-permute-done.2.away
  16.9 0.0 collective-permute-done.3.near
  16.9 1.4 %middle.1.inner = f32[128,1536]{1,0:T(8,128)S(1)} custom-call(f32[64,1664]{1,0:T(8,128)S(1)} %collective-permute-done.2.away, f32[128,896]{1,0:T(8,128)S(1)} %collective-permute-done.3.near, bf16[12,2432,256]{2,1,0:T(8,128)(2,1)S(1)} %get-tuple-element.23.band, f32[128,1536]{1,0:T(8,128)S(1)} %get-tuple-element.27.inner), custom_call_target="tpu_custom_call" | custom-call | flops 2415919104 | tf_op jit(solution)/shard_map/middle/pallas_call | solution.py:339
  18.3 1.6 %collective-permute-done.1.far = f32[128,512]{1,0:T(8,128)S(1)} collective-permute-done((f32[128,512]{1,0:T(8,128)S(1)}, f32[128,512]{1,0:T(8,128)S(1)}, u32[]{:S(2)}, u32[]{:S(2)}) %collective-permute-start.1) | collective-permute-done | bytes 262176 | tf_op jit(solution)/shard_map/ppermute | solution.py:22
  19.9 1.3 %first.1 = (f32[128,1536]{1,0:T(8,128)S(1)}, f32[128,512]{1,0:T(8,128)S(1)}, f32[64,1664]{1,0:T(8,128)S(1)}, f32[128,896]{1,0:T(8,128)S(1)}) custom-call(s32[1,8]{1,0:T(1,128)S(1)} %collective-permute-done.asked.listed, f32[128,512]{1,0:T(8,128)S(1)} %collective-permute-done.1.far, bf16[12,2432,256]{2,1,0:T(8,128)(2,1)S(1)} %get-tuple-element.23.band, ...), custom_call_target="tpu_custom_call" | custom-call | flops 603979776 | tf_op jit(solution)/shard_map/first/pallas_call | solution.py:434
  21.1 3.3 %collective-permute-start.4 = (f32[64,1664]{1,0:T(8,128)S(1)}, f32[64,1664]{1,0:T(8,128)S(1)}, u32[]{:S(2)}, u32[]{:S(2)}) collective-permute-start(f32[64,1664]{1,0:T(8,128)S(1)} %get-tuple-element.28), channel_id=1, source_target_pairs={{0,31},{1,2},{2,1},{3,4},{4,3},{5,6},{6,5},{7,8},{8,7},{9,10},{10,... | collective-permute-start | bytes 1277960 | tf_op jit(solution)/shard_map/ppermute | solution.py:28
  24.4 0.0 collective-permute-start.5
  24.4 2.6 %all-gather = f32[256,896]{1,0:T(8,128)S(1)} all-gather(f32[128,896]{1,0:T(8,128)S(1)} %get-tuple-element.30), channel_id=2, replica_groups={{0,1},{2,3},{4,5},{6,7},{8,9},{10,11},{12,13},{14,15},{16,17},{18,19},{..., dimensions={0}, use_global_device_ids=true | all-gather | bytes 1376256 | tf_op jit(solution)/shard_map/all_gather | solution.py:551
  27.1 2.4 %inner.1 = f32[128,1536]{1,0:T(8,128)S(1)} custom-call(f32[128,1536]{1,0:T(8,128)S(1)} %get-tuple-element.31.vectors.own, bf16[12,2432,256]{2,1,0:T(8,128)(2,1)S(1)} %get-tuple-element.23.band), custom_call_target="tpu_custom_call" | custom-call | flops 2415919104 | tf_op jit(solution)/shard_map/inner/pallas_call | solution.py:358
  29.5 0.8 %near.1.inner = f32[128,1536]{1,0:T(8,128)S(1)} custom-call(f32[128,896]{1,0:T(8,128)S(1)} %dynamic-slice_bitcast_fusion.near, bf16[12,2432,256]{2,1,0:T(8,128)(2,1)S(1)} %get-tuple-element.23.band, f32[128,1536]{1,0:T(8,128)S(1)} %inner.1), custom_call_target="tpu_custom_call" | custom-call | flops 603979776 | tf_op jit(solution)/shard_map/near/pallas_call | solution.py:378
  30.2 5.0 %collective-permute-done.5.far = f32[128,512]{1,0:T(8,128)S(1)} collective-permute-done((f32[128,512]{1,0:T(8,128)S(1)}, f32[128,512]{1,0:T(8,128)S(1)}, u32[]{:S(2)}, u32[]{:S(2)}) %collective-permute-start.5) | collective-permute-done | bytes 262176 | tf_op jit(solution)/shard_map/ppermute | solution.py:22
  35.3 0.0 collective-permute-done.4.away
  35.3 2.5 %second.1 = f32[1536,128]{1,0:T(8,128)} custom-call(f32[64,1664]{1,0:T(8,128)S(1)} %collective-permute-done.4.away, bf16[256,512]{1,0:T(8,128)(2,1)S(1)} %split.1.far, bf16[12,2432,256]{2,1,0:T(8,128)(2,1)S(1)} %get-tuple-element.23.band, f32[128,1536]{1,0:T(8,128)S(1)} %near.1.inner, f32[128,1536]{1,0:T(8,128)S(1)} %get-tuple-element.31.vectors.own, ...), custom_call_target="tpu_custom_call" | custom-call | flops 603979776 | tf_op jit(solution)/shard_map/second/pallas_call | solution.py:474
  (5 shorter events, 0.1 us)
Async XLA Ops:
  1.6 6.7 %collective-permute-start = (s32[1,8]{1,0:T(1,128)}, s32[1,8]{1,0:T(1,128)S(1)}, u32[]{:S(2)}, u32[]{:S(2)}) collective-permute-start(s32[1,8]{1,0:T(1,128)} %param.7), channel_id=1, source_target_pairs={{0,4},{1,5},{2,6},{3,7},{4,0},{5,1},{6,2},{7,3},{8,12},{9,13},{10,... | collective-permute-start | bytes 104 | tf_op jit(solution)/shard_map/ppermute | solution.py:22
  4.6 12.3 %collective-permute-start.2 = (f32[64,1664]{1,0:T(8,128)S(1)}, f32[64,1664]{1,0:T(8,128)S(1)}, u32[]{:S(2)}, u32[]{:S(2)}) collective-permute-start(f32[64,1664]{1,0:T(8,128)S(1)} %get-tuple-element.24), channel_id=1, source_target_pairs={{0,31},{1,2},{2,1},{3,4},{4,3},{5,6},{6,5},{7,8},{8,7},{9,10},{10,... | collective-permute-start | bytes 1277960 | tf_op jit(solution)/shard_map/ppermute | solution.py:28
  9.0 10.8 %collective-permute-start.1 = (f32[128,512]{1,0:T(8,128)S(1)}, f32[128,512]{1,0:T(8,128)S(1)}, u32[]{:S(2)}, u32[]{:S(2)}) collective-permute-start(f32[128,512]{1,0:T(8,128)S(1)} %far.1), channel_id=1, source_target_pairs={{0,4},{1,5},{2,6},{3,7},{4,0},{5,1},{6,2},{7,3},{8,12},{9,13},{10,... | collective-permute-start | bytes 786440 | tf_op jit(solution)/shard_map/ppermute | solution.py:22
  9.1 7.8 %collective-permute-start.3 = (f32[128,896]{1,0:T(8,128)S(1)}, f32[128,896]{1,0:T(8,128)S(1)}, u32[]{:S(2)}, u32[]{:S(2)}) collective-permute-start(f32[128,896]{1,0:T(8,128)S(1)} %get-tuple-element.26), channel_id=1, source_target_pairs={{0,1},{1,0},{2,3},{3,2},{4,5},{5,4},{6,7},{7,6},{8,9},{9,8},{10,11... | collective-permute-start | bytes 1376264 | tf_op jit(solution)/shard_map/ppermute | solution.py:22
  21.1 14.2 %collective-permute-start.4 = (f32[64,1664]{1,0:T(8,128)S(1)}, f32[64,1664]{1,0:T(8,128)S(1)}, u32[]{:S(2)}, u32[]{:S(2)}) collective-permute-start(f32[64,1664]{1,0:T(8,128)S(1)} %get-tuple-element.28), channel_id=1, source_target_pairs={{0,31},{1,2},{2,1},{3,4},{4,3},{5,6},{6,5},{7,8},{8,7},{9,10},{10,... | collective-permute-start | bytes 1277960 | tf_op jit(solution)/shard_map/ppermute | solution.py:28
  24.4 10.9 %collective-permute-start.5 = (f32[128,512]{1,0:T(8,128)S(1)}, f32[128,512]{1,0:T(8,128)S(1)}, u32[]{:S(2)}, u32[]{:S(2)}) collective-permute-start(f32[128,512]{1,0:T(8,128)S(1)} %get-tuple-element.29), channel_id=1, source_target_pairs={{0,4},{1,5},{2,6},{3,7},{4,0},{5,1},{6,2},{7,3},{8,12},{9,13},{10,... | collective-permute-start | bytes 786440 | tf_op jit(solution)/shard_map/ppermute | solution.py:22

commit v14 on v12

--- a/solution.py
+++ b/solution.py
@@ -114,7 +114,7 @@
         even = jnp.where(lane < plan.size, value[:half], turned[half:])
         odd = jnp.where(lane < plan.size, turned[:half], value[half:])
         to_away[:, at : at + tile] = jnp.where(side[0] == 0, even, odd)
-    if at >= skip:
+    if at >= skip and to_near is not None:
         to_near[:, at - skip : at - skip + tile] = value
 
 
@@ -348,26 +348,27 @@
     )(away, near, band, inner)
 
 
-def inner_kernel(plan, vectors, near, band, out, halves, near_halves):
+def inner_kernel(plan, vectors, low, high, band, out, halves, near_halves):
     own_halves(plan, vectors, halves)
-    put_halves(plan, near_halves, near_tiles(plan, near))
+    tiles = zip(near_tiles(plan, low), near_tiles(plan, high))
+    put_halves(plan, near_halves, [jnp.concatenate(pair, axis=0) for pair in tiles])
     for p in range(plan.pairs):
         total = own_product(plan, p, halves, band)
         total += message_product(plan, "near", p, near_halves, band)
         out[:, p * plan.tile : (p + 1) * plan.tile] = total
 
 
-def run_inner(plan, vectors, near, band):
+def run_inner(plan, vectors, low, high, band):
     return pl.pallas_call(
         functools.partial(inner_kernel, plan),
         out_shape=pltpu.VMEM((plan.width, plan.rows), F32),
-        in_specs=[VMEM] * 3,
+        in_specs=[VMEM] * 4,
         out_specs=VMEM,
         scratch_shapes=[halves_scratch(plan, plan.pairs), halves_scratch(plan, plan.near)],
         compiler_params=params(8),
-        cost_estimate=cost(8 * plan.width * plan.rows**2, 0),
+        cost_estimate=cost(1, 1),
         name="inner",
-    )(vectors, near, band)
+    )(vectors, low, high, band)
 
 
 def far_tiles(plan, far):
@@ -391,7 +392,7 @@
 
 
 def first_kernel(
-    plan, listed, far, band, inner, own, value, to_far, to_away, to_near, halves, asked, sem
+    plan, listed, far, band, inner, own, value, to_far, to_away, low, high, halves, asked, sem
 ):
     copy = pltpu.make_async_copy(listed, asked, sem)
     copy.start()
@@ -403,7 +404,11 @@
         product += message_product(plan, "far", p, halves, band)
         term = product * (1.0 / HALF_WIDTH)
         value[:, lanes] = term
-        write_sends(plan, side, lanes.start, term, to_away, to_near)
+        write_sends(plan, side, lanes.start, term, to_away, None)
+        at = lanes.start - plan.rows + plan.edge
+        if at >= 0:
+            low[:, at : at + plan.tile] = term[: plan.half]
+            high[:, at : at + plan.tile] = term[plan.half :]
 
     def write(at, term):
         to_far[:, at : at + plan.tile] = term
@@ -413,7 +418,8 @@
 
 
 def run_first(plan, asked, far, band, inner, own):
-    shapes = [jax.ShapeDtypeStruct(far.shape, F32)] + send_shapes(plan)
+    near = jax.ShapeDtypeStruct((plan.half, plan.edge), F32)
+    shapes = [jax.ShapeDtypeStruct(far.shape, F32), send_shapes(plan)[0], near, near]
     return pl.pallas_call(
         functools.partial(first_kernel, plan),
         out_shape=[pltpu.VMEM((plan.width, plan.rows), F32)] + shapes,
@@ -527,9 +533,10 @@
     band, inner = make_band(plan, inverse, hamiltonian.T, start)
 
     inner = run_middle(plan, away, near, band, inner)
-    value, listed, *sends = run_first(plan, asked, far, band, inner, start)
-    away, far, near = exchange(listed, sends)
-    inner = run_inner(plan, value, near, band)
+    value, listed, to_away, *to_near = run_first(plan, asked, far, band, inner, start)
+    far, away = partner(listed, "rows", swap_level), swap_chips(to_away, "rows")
+    low, high = (partner(part, "rows", 0) for part in to_near)
+    inner = run_inner(plan, value, low, high, band)
     far = split_far(plan, after(far, inner))
     return run_second(plan, away, far, band, inner, value, start)
 

time: 37.2 us -> 36.5 us (0.981); the launches traced: 37 us -> 35.8 us
  waiting for transfers between devices: 7.11 us -> 5.75 us
    ppermute x5 -> x6, waiting for transfers between devices: 7.11 us -> 3.34 us  [partner(): return lax.ppermute(value, axis, pairs)]
    ppermute x2, waiting for transfers between devices: 0.01 us -> 2.42 us  [swap_chips(): return lax.ppermute(value, axis, pairs)]
    ppermute x2, starting transfers between devices: 7.34 us -> 7.75 us  [swap_chips(): return lax.ppermute(value, axis, pairs)]
    ppermute x5 -> x6, starting transfers between devices: 4.36 us -> 4.11 us  [partner(): return lax.ppermute(value, axis, pairs)]
  transfers between devices with their start and end apart: 7 -> 8, of which waited for: 2 -> 3; matrix products, arithmetic and copies ran while one was open for 1% -> 1% of each run, Pallas kernels for 34% -> 35%
where the time goes in v14:
time: 36.5 us; the launch traced here: 35.8 us
  Pallas kernels  17.8 us (49%)
  starting transfers between devices  11.9 us (33%)
  waiting for transfers between devices  5.75 us (16%)
    ppermute x2, starting transfers between devices, swap_chips(): return lax.ppermute(value, axis, pairs)  7.75 us
    pallas_call x1, Pallas kernels, make_band(): pl.pallas_call(functools.partial(band_kernel, plan, depth), out_shape=[pl...  7.37 us
    ppermute x6, starting transfers between devices, partner(): return lax.ppermute(value, axis, pairs)  4.11 us
    ppermute x6, waiting for transfers between devices, partner(): return lax.ppermute(value, axis, pairs)  3.34 us
    pallas_call x1, Pallas kernels, run_inner(): pl.pallas_call(functools.partial(inner_kernel, plan), out_shape=pltpu.VME...  2.95 us
    pallas_call x1, Pallas kernels, run_second(): pl.pallas_call(functools.partial(second_kernel, plan), out_shape=jax.Shap...  2.49 us
    ppermute x2, waiting for transfers between devices, swap_chips(): return lax.ppermute(value, axis, pairs)  2.42 us
    pallas_call x1, Pallas kernels, pack(): pl.pallas_call(functools.partial(pack_kernel, plan, chunks), out_shape=[p...  1.6 us
  transfers between devices with their start and end apart: 8, of which 3 were waited for; matrix products, arithmetic and copies ran while one was open for 1% of the time, Pallas kernels for 35%

profile of v14, /device:TPU:0, one launch (start us, length us, event | category | flops | bytes accessed | tf_op | source)
XLA Modules:
  0.0 35.8 jit_solution(17121987155366094026)
XLA Ops:
  0.0 1.6 %pack.1 = (f32[128,1536]{1,0:T(8,128)S(1)}, s32[24,27]{1,0:T(8,128)S(1)}, f32[64,1664]{1,0:T(8,128)S(1)}, f32[128,896]{1,0:T(8,128)S(1)}) custom-call(f32[1536,128]{1,0:T(8,128)} %natural.1, s32[24,27]{1,0:T(8,128)} %codes.1), custom_call_target="tpu_custom_call" | custom-call | tf_op jit(solution)/shard_map/pack/pallas_call | solution.py:168
  1.6 3.0 %collective-permute-start = (s32[1,8]{1,0:T(1,128)}, s32[1,8]{1,0:T(1,128)S(1)}, u32[]{:S(2)}, u32[]{:S(2)}) collective-permute-start(s32[1,8]{1,0:T(1,128)} %param.7), channel_id=1, source_target_pairs={{0,4},{1,5},{2,6},{3,7},{4,0},{5,1},{6,2},{7,3},{8,12},{9,13},{10,... | collective-permute-start | bytes 104 | tf_op jit(solution)/shard_map/ppermute | solution.py:22
  4.6 3.6 %collective-permute-start.2 = (f32[64,1664]{1,0:T(8,128)S(1)}, f32[64,1664]{1,0:T(8,128)S(1)}, u32[]{:S(2)}, u32[]{:S(2)}) collective-permute-start(f32[64,1664]{1,0:T(8,128)S(1)} %get-tuple-element.25), channel_id=1, source_target_pairs={{0,31},{1,2},{2,1},{3,4},{4,3},{5,6},{6,5},{7,8},{8,7},{9,10},{10,... | collective-permute-start | bytes 1277960 | tf_op jit(solution)/shard_map/ppermute | solution.py:28
  8.3 0.0 collective-permute-done.asked.listed
  8.3 0.8 %far.1 = f32[128,512]{1,0:T(8,128)S(1)} custom-call(s32[1,8]{1,0:T(1,128)S(1)} %collective-permute-done.asked.listed, f32[128,1536]{1,0:T(8,128)S(1)} %get-tuple-element.20.turned.vectors.own.start), custom_call_target="tpu_custom_call" | custom-call | tf_op jit(solution)/shard_map/far/pallas_call | solution.py:194
  9.0 0.1 collective-permute-start.1
  9.1 0.0 collective-permute-start.3
  9.2 0.1 copy.5
  9.3 0.2 select_reduce_fusion
  9.5 7.4 %band.1 = (bf16[12,2432,256]{2,1,0:T(8,128)(2,1)S(1)}, f32[128,1536]{1,0:T(8,128)S(1)}) custom-call(s32[24,60]{1,0:T(8,128)S(1)} %broadcast_add_fusion.table, f32[1728,1536]{1,0:T(8,128)} %bitcast.1, f32[128,1536]{1,0:T(8,128)S(1)} %get-tuple-element.20.turned.vectors.own.start), custom_call_target="tpu_custom_call" | custom-call | bytes 21233664 | tf_op jit(solution)/shard_map/band/pallas_call | solution.py:280
  16.9 0.0 collective-permute-done.2.away
  16.9 0.0 collective-permute-done.3.near
  16.9 1.3 %middle.1.inner = f32[128,1536]{1,0:T(8,128)S(1)} custom-call(f32[64,1664]{1,0:T(8,128)S(1)} %collective-permute-done.2.away, f32[128,896]{1,0:T(8,128)S(1)} %collective-permute-done.3.near, bf16[12,2432,256]{2,1,0:T(8,128)(2,1)S(1)} %get-tuple-element.24.band, f32[128,1536]{1,0:T(8,128)S(1)} %get-tuple-element.28.inner), custom_call_target="tpu_custom_call" | custom-call | flops 2415919104 | tf_op jit(solution)/shard_map/middle/pallas_call | solution.py:339
  18.3 1.6 %collective-permute-done.1.far = f32[128,512]{1,0:T(8,128)S(1)} collective-permute-done((f32[128,512]{1,0:T(8,128)S(1)}, f32[128,512]{1,0:T(8,128)S(1)}, u32[]{:S(2)}, u32[]{:S(2)}) %collective-permute-start.1) | collective-permute-done | bytes 262176 | tf_op jit(solution)/shard_map/ppermute | solution.py:22
  19.9 1.3 %first.1 = (f32[128,1536]{1,0:T(8,128)S(1)}, f32[128,512]{1,0:T(8,128)S(1)}, f32[64,1664]{1,0:T(8,128)S(1)}, f32[64,896]{1,0:T(8,128)S(1)}, f32[64,896]{1,0:T(8,128)S(1)}) custom-call(s32[1,8]{1,0:T(1,128)S(1)} %collective-permute-done.asked.listed, f32[128,512]{1,0:T(8,128)S(1)} %collective-permute-done.1.far, ...), custom_call_target="tpu_custom_call" | custom-call | flops 603979776 | tf_op jit(solution)/shard_map/first/pallas_call | solution.py:423
  21.1 0.4 %collective-permute-start.5 = (f32[128,512]{1,0:T(8,128)S(1)}, f32[128,512]{1,0:T(8,128)S(1)}, u32[]{:S(2)}, u32[]{:S(2)}) collective-permute-start(f32[128,512]{1,0:T(8,128)S(1)} %get-tuple-element.30), channel_id=1, source_target_pairs={{0,4},{1,5},{2,6},{3,7},{4,0},{5,1},{6,2},{7,3},{8,12},{9,13},{10,... | collective-permute-start | bytes 786440 | tf_op jit(solution)/shard_map/ppermute | solution.py:22
  21.6 0.5 %collective-permute-start.6 = (f32[64,896]{1,0:T(8,128)S(1)}, f32[64,896]{1,0:T(8,128)S(1)}, u32[]{:S(2)}, u32[]{:S(2)}) collective-permute-start(f32[64,896]{1,0:T(8,128)S(1)} %get-tuple-element.32), channel_id=1, source_target_pairs={{0,1},{1,0},{2,3},{3,2},{4,5},{5,4},{6,7},{7,6},{8,9},{9,8},{10,11... | collective-permute-start | bytes 688136 | tf_op jit(solution)/shard_map/ppermute | solution.py:22
  22.0 0.0 collective-permute-start.7
  22.1 4.1 %collective-permute-start.4 = (f32[64,1664]{1,0:T(8,128)S(1)}, f32[64,1664]{1,0:T(8,128)S(1)}, u32[]{:S(2)}, u32[]{:S(2)}) collective-permute-start(f32[64,1664]{1,0:T(8,128)S(1)} %get-tuple-element.29), channel_id=1, source_target_pairs={{0,31},{1,2},{2,1},{3,4},{4,3},{5,6},{6,5},{7,8},{8,7},{9,10},{10,... | collective-permute-start | bytes 1277960 | tf_op jit(solution)/shard_map/ppermute | solution.py:28
  26.2 0.0 collective-permute-done.6.low
  26.2 0.0 collective-permute-done.7.high
  26.2 3.0 %inner.1 = f32[128,1536]{1,0:T(8,128)S(1)} custom-call(f32[128,1536]{1,0:T(8,128)S(1)} %get-tuple-element.31.vectors.own, f32[64,896]{1,0:T(8,128)S(1)} %collective-permute-done.6.low, f32[64,896]{1,0:T(8,128)S(1)} %collective-permute-done.7.high, bf16[12,2432,256]{2,1,0:T(8,128)(2,1)S(1)} %get-tuple-element.24.band), custom_call_target="tpu_custom_call" | custom-call | flops 1 | bytes 1 | tf_op jit(solution)/shard_map/inner/pallas_call | solution.py:362
  29.2 1.7 %collective-permute-done.5.far = f32[128,512]{1,0:T(8,128)S(1)} collective-permute-done((f32[128,512]{1,0:T(8,128)S(1)}, f32[128,512]{1,0:T(8,128)S(1)}, u32[]{:S(2)}, u32[]{:S(2)}) %collective-permute-start.5) | collective-permute-done | bytes 262176 | tf_op jit(solution)/shard_map/ppermute | solution.py:22
  30.9 2.4 %collective-permute-done.4.away = f32[64,1664]{1,0:T(8,128)S(1)} collective-permute-done((f32[64,1664]{1,0:T(8,128)S(1)}, f32[64,1664]{1,0:T(8,128)S(1)}, u32[]{:S(2)}, u32[]{:S(2)}) %collective-permute-start.4) | collective-permute-done | bytes 426016 | tf_op jit(solution)/shard_map/ppermute | solution.py:28
  33.4 2.5 %second.1 = f32[1536,128]{1,0:T(8,128)} custom-call(f32[64,1664]{1,0:T(8,128)S(1)} %collective-permute-done.4.away, bf16[256,512]{1,0:T(8,128)(2,1)S(1)} %split.1.far, bf16[12,2432,256]{2,1,0:T(8,128)(2,1)S(1)} %get-tuple-element.24.band, f32[128,1536]{1,0:T(8,128)S(1)} %inner.1, f32[128,1536]{1,0:T(8,128)S(1)} %get-tuple-element.31.vectors.own, ...), custom_call_target="tpu_custom_call" | custom-call | flops 603979776 | tf_op jit(solution)/shard_map/second/pallas_call | solution.py:463
  (4 shorter events, 0.1 us)
Async XLA Ops:
  1.6 6.7 %collective-permute-start = (s32[1,8]{1,0:T(1,128)}, s32[1,8]{1,0:T(1,128)S(1)}, u32[]{:S(2)}, u32[]{:S(2)}) collective-permute-start(s32[1,8]{1,0:T(1,128)} %param.7), channel_id=1, source_target_pairs={{0,4},{1,5},{2,6},{3,7},{4,0},{5,1},{6,2},{7,3},{8,12},{9,13},{10,... | collective-permute-start | bytes 104 | tf_op jit(solution)/shard_map/ppermute | solution.py:22
  4.6 12.3 %collective-permute-start.2 = (f32[64,1664]{1,0:T(8,128)S(1)}, f32[64,1664]{1,0:T(8,128)S(1)}, u32[]{:S(2)}, u32[]{:S(2)}) collective-permute-start(f32[64,1664]{1,0:T(8,128)S(1)} %get-tuple-element.25), channel_id=1, source_target_pairs={{0,31},{1,2},{2,1},{3,4},{4,3},{5,6},{6,5},{7,8},{8,7},{9,10},{10,... | collective-permute-start | bytes 1277960 | tf_op jit(solution)/shard_map/ppermute | solution.py:28
  9.0 10.8 %collective-permute-start.1 = (f32[128,512]{1,0:T(8,128)S(1)}, f32[128,512]{1,0:T(8,128)S(1)}, u32[]{:S(2)}, u32[]{:S(2)}) collective-permute-start(f32[128,512]{1,0:T(8,128)S(1)} %far.1), channel_id=1, source_target_pairs={{0,4},{1,5},{2,6},{3,7},{4,0},{5,1},{6,2},{7,3},{8,12},{9,13},{10,... | collective-permute-start | bytes 786440 | tf_op jit(solution)/shard_map/ppermute | solution.py:22
  9.1 7.8 %collective-permute-start.3 = (f32[128,896]{1,0:T(8,128)S(1)}, f32[128,896]{1,0:T(8,128)S(1)}, u32[]{:S(2)}, u32[]{:S(2)}) collective-permute-start(f32[128,896]{1,0:T(8,128)S(1)} %get-tuple-element.27), channel_id=1, source_target_pairs={{0,1},{1,0},{2,3},{3,2},{4,5},{5,4},{6,7},{7,6},{8,9},{9,8},{10,11... | collective-permute-start | bytes 1376264 | tf_op jit(solution)/shard_map/ppermute | solution.py:22
  21.1 9.8 %collective-permute-start.5 = (f32[128,512]{1,0:T(8,128)S(1)}, f32[128,512]{1,0:T(8,128)S(1)}, u32[]{:S(2)}, u32[]{:S(2)}) collective-permute-start(f32[128,512]{1,0:T(8,128)S(1)} %get-tuple-element.30), channel_id=1, source_target_pairs={{0,4},{1,5},{2,6},{3,7},{4,0},{5,1},{6,2},{7,3},{8,12},{9,13},{10,... | collective-permute-start | bytes 786440 | tf_op jit(solution)/shard_map/ppermute | solution.py:22
  21.6 4.6 %collective-permute-start.6 = (f32[64,896]{1,0:T(8,128)S(1)}, f32[64,896]{1,0:T(8,128)S(1)}, u32[]{:S(2)}, u32[]{:S(2)}) collective-permute-start(f32[64,896]{1,0:T(8,128)S(1)} %get-tuple-element.32), channel_id=1, source_target_pairs={{0,1},{1,0},{2,3},{3,2},{4,5},{5,4},{6,7},{7,6},{8,9},{9,8},{10,11... | collective-permute-start | bytes 688136 | tf_op jit(solution)/shard_map/ppermute | solution.py:22
  22.0 4.2 %collective-permute-start.7 = (f32[64,896]{1,0:T(8,128)S(1)}, f32[64,896]{1,0:T(8,128)S(1)}, u32[]{:S(2)}, u32[]{:S(2)}) collective-permute-start(f32[64,896]{1,0:T(8,128)S(1)} %get-tuple-element.33), channel_id=1, source_target_pairs={{0,1},{1,0},{2,3},{3,2},{4,5},{5,4},{6,7},{7,6},{8,9},{9,8},{10,11... | collective-permute-start | bytes 688136 | tf_op jit(solution)/shard_map/ppermute | solution.py:22
  22.1 11.3 %collective-permute-start.4 = (f32[64,1664]{1,0:T(8,128)S(1)}, f32[64,1664]{1,0:T(8,128)S(1)}, u32[]{:S(2)}, u32[]{:S(2)}) collective-permute-start(f32[64,1664]{1,0:T(8,128)S(1)} %get-tuple-element.29), channel_id=1, source_target_pairs={{0,31},{1,2},{2,1},{3,4},{4,3},{5,6},{6,5},{7,8},{8,7},{9,10},{10,... | collective-permute-start | bytes 1277960 | tf_op jit(solution)/shard_map/ppermute | solution.py:28
